TPU v7x, 128 devices: a whole 4x4x4 slice. The times are simulated.
128 devices in a mesh: ctx: 16 (over x_lo, z, core), tp: 8 (over x_hi, y).
Axes of the slice: x: 4 (x_hi: 2, x_lo: 2; x = x_hi * 2 + x_lo), y: 4, z: 4, core: 2. Of those that a mesh axis runs over, the one named last changes fastest.
Arguments:
- text_embed: bfloat16 [16384, 3584], P('ctx', 'tp'), may hold values from -6 to 6
- frame_features: bfloat16 [8192, 1152], P(('ctx', 'tp')), may hold values from -6 to 6
- frame_positions: int32 [8192], P(('ctx', 'tp')), may hold values from 0 to 16383, as said below
- span_order: int32 [32], replicated, may hold values from 0 to 31, as said below
- projector: bfloat16 [1152, 3584], replicated, may hold values from -0.1875 to 0.1875
- norm_gain: bfloat16 [3584], P('tp'), may hold values from 0.099609375 to 1.8984375
- query_weight: bfloat16 [3584, 2048], P(None, 'tp'), may hold values from -1 to 1
- key_weight: bfloat16 [3584, 512], replicated, may hold values from -0.125 to 0.125
- value_weight: bfloat16 [3584, 512], replicated, may hold values from -0.09375 to 0.09375
- out_weight: bfloat16 [2048, 3584], P('tp'), may hold values from -0.5 to 0.5
Outputs:
- mixed: bfloat16 [16384, 3584], P('ctx', 'tp')
Inputs may be any that keep to these rules, and one draw needn't show every extreme that they name: `span_order`: each span of the sequence once. `frame_positions`: distinct; the 64 frame tokens of one device lie in the rows of exactly 8 indices of ctx, 8 in each.
All inputs are finite; a program needn't handle non-finite values.
Results may differ from a plain program's by a relative error of at most 0.028.
The roundings to bfloat16 on the way count: a program that leaves them out, or rounds other values in their place, can miss the bound.
Values may be sent and summed in bfloat16 or wider, within the bound.
A program may use at most 128 MiB of HBM per device.

v0:
```python
import math

import jax
import jax.numpy as jnp
from jax import lax
from jax.sharding import PartitionSpec as P

HS = 128
KVH = 4
CAP = 8


def rotate(field, positions):
    half = field.shape[-1] // 2
    freqs = 1000000.0 ** (-(jnp.arange(half, dtype=jnp.float32) * 2.0 / field.shape[-1]))
    angles = positions.astype(jnp.float32)[:, None] * freqs[None, :]
    cosine = jnp.cos(angles)[:, None, :]
    sine = jnp.sin(angles)[:, None, :]
    first = field[..., :half]
    second = field[..., half:]
    return jnp.concatenate(
        [first * cosine - second * sine, second * cosine + first * sine], axis=-1
    )


def per_device(
    text_embed,
    frame_features,
    frame_positions,
    span_order,
    projector,
    norm_gain,
    query_weight,
    key_weight,
    value_weight,
    out_weight,
):
    tok_rows, part_width = text_embed.shape
    width = projector.shape[1]
    ctx_count = lax.axis_size("ctx")
    tp_count = lax.axis_size("tp")
    span = tok_rows // 2
    slots = span_order.shape[0]
    slot_of = jnp.zeros((slots,), jnp.int32).at[span_order].set(jnp.arange(slots, dtype=jnp.int32))
    projected = jax.nn.gelu(
        jnp.dot(frame_features, projector, preferred_element_type=jnp.float32), approximate=False
    ).astype(jnp.bfloat16)
    slot = slot_of[frame_positions // span]
    target = slot // 2
    target_row = slot % 2 * span + frame_positions % span
    onehot = (target[:, None] == jnp.arange(ctx_count, dtype=jnp.int32)[None, :]).astype(jnp.int32)
    before = jnp.cumsum(onehot, axis=0) - onehot
    place = jnp.sum(before * onehot, axis=1)
    outgoing = jnp.zeros((ctx_count, tp_count, CAP, part_width), jnp.bfloat16)
    outgoing = outgoing.at[target, :, place].set(projected.reshape(-1, tp_count, part_width))
    row_slots = jnp.full((ctx_count, CAP), tok_rows, jnp.int32).at[target, place].set(target_row)
    row_slots = jnp.broadcast_to(row_slots[:, None, :], (ctx_count, tp_count, CAP))
    arrived, arrived_rows = (
        lax.all_to_all(
            outgoing.reshape(ctx_count * tp_count, CAP, part_width),
            ("ctx", "tp"),
            split_axis=0,
            concat_axis=0,
            tiled=True,
        ),
        lax.all_to_all(
            row_slots.reshape(ctx_count * tp_count, CAP),
            ("ctx", "tp"),
            split_axis=0,
            concat_axis=0,
            tiled=True,
        ),
    )
    incoming = arrived.reshape(-1, part_width)
    incoming_rows = arrived_rows.reshape(-1)
    placed = text_embed.at[incoming_rows].set(incoming, mode="drop")
    placed_f = placed.astype(jnp.float32)
    row_total = lax.psum(jnp.sum(placed_f * placed_f, axis=1), "tp")
    normed = (
        placed_f
        * lax.rsqrt(row_total[:, None] / width + 1e-06)
        * norm_gain.astype(jnp.float32)[None, :]
    ).astype(jnp.bfloat16)
    kv_start = lax.axis_index("tp") * KVH // tp_count * HS
    combined = jnp.concatenate(
        [
            query_weight,
            lax.dynamic_slice_in_dim(key_weight, kv_start, HS, 1),
            lax.dynamic_slice_in_dim(value_weight, kv_start, HS, 1),
        ],
        axis=1,
    )
    q_cols = query_weight.shape[1]
    projections = jnp.dot(
        lax.all_gather(normed, "tp", axis=1, tiled=True),
        combined,
        preferred_element_type=jnp.float32,
    )
    rows = jnp.arange(tok_rows, dtype=jnp.int32)
    positions = span_order[2 * lax.axis_index("ctx") + rows // span] * span + rows % span
    heads = q_cols // HS
    query = rotate(projections[:, :q_cols].reshape(tok_rows, heads, HS), positions).astype(
        jnp.bfloat16
    )
    keys = (
        rotate(projections[:, q_cols : q_cols + HS].reshape(tok_rows, 1, HS), positions)
        .reshape(tok_rows, HS)
        .astype(jnp.bfloat16)
    )
    values = projections[:, q_cols + HS :].astype(jnp.bfloat16)
    scale = 1.0 / math.sqrt(HS)

    def update(state, block):
        largest_old, total_old, summed_old = state
        key_block, value_block, pos_block = block
        scores = (
            jnp.einsum("qhd,kd->qhk", query, key_block, preferred_element_type=jnp.float32) * scale
        )
        allowed = pos_block[None, None, :] <= positions[:, None, None]
        largest = jnp.maximum(largest_old, jnp.max(jnp.where(allowed, scores, -1e30), axis=2))
        weights = jnp.where(allowed, jnp.exp(scores - largest[:, :, None]), 0.0)
        factor = jnp.exp(largest_old - largest)
        total = total_old * factor + jnp.sum(weights, axis=2)
        summed = summed_old * factor[:, :, None] + jnp.einsum(
            "qhk,kd->qhd",
            weights.astype(jnp.bfloat16),
            value_block,
            preferred_element_type=jnp.float32,
        )
        return (largest, total, summed)

    def advance(state, block):
        return (update(state, block), None)

    initial = (
        jnp.full((tok_rows, heads), -1e30, jnp.float32),
        jnp.zeros((tok_rows, heads), jnp.float32),
        jnp.zeros((tok_rows, heads, HS), jnp.float32),
    )
    key_piece = lax.all_gather(keys, "ctx", axis=0, tiled=True)
    value_piece = lax.all_gather(values, "ctx", axis=0, tiled=True)
    pos_piece = lax.all_gather(positions, "ctx", axis=0, tiled=True)
    count = key_piece.shape[0] // tok_rows
    blocks = (
        key_piece.reshape(count, tok_rows, HS),
        value_piece.reshape(count, tok_rows, HS),
        pos_piece.reshape(count, tok_rows),
    )
    final, unused = lax.scan(advance, initial, blocks)
    largest, total, summed = final
    attended = (summed / total[:, :, None]).astype(jnp.bfloat16).reshape(tok_rows, heads * HS)
    partial_sum = jnp.dot(attended, out_weight, preferred_element_type=jnp.float32)
    mixed_part = lax.psum_scatter(
        partial_sum.astype(jnp.bfloat16), "tp", scatter_dimension=1, tiled=True
    ).astype(jnp.float32)
    return (placed_f + mixed_part).astype(jnp.bfloat16)


def solution(mesh):
    in_specs = (
        P("ctx", "tp"),
        P(("ctx", "tp"), None),
        P(("ctx", "tp")),
        P(),
        P(),
        P("tp"),
        P(None, "tp"),
        P(),
        P(),
        P("tp", None),
    )
    out_specs = P("ctx", "tp")
    return jax.shard_map(
        per_device, mesh=mesh, in_specs=in_specs, out_specs=out_specs, check_vma=False
    )
```

profile of v0, /device:TPU:29, one launch (start us, length us, event | category | flops | bytes accessed | tf_op | source)
XLA Modules:
  0.0 677.8 jit_solution(10988909189073004082)
XLA Ops:
  14.7 10.6 %all-to-all-start = ((s32[128,1,8]{2,1,0:T(1,128)}), s32[128,1,8]{2,1,0:T(1,128)S(1)}, u32[]{:S(2)}, u32[]{:S(2)}) async-start(s32[128,1,8]{2,1,0:T(1,128)} %bitcast.3), calls=%async_computation | async-start | bytes 131072 | tf_op jit(solution)/shard_map/all_to_all | solution.py:66
  25.3 6.4 fusion.36
  37.0 9.8 %all-to-all-start.1 = ((bf16[128,8,448]{2,1,0:T(8,128)(2,1)}), bf16[128,8,448]{2,1,0:T(8,128)(2,1)S(1)}, u32[]{:S(2)}, u32[]{:S(2)}) async-start(bf16[128,8,448]{2,1,0:T(8,128)(2,1)} %bitcast.112), calls=%async_computation.1 | async-start | bytes 2097152 | tf_op jit(solution)/shard_map/all_to_all | solution.py:59
  50.5 12.3 %all-to-all-done.1 = bf16[128,8,448]{2,1,0:T(8,128)(2,1)S(1)} async-done(((bf16[128,8,448]{2,1,0:T(8,128)(2,1)}), bf16[128,8,448]{2,1,0:T(8,128)(2,1)S(1)}, u32[]{:S(2)}, u32[]{:S(2)}) %all-to-all-start.1) | async-done | bytes 917536 | tf_op jit(solution)/shard_map/all_to_all | solution.py:59
  62.8 7.3 %scatter_custom_fusion.3 = bf16[1024,448]{1,0:T(8,128)(2,1)} fusion(bf16[1024,448]{1,0:T(8,128)(2,1)} %copy.30, s32[1024]{0:T(1024)S(1)} %bitcast.117, bf16[128,8,448]{2,1,0:T(8,128)(2,1)S(1)} %all-to-all-done.1), kind=kCustom, calls=%fused_computation.47 | custom fusion | bytes 1966080 | tf_op jit(solution)/shard_map/scatter | solution.py:76
  71.8 15.2 %psum.7 = f32[1024]{0:T(1024)S(1)} all-reduce(f32[1024]{0:T(1024)S(1)} %fusion.28), channel_id=1, replica_groups=mesh['ctx'=16,'tp'=8] {'tp'}, use_global_device_ids=true, to_apply=%region_7.8 | all-reduce | flops 1024 | bytes 8192 | tf_op jit(solution)/shard_map/psum | solution.py:78
  89.8 4.3 compare_select_fusion.2
  94.8 15.6 %fusion.65 = (f32[1024]{0:T(1024)S(1)}, s32[1024]{0:T(1024)S(1)}) fusion(pred[1024]{0:T(1024)(128)(4,1)S(1)} %get-tuple-element.180, pred[1024]{0:T(1024)(128)(4,1)S(1)} %get-tuple-element.181, pred[1024]{0:T(1024)(128)(4,1)S(1)} %get-tuple-element.182, pred[1024]{0:T(1024)(128)(4,1)S(1)} %get-tuple-element.183, pred[1024]{0:T(1024)(128)(4,1)S(1)} %get-tuple-element.184, ...), kind=kLoop, calls=%fused_computation.168 | loop fusion | flops 34816 | bytes 37988 | tf_op jit(solution)/shard_map/convert_element_type | solution.py:16
  113.3 72.1 %all-gather.5.cloned.1.call-done = bf16[1024,3584]{0,1:T(8,128)(2,1)} async-done(((bf16[1024,448]{0,1:T(8,128)(2,1)}), bf16[1024,3584]{0,1:T(8,128)(2,1)}) %all-gather.5.cloned.1.call-update) | async-done | bytes 7340048 | tf_op jit(solution)/shard_map/all_gather | solution.py:95
  185.5 7.4 %fusion.22 = f32[1024,512]{0,1:T(8,128)S(1)} fusion(bf16[1024,3584]{0,1:T(8,128)(2,1)} %all-gather.5.cloned.1.call-done, bf16[3584,128]{1,0:T(8,128)(2,1)} %get-tuple-element.178, bf16[3584,128]{1,0:T(8,128)(2,1)} %get-tuple-element.179, bf16[3584,256]{1,0:T(8,128)(2,1)} %param.18), kind=kOutput, calls=%fused_computation.33 | convolution fusion | flops 3769106432 | bytes 13107200 | tf_op jit(solution)/shard_map/dot_general | solution.py:94
  198.1 21.5 %all_gather.12 = s32[16384]{0:T(1024)S(1)} all-gather(s32[1024]{0:T(1024)S(1)} %get-tuple-element.272), channel_id=1, replica_groups=mesh['ctx'=16,'tp'=8] {'ctx'}, dimensions={0}, use_global_device_ids=true | all-gather | bytes 69632 | tf_op jit(solution)/shard_map/all_gather | solution.py:142
  228.5 8.4 %all-gather.9.cloned.1.call-done = bf16[16384,1,128]{0,2,1:T(8,128)(2,1)} async-done(((bf16[1024,1,128]{0,2,1:T(8,128)(2,1)}), bf16[16384,1,128]{0,2,1:T(8,128)(2,1)}) %all-gather.9.cloned.1.call-update) | async-done | bytes 4194320 | tf_op jit(solution)/shard_map/all_gather | solution.py:140
  236.9 6.3 copy.38
  243.3 32.7 %all-gather.7.cloned.1.call-done = bf16[16384,128]{0,1:T(8,128)(2,1)} async-done(((bf16[1024,128]{0,1:T(8,128)(2,1)}), bf16[16384,128]{0,1:T(8,128)(2,1)}) %all-gather.7.cloned.1.call-update) | async-done | bytes 4194320 | tf_op jit(solution)/shard_map/all_gather | solution.py:141
  276.0 6.4 copy.39
  282.4 277.8 %while.15 = (s32[]{:T(128)}, f32[1024,2]{0,1:T(2,128)S(1)}, f32[1024,2]{0,1:T(2,128)S(1)}, f32[1024,2,128]{2,0,1:T(8,128)}, s32[16,1024]{1,0:T(8,128)S(1)}, /*in...) while((s32[]{:T(128)}, f32[1024,2]{0,1:T(2,128)S(1)}, ...), condition=%wide.region_11.12_spmd.clone, body=%wide.region_8.11_spmd.clone.sunk | while | flops 1098655744 | bytes 74597592 | solution.py:149
  283.1 6.0 fusion.87
  289.1 4.6 fusion.89
  295.1 3.7 fusion.91
  300.4 6.0 fusion.87
  306.4 4.6 fusion.89
  312.5 3.7 fusion.91
  317.8 6.0 fusion.87
  323.8 4.6 fusion.89
  329.8 3.6 fusion.91
  335.2 6.0 fusion.87
  341.1 4.6 fusion.89
  347.2 3.7 fusion.91
  352.5 6.0 fusion.87
  358.5 4.6 fusion.89
  364.6 3.6 fusion.91
  369.9 6.0 fusion.87
  375.9 4.6 fusion.89
  381.9 3.7 fusion.91
  387.3 6.0 fusion.87
  393.2 4.6 fusion.89
  399.3 3.6 fusion.91
  404.6 6.0 fusion.87
  410.6 4.6 fusion.89
  416.7 3.7 fusion.91
  422.0 6.0 fusion.87
  428.0 4.6 fusion.89
  434.0 3.6 fusion.91
  439.3 6.0 fusion.87
  445.3 4.6 fusion.89
  451.4 3.7 fusion.91
  456.7 6.0 fusion.87
  462.7 4.6 fusion.89
  468.7 3.6 fusion.91
  474.1 6.0 fusion.87
  480.1 4.6 fusion.89
  486.1 3.7 fusion.91
  491.4 6.0 fusion.87
  497.4 4.6 fusion.89
  508.8 6.0 fusion.87
  514.8 4.6 fusion.89
  520.8 3.7 fusion.91
  526.2 6.0 fusion.87
  532.2 4.6 fusion.89
  543.5 6.0 fusion.87
  549.5 4.6 fusion.89
  555.6 3.7 fusion.91
  561.9 5.1 convolution_convert_fusion
  567.0 101.8 %reduce-scatter.2.cloned.1.call-done = bf16[1024,448]{0,1:T(8,128)(2,1)} async-done(((bf16[1024,3584]{0,1:T(8,128)(2,1)}), bf16[1024,448]{0,1:T(8,128)(2,1)}) %reduce-scatter.2.cloned.1.call-update) | async-done | bytes 917520 | tf_op jit(solution)/shard_map/reduce_scatter | solution.py:153
  (264 shorter events, 100.2 us)
Async XLA Ops:
  6.5 555.4 %copy-start = (bf16[256,3584]{1,0:T(8,128)(2,1)S(1)}, bf16[256,3584]{1,0:T(8,128)(2,1)}, u32[]{:S(2)}) copy-start(bf16[256,3584]{1,0:T(8,128)(2,1)} %param.21) | copy-start | bytes 5505028
  14.7 22.3 %all-to-all-start = ((s32[128,1,8]{2,1,0:T(1,128)}), s32[128,1,8]{2,1,0:T(1,128)S(1)}, u32[]{:S(2)}, u32[]{:S(2)}) async-start(s32[128,1,8]{2,1,0:T(1,128)} %bitcast.3), calls=%async_computation | async-start | bytes 131072 | tf_op jit(solution)/shard_map/all_to_all | solution.py:66
  32.3 16.8 %copy-start.8 = (bf16[448]{0:T(512)(128)(2,1)S(1)}, bf16[448]{0:T(512)(128)(2,1)}, u32[]{:S(2)}) copy-start(bf16[448]{0:T(512)(128)(2,1)} %param.17) | copy-start | bytes 2692
  37.0 25.8 %all-to-all-start.1 = ((bf16[128,8,448]{2,1,0:T(8,128)(2,1)}), bf16[128,8,448]{2,1,0:T(8,128)(2,1)S(1)}, u32[]{:S(2)}, u32[]{:S(2)}) async-start(bf16[128,8,448]{2,1,0:T(8,128)(2,1)} %bitcast.112), calls=%async_computation.1 | async-start | bytes 2097152 | tf_op jit(solution)/shard_map/all_to_all | solution.py:59
  46.8 138.7 %all-gather.5.cloned.1.call-start = ((), (), s32[]{:S(2)}) async-start(), calls=%async_computation.3 | async-start | bytes 8257536 | tf_op jit(solution)/shard_map/all_gather | solution.py:95
  49.1 40.0 %copy-start.7 = (s32[32]{0:T(128)S(1)}, s32[32]{0:T(128)}, u32[]{:S(2)}) copy-start(s32[32]{0:T(128)} %param.15) | copy-start | bytes 388
  71.6 121.3 %copy-start.2 = (bf16[1024,448]{0,1:T(8,128)(2,1)}, bf16[1024,448]{0,1:T(8,128)(2,1)S(1)}, u32[]{:S(2)}) copy-start(bf16[1024,448]{0,1:T(8,128)(2,1)S(1)} %copy.31) | copy-start | bytes 2752516
  88.3 148.6 %all-gather.9.cloned.1.call-start = ((), (), s32[]{:S(2)}) async-start(), calls=%async_computation.6 | async-start | bytes 4456448 | tf_op jit(solution)/shard_map/all_gather | solution.py:140
  192.9 1.4 copy-start.4
  194.3 28.4 %slice-start = ((f32[1024,512]{0,1:T(8,128)}), f32[1024,256]{0,1:T(8,128)S(1)}, s32[]{:S(2)}) async-start(f32[1024,512]{0,1:T(8,128)} %copy-done.4), calls=%async_computation.7 | async-start | bytes 2097152 | tf_op jit(solution)/shard_map/slice | solution.py:102
  196.2 79.9 %all-gather.7.cloned.1.call-start = ((), (), s32[]{:S(2)}) async-start(), calls=%async_computation.4 | async-start | bytes 4456448 | tf_op jit(solution)/shard_map/all_gather | solution.py:141
  198.0 470.8 %reduce-scatter.2.cloned.1.call-start = ((), (), s32[]{:S(2)}) async-start(), calls=%async_computation.5 | async-start | bytes 8257536 | tf_op jit(solution)/shard_map/reduce_scatter | solution.py:153
  289.0 5.8 copy-start.1
  289.0 6.1 copy-start.5
  298.8 1.0 copy-start.6
  306.4 5.8 copy-start.1
  306.4 6.1 copy-start.5
  316.1 1.0 copy-start.6
  323.8 5.8 copy-start.1
  323.8 6.1 copy-start.5
  333.5 1.0 copy-start.6
  341.1 5.8 copy-start.1
  341.1 6.1 copy-start.5
  350.9 1.0 copy-start.6
  358.5 5.8 copy-start.1
  358.5 6.1 copy-start.5
  368.2 1.0 copy-start.6
  375.9 5.8 copy-start.1
  375.9 6.1 copy-start.5
  385.6 1.0 copy-start.6
  393.2 5.8 copy-start.1
  393.2 6.1 copy-start.5
  402.9 1.0 copy-start.6
  410.6 5.8 copy-start.1
  410.6 6.1 copy-start.5
  420.3 1.0 copy-start.6
  428.0 5.8 copy-start.1
  428.0 6.1 copy-start.5
  437.7 1.0 copy-start.6
  445.3 5.8 copy-start.1
  445.3 6.1 copy-start.5
  455.0 1.0 copy-start.6
  462.7 5.8 copy-start.1
  462.7 6.1 copy-start.5
  472.4 1.0 copy-start.6
  480.0 5.8 copy-start.1
  480.1 6.1 copy-start.5
  489.8 1.0 copy-start.6
  497.4 5.8 copy-start.1
  497.4 6.1 copy-start.5
  507.1 1.0 copy-start.6
  514.8 5.8 copy-start.1
  514.8 6.1 copy-start.5
  524.5 1.0 copy-start.6
  532.1 5.8 copy-start.1
  532.1 6.1 copy-start.5
  541.9 1.0 copy-start.6
  549.5 5.8 copy-start.1
  549.5 6.1 copy-start.5
  559.2 1.0 copy-start.6
  567.0 101.8 %copy-start.3 = (bf16[1024,448]{0,1:T(8,128)(2,1)S(1)}, bf16[1024,448]{0,1:T(8,128)(2,1)}, u32[]{:S(2)}) copy-start(bf16[1024,448]{0,1:T(8,128)(2,1)} %copy-done.2) | copy-start | bytes 2752516
Sparse Core Ops, SparseCore 0:
  88.4 97.0 all-gather.4
  196.3 40.5 all-gather.8
  238.6 37.3 all-gather.6
  567.1 101.5 reduce-scatter.1
where the time goes:
time: 685 us; the launch traced here: 678 us
  waiting for transfers between devices  227 us (33%)
  matrix products  173 us (25%)
  other arithmetic  119 us (17%)
  local copies, waits for them, and re-layouts  86.7 us (13%)
  blocking collectives  36.7 us (5%)
  starting transfers between devices  20.7 us (3%)
  between operations  13.4 us (2%)
    reduce_scatter x1, waiting for transfers between devices, per_device(): lax.psum_scatter(partial_sum.astype(jnp.bfloat16), 'tp', scatter_dimensio...  102 us
    dot_general x16, matrix products, update(): jnp.einsum('qhd,kd->qhk', query, key_block, preferred_element_type=jnp.fl...  95.4 us
    reduce_sum x16, other arithmetic, update(): total = total_old * factor + jnp.sum(weights, axis=2)  73.6 us
    all_gather x1, waiting for transfers between devices, per_device(): lax.all_gather(normed, 'tp', axis=1, tiled=True)  72.1 us
    dot_general x16, matrix products, update(): jnp.einsum('qhk,kd->qhd', weights.astype(jnp.bfloat16), value_block, pref...  58.4 us
    while x112, local copies, waits for them, and re-layouts  38.5 us
    all_gather x1, waiting for transfers between devices, per_device(): value_piece = lax.all_gather(values, 'ctx', axis=0, tiled=True)  32.7 us
    all_gather x1, blocking collectives, per_device(): pos_piece = lax.all_gather(positions, 'ctx', axis=0, tiled=True)  21.5 us
  transfers between devices with their start and end apart: 6, of which 5 were waited for; matrix products, arithmetic and copies ran while one was open for 8% of the time, Pallas kernels for 0%

commit v1 on v0

v1 whole, which is shorter than its diff:
```python
import functools
import math

import jax
import jax.numpy as jnp
from jax import lax
from jax.experimental import pallas as pl
from jax.experimental.pallas import tpu as pltpu
from jax.sharding import PartitionSpec as P

HS = 128
KVH = 4
CAP = 8
CH = 512
N_CTX = 16
N_TP = 8
PAIRS = 8
OFF = 64
HALF = 32
MESH = pl.DeviceIdType.MESH
LOG2E = math.log2(math.e)


def signal(sem, ctx, tp):
    pl.semaphore_signal(sem, inc=1, device_id=(ctx, tp), device_id_type=MESH)


def push(src, dst, send_sem, recv_sem, ctx, tp):
    return pltpu.make_async_remote_copy(
        src_ref=src, dst_ref=dst, send_sem=send_sem, recv_sem=recv_sem,
        device_id=(ctx, tp), device_id_type=MESH,
    )


def rows_kernel(placed, gain, rows, normed, gains, send, recv, fsend, frecv, gsend, grecv):
    c = lax.axis_index("ctx")
    t = lax.axis_index("tp")
    pair = c // 2
    core = c % 2
    sibling = pair * 2 + 1 - core
    own = t == pair
    barrier = pltpu.get_barrier_semaphore()
    signal(barrier, sibling, t)
    for j in range(N_TP):
        if_self = jnp.logical_and(own, j == t)

        @pl.when(jnp.logical_not(if_self))
        def _():
            signal(barrier, 2 * t + core, j)

    pl.semaphore_wait(barrier, jnp.where(own, PAIRS, PAIRS + 1))

    def block(d):
        e = lax.rem(pair + d, PAIRS)
        return push(placed.at[:, e], rows.at[core, t], send.at[d], recv.at[t], 2 * e + core, pair)

    def gain_block(d):
        e = lax.rem(pair + d, PAIRS)
        return push(gain, gains.at[t], gsend.at[d], grecv.at[t], 2 * e + core, pair)

    @pl.when(own)
    def _():
        pltpu.make_async_copy(placed.at[:, pair], rows.at[core, t], recv.at[t]).start()
        pltpu.make_async_copy(gain, gains.at[t], grecv.at[t]).start()

    @pl.when(jnp.logical_not(own))
    def _():
        block(0).start()
        gain_block(0).start()

    for d in range(1, PAIRS):
        block(d).start()
        gain_block(d).start()

    def forward(j):
        return push(rows.at[core, j], rows.at[core, j], fsend.at[j], frecv.at[j], sibling, t)

    for d in range(N_TP):
        j = lax.rem(t + d, N_TP)
        push(rows.at[core, j], rows.at[core, j], send.at[0], recv.at[j], sibling, t).wait_recv()
        forward(j).start()
    for j in range(N_TP):
        push(gain, gains.at[j], gsend.at[0], grecv.at[j], sibling, t).wait_recv()

    def receive(j):
        push(
            rows.at[1 - core, j], rows.at[1 - core, j], fsend.at[j], frecv.at[j], sibling, t
        ).wait_recv()

    width = N_TP * placed.shape[-1]

    def normalise(a):
        total = jnp.zeros((2 * OFF, 1), jnp.float32)
        for j in range(N_TP):
            x = rows[a, j].reshape(2 * OFF, -1).astype(jnp.float32)
            total = total + jnp.sum(x * x, axis=1, keepdims=True)
        inverse = lax.rsqrt(total / width + 1e-06)
        for j in range(N_TP):
            x = rows[a, j].reshape(2 * OFF, -1).astype(jnp.float32)
            g = gains[j, 0:1, :].astype(jnp.float32)
            normed[j, a] = (x * inverse * g).astype(jnp.bfloat16)

    normalise(core)
    for j in range(N_TP):
        receive(j)
    normalise(1 - core)

    @pl.when(jnp.logical_not(own))
    def _():
        block(0).wait_send()
        gain_block(0).wait_send()

    for d in range(1, PAIRS):
        block(d).wait_send()
        gain_block(d).wait_send()
    for j in range(N_TP):
        forward(j).wait_send()


def rows_exchange(placed, gain):
    part = placed.shape[-1]
    vm = pl.BlockSpec(memory_space=pltpu.VMEM)
    return pl.pallas_call(
        rows_kernel,
        out_shape=(
            jax.ShapeDtypeStruct((2, N_TP, 2, OFF, part), jnp.bfloat16),
            jax.ShapeDtypeStruct((N_TP, 2, 2 * OFF, part), jnp.bfloat16),
        ),
        in_specs=[vm, vm],
        out_specs=(vm, vm),
        scratch_shapes=[
            pltpu.VMEM((N_TP, 16, part), jnp.bfloat16),
            pltpu.SemaphoreType.DMA((PAIRS,)),
            pltpu.SemaphoreType.DMA((N_TP,)),
            pltpu.SemaphoreType.DMA((N_TP,)),
            pltpu.SemaphoreType.DMA((N_TP,)),
            pltpu.SemaphoreType.DMA((PAIRS,)),
            pltpu.SemaphoreType.DMA((N_TP,)),
        ],
        compiler_params=pltpu.CompilerParams(
            collective_id=1, has_side_effects=True, vmem_limit_bytes=24 * 2**20
        ),
        name="rows",
    )(placed, gain)


def qkv_kernel(
    normed, query_weight, key_weight, value_weight, cosine, sine, kv_cosine, kv_sine,
    query_out, kv_out, weight, query, kv, wsem, qsend, qrecv, ksend, krecv,
):
    c = lax.axis_index("ctx")
    t = lax.axis_index("tp")
    pair = c // 2
    core = c % 2
    q_cols = N_TP * HS
    kv_cols = KVH * HS

    def load(j):
        return pltpu.make_async_copy(
            query_weight.at[j], weight.at[:, pl.ds(j * HS, HS)], wsem.at[j]
        )

    kv_slot = weight.at[:, pl.ds(q_cols, kv_cols)]

    @pl.when(core == 0)
    def _():
        pltpu.make_async_copy(key_weight, kv_slot, wsem.at[N_TP]).start()

    @pl.when(core == 1)
    def _():
        pltpu.make_async_copy(value_weight, kv_slot, wsem.at[N_TP]).start()

    for j in range(N_TP):
        load(j).start()

    barrier = pltpu.get_barrier_semaphore()
    for k in range(2):
        for d in range(N_TP):
            if d == 0:

                @pl.when(core != k)
                def _():
                    signal(barrier, 2 * pair + k, t)

            else:
                signal(barrier, 2 * pair + k, lax.rem(t + d, N_TP))
    pl.semaphore_wait(barrier, 2 * N_TP - 1)

    part = normed.shape[-1]

    def product(start, cols):
        total = jnp.zeros((4 * OFF, cols), jnp.float32)
        for j in range(N_TP):
            x = normed[j].reshape(4 * OFF, part)
            total = total + jnp.dot(
                x, weight[j * part : (j + 1) * part, start : start + cols],
                preferred_element_type=jnp.float32,
            )
        return total

    def rotated(x, cos, sin):
        return (x * cos + pltpu.roll(x, HS // 2, 1) * sin).astype(jnp.bfloat16)

    def kv_push(d):
        j = lax.rem(t + d, N_TP)
        return push(kv.at[j // 2], kv_out.at[t], ksend.at[d], krecv.at[t], c, j)

    def q_push(d, k):
        j = lax.rem(t + d, N_TP)
        return push(
            query.at[j, :, pl.ds(k * HALF, HALF), :], query_out.at[core, t],
            qsend.at[d, k], qrecv.at[core, t], 2 * pair + k, j,
        )

    pltpu.make_async_copy(key_weight, kv_slot, wsem.at[N_TP]).wait()
    total = product(q_cols, kv_cols)
    for h in range(KVH):
        kv[h] = rotated(total[:, h * HS : (h + 1) * HS], kv_cosine[...], kv_sine[...]).reshape(
            4, OFF, HS
        )
    pltpu.make_async_copy(kv.at[t // 2], kv_out.at[t], krecv.at[t]).start()
    for d in range(1, N_TP):
        kv_push(d).start()
    for g in range(2):
        for j in range(4 * g, 4 * g + 4):
            load(j).wait()
        total = product(g * 4 * HS, 4 * HS)
        for h in range(4):
            query[4 * g + h] = rotated(
                total[:, h * HS : (h + 1) * HS], cosine[...], sine[...]
            ).reshape(4, OFF, HS)
    for d in range(N_TP):
        for k in range(2):
            if d == 0:

                @pl.when(core == k)
                def _():
                    pltpu.make_async_copy(
                        query.at[t, :, pl.ds(k * HALF, HALF), :], query_out.at[core, t],
                        qrecv.at[core, t],
                    ).start()

                @pl.when(core != k)
                def _():
                    q_push(0, k).start()

            else:
                q_push(d, k).start()
    for j in range(N_TP):
        push(kv.at[0], kv_out.at[j], ksend.at[0], krecv.at[j], c, t).wait_recv()
        for k in range(2):
            push(
                query_out.at[k, j], query_out.at[k, j], qsend.at[0, 0], qrecv.at[k, j], c, t
            ).wait_recv()
    for d in range(N_TP):
        if d > 0:
            kv_push(d).wait_send()
        for k in range(2):
            if d == 0:

                @pl.when(core != k)
                def _():
                    q_push(0, k).wait_send()

            else:
                q_push(d, k).wait_send()


def qkv_exchange(normed, query_weight, key_weight, value_weight, tables):
    width = key_weight.shape[0]
    vm = pl.BlockSpec(memory_space=pltpu.VMEM)
    anywhere = pl.BlockSpec(memory_space=pl.ANY)
    return pl.pallas_call(
        qkv_kernel,
        out_shape=(
            jax.ShapeDtypeStruct((2, N_TP, 4, HALF, HS), jnp.bfloat16),
            jax.ShapeDtypeStruct((N_TP, 4, OFF, HS), jnp.bfloat16),
        ),
        in_specs=[vm, anywhere, anywhere, anywhere, vm, vm, vm, vm],
        out_specs=(vm, vm),
        scratch_shapes=[
            pltpu.VMEM((width, (N_TP + KVH) * HS), jnp.bfloat16),
            pltpu.VMEM((N_TP, 4, OFF, HS), jnp.bfloat16),
            pltpu.VMEM((KVH, 4, OFF, HS), jnp.bfloat16),
            pltpu.SemaphoreType.DMA((N_TP + 1,)),
            pltpu.SemaphoreType.DMA((N_TP, 2)),
            pltpu.SemaphoreType.DMA((2, N_TP)),
            pltpu.SemaphoreType.DMA((N_TP,)),
            pltpu.SemaphoreType.DMA((N_TP,)),
        ],
        compiler_params=pltpu.CompilerParams(
            collective_id=2, has_side_effects=True, vmem_limit_bytes=40 * 2**20
        ),
        name="qkv",
    )(normed, query_weight, key_weight, value_weight, *tables)


def attention_kernel(slot_of, offset, query, kv, out):
    scale = LOG2E / math.sqrt(HS)
    first = offset[0]

    def chunk(i, unused):
        q = jnp.concatenate(
            [query[:, slot_of[4 * i + a]].reshape(2 * HALF, HS) for a in range(4)], axis=0
        )

        def keys_of(j, which):
            return jnp.concatenate(
                [kv[:, which, slot_of[4 * j + a]].reshape(CH, HS) for a in range(4)], axis=0
            )

        def scores_of(j):
            return lax.dot_general(
                q, keys_of(j, 0), (((1,), (1,)), ((), ())), preferred_element_type=jnp.float32
            )

        def update(state, s, j):
            largest_old, total_old, summed_old = state
            largest = jnp.maximum(largest_old, jnp.max(s, axis=1, keepdims=True))
            weights = jnp.exp2((s - largest) * scale)
            factor = jnp.exp2((largest_old - largest) * scale)
            total = total_old * factor + jnp.sum(weights, axis=1, keepdims=True)
            summed = summed_old * factor + jnp.dot(
                weights.astype(jnp.bfloat16), keys_of(j, 1), preferred_element_type=jnp.float32
            )
            return largest, total, summed

        rows = 8 * HALF
        initial = (
            jnp.full((rows, 1), -1e30, jnp.float32),
            jnp.zeros((rows, 1), jnp.float32),
            jnp.zeros((rows, HS), jnp.float32),
        )
        s = scores_of(i)
        row = lax.broadcasted_iota(jnp.int32, (rows, 1), 0)
        limit = row // (2 * HALF) * CH + first + row % HALF
        col = lax.broadcasted_iota(jnp.int32, s.shape, 1)
        s = jnp.where(col <= limit, s, -1e30)
        state = update(initial, s, i)
        state = lax.fori_loop(0, i, lambda j, st: update(st, scores_of(j), j), state)
        attended = (state[2] / state[1]).astype(jnp.bfloat16).reshape(4, 2, HALF, HS)
        for a in range(4):
            out[slot_of[4 * i + a]] = jnp.concatenate([attended[a, 0], attended[a, 1]], axis=1)
        return unused

    lax.fori_loop(0, 8, chunk, 0)


def attention(slot_of, offset, query, kv):
    vm = pl.BlockSpec(memory_space=pltpu.VMEM)
    sm = pl.BlockSpec(memory_space=pltpu.SMEM)
    return pl.pallas_call(
        attention_kernel,
        out_shape=jax.ShapeDtypeStruct((32, HALF, 2 * HS), jnp.bfloat16),
        in_specs=[sm, sm, vm, vm],
        out_specs=vm,
        compiler_params=pltpu.CompilerParams(vmem_limit_bytes=48 * 2**20),
        name="attention",
    )(slot_of, offset, query, kv)


def out_kernel(
    attended, out_weight, rows, out, heads, weight, result,
    wsem, hsend, hrecv, fsend, frecv, rsend, rrecv,
):
    c = lax.axis_index("ctx")
    t = lax.axis_index("tp")
    pair = c // 2
    core = c % 2
    sibling = pair * 2 + 1 - core
    side = t // 4
    parts = out_weight.shape[1]

    def load(g):
        return pltpu.make_async_copy(out_weight.at[g], weight.at[g], wsem.at[g])

    for g in range(N_TP):
        load(g).start()

    barrier = pltpu.get_barrier_semaphore()
    signal(barrier, sibling, t)
    for d in range(1, N_TP):
        signal(barrier, c, lax.rem(t + d, N_TP))
    home = jnp.logical_and(t == pair, side == core)
    for d in range(PAIRS):
        e = lax.rem(pair + d, PAIRS)
        if d == 0:

            @pl.when(jnp.logical_not(home))
            def _():
                signal(barrier, 2 * e + side, pair)

        else:
            signal(barrier, 2 * e + side, pair)
    pl.semaphore_wait(barrier, 1 + N_TP - 1 + 2 * parts - jnp.where(home, 1, 0))

    mine = pl.ds(core * HALF, HALF)
    theirs = pl.ds((1 - core) * HALF, HALF)

    def gather(d):
        j = lax.rem(t + d, N_TP)
        return push(
            attended.at[pl.ds(4 * j, 4)], heads.at[t, :, mine, :], hsend.at[d], hrecv.at[t], c, j
        )

    pltpu.make_async_copy(
        attended.at[pl.ds(4 * t, 4)], heads.at[t, :, mine, :], hrecv.at[t]
    ).start()
    for d in range(1, N_TP):
        gather(d).start()

    def forward(j):
        return push(
            heads.at[j, :, mine, :], heads.at[j, :, mine, :], fsend.at[j], frecv.at[j], sibling, t
        )

    for d in range(N_TP):
        j = lax.rem(t + N_TP - d, N_TP)
        push(
            heads.at[j, :, mine, :], heads.at[j, :, mine, :], hsend.at[0], hrecv.at[j], sibling, t
        ).wait_recv()
        forward(j).start()
    for j in range(N_TP):
        push(
            heads.at[j, :, theirs, :], heads.at[j, :, theirs, :], fsend.at[j], frecv.at[j],
            sibling, t,
        ).wait_recv()
    for g in range(N_TP):
        load(g).wait()

    part = out.shape[-1]

    def send_home(j, a):
        return push(
            result.at[j, a], out.at[:, pl.ds(OFF * pair, OFF), :], rsend.at[j, a], rrecv.at[pair],
            2 * t + a, parts * core + j,
        )

    def is_home(j, a):
        return jnp.logical_and(home, jnp.logical_and(a == core, parts * core + j == t))

    for j in range(parts):
        total = jnp.zeros((4 * OFF, part), jnp.float32)
        for g in range(N_TP):
            x = heads[g].reshape(4 * OFF, 2 * HS)
            total = total + jnp.dot(
                x, weight[g, j], preferred_element_type=jnp.float32
            ).astype(jnp.bfloat16).astype(jnp.float32)
        for a in range(2):
            placed = rows[a, parts * core + j].reshape(2 * OFF, part).astype(jnp.float32)
            result[j, a] = (placed + total[a * 2 * OFF : (a + 1) * 2 * OFF]).astype(
                jnp.bfloat16
            ).reshape(2, OFF, part)

            @pl.when(is_home(j, a))
            def _():
                pltpu.make_async_copy(
                    result.at[j, a], out.at[:, pl.ds(OFF * pair, OFF), :], rrecv.at[pair]
                ).start()

            @pl.when(jnp.logical_not(is_home(j, a)))
            def _():
                send_home(j, a).start()

    for e in range(PAIRS):
        push(
            result.at[0, 0], out.at[:, pl.ds(OFF * e, OFF), :], rsend.at[0, 0], rrecv.at[e],
            sibling, t,
        ).wait_recv()
    for d in range(1, N_TP):
        gather(d).wait_send()
    for j in range(N_TP):
        forward(j).wait_send()
    for j in range(parts):
        for a in range(2):

            @pl.when(jnp.logical_not(is_home(j, a)))
            def _():
                send_home(j, a).wait_send()


def out_exchange(attended, out_weight, rows):
    part = rows.shape[-1]
    parts = out_weight.shape[1]
    vm = pl.BlockSpec(memory_space=pltpu.VMEM)
    anywhere = pl.BlockSpec(memory_space=pl.ANY)
    return pl.pallas_call(
        out_kernel,
        out_shape=jax.ShapeDtypeStruct((2, CH, part), jnp.bfloat16),
        in_specs=[vm, anywhere, vm],
        out_specs=vm,
        scratch_shapes=[
            pltpu.VMEM((N_TP, 4, OFF, 2 * HS), jnp.bfloat16),
            pltpu.VMEM((N_TP, parts, 2 * HS, part), jnp.bfloat16),
            pltpu.VMEM((parts, 2, 2, OFF, part), jnp.bfloat16),
            pltpu.SemaphoreType.DMA((N_TP,)),
            pltpu.SemaphoreType.DMA((N_TP,)),
            pltpu.SemaphoreType.DMA((N_TP,)),
            pltpu.SemaphoreType.DMA((N_TP,)),
            pltpu.SemaphoreType.DMA((N_TP,)),
            pltpu.SemaphoreType.DMA((parts, 2)),
            pltpu.SemaphoreType.DMA((PAIRS,)),
        ],
        compiler_params=pltpu.CompilerParams(
            collective_id=3, has_side_effects=True, vmem_limit_bytes=40 * 2**20
        ),
        name="out",
    )(attended, out_weight, rows)


def place_frames(text_embed, frame_features, frame_positions, slot_of, projector):
    tok_rows, part = text_embed.shape
    tokens = frame_positions.shape[0]
    spans = jnp.arange(slot_of.shape[0], dtype=jnp.int32)
    slot = jnp.sum(
        jnp.where((frame_positions // CH)[:, None] == spans[None, :], slot_of[None, :], 0), axis=1
    )
    target = slot // 2
    target_row = slot % 2 * CH + frame_positions % CH
    index = jnp.arange(tokens, dtype=jnp.int32)
    earlier = jnp.logical_and(target[None, :] == target[:, None], index[None, :] < index[:, None])
    place = jnp.sum(earlier.astype(jnp.int32), axis=1)
    entry = target * CAP + place
    entries = N_CTX * CAP
    chosen = jnp.arange(entries, dtype=jnp.int32)[:, None] == entry[None, :]
    sorted_features = jnp.dot(
        chosen.astype(jnp.bfloat16), frame_features, preferred_element_type=jnp.float32
    ).astype(jnp.bfloat16)
    row = jnp.sum(jnp.where(chosen, target_row[None, :] + 1, 0), axis=1) - 1
    projected = jax.nn.gelu(
        jnp.dot(sorted_features, projector, preferred_element_type=jnp.float32), approximate=False
    ).astype(jnp.bfloat16)
    outgoing = jnp.transpose(
        projected.reshape(N_CTX, CAP, N_TP, part), (0, 2, 1, 3)
    )
    row = row.reshape(N_CTX, 1, CAP, 1)
    high = jnp.broadcast_to(jnp.where(row < 0, -1, row // 32), (N_CTX, N_TP, CAP, 32))
    low = jnp.broadcast_to(jnp.where(row < 0, 0, row % 32), (N_CTX, N_TP, CAP, 32))
    outgoing = jnp.concatenate(
        [outgoing, high.astype(jnp.bfloat16), low.astype(jnp.bfloat16)], axis=3
    )
    arrived = lax.all_to_all(
        outgoing.reshape(N_CTX * N_TP, CAP, part + 64),
        ("ctx", "tp"),
        split_axis=0,
        concat_axis=0,
        tiled=True,
    ).reshape(N_CTX * N_TP * CAP, part + 64)
    at = (
        arrived[:, part].astype(jnp.float32) * 32.0 + arrived[:, part + 32].astype(jnp.float32)
    ).astype(jnp.int32)
    hit = jnp.arange(tok_rows, dtype=jnp.int32)[:, None] == at[None, :]
    inserted = jnp.dot(
        hit.astype(jnp.bfloat16), arrived[:, :part], preferred_element_type=jnp.float32
    ).astype(jnp.bfloat16)
    return jnp.where(jnp.any(hit, axis=1)[:, None], inserted, text_embed)


def per_device(
    text_embed,
    frame_features,
    frame_positions,
    span_order,
    projector,
    norm_gain,
    query_weight,
    key_weight,
    value_weight,
    out_weight,
):
    tok_rows, part = text_embed.shape
    c = lax.axis_index("ctx")
    t = lax.axis_index("tp")
    pair = c // 2
    core = c % 2
    q_half = lax.all_gather(lax.dynamic_slice_in_dim(query_weight, core * HS, HS, 1), "tp")
    out_cols = out_weight.shape[1] // 2
    out_half = jnp.transpose(
        lax.dynamic_slice_in_dim(out_weight, core * out_cols, out_cols, 1).reshape(
            2 * HS, N_TP // 2, part
        ),
        (1, 0, 2),
    )
    out_half = lax.all_gather(out_half, "tp")

    slots = span_order.shape[0]
    index = jnp.arange(slots, dtype=jnp.int32)
    slot_of = jnp.sum(
        jnp.where(span_order[None, :] == index[:, None], index[None, :], 0), axis=1
    )
    placed = place_frames(text_embed, frame_features, frame_positions, slot_of, projector)
    gain = jnp.broadcast_to(norm_gain[None, :], (16, part))
    rows, normed = rows_exchange(placed.reshape(2, PAIRS, OFF, part), gain)

    spans = lax.dynamic_slice_in_dim(span_order, 4 * t, 4, 0)
    positions = (
        spans[:, None] * CH + OFF * pair + jnp.arange(OFF, dtype=jnp.int32)[None, :]
    ).reshape(-1)
    half = HS // 2
    freqs = 1000000.0 ** (-(jnp.arange(half, dtype=jnp.float32) * 2.0 / HS))
    angles = positions.astype(jnp.float32)[:, None] * freqs[None, :]
    cos = jnp.cos(angles)
    sin = jnp.sin(angles)
    cosine = jnp.concatenate([cos, cos], axis=1)
    sine = jnp.concatenate([-sin, sin], axis=1)
    kv_cosine = jnp.where(core == 0, cosine, 1.0)
    kv_sine = jnp.where(core == 0, sine, 0.0)
    query, kv = qkv_exchange(
        normed, q_half, key_weight, value_weight, (cosine, sine, kv_cosine, kv_sine)
    )
    kv_all = lax.all_gather(kv.reshape(32, OFF, HS), "ctx").reshape(PAIRS, 2, 32, OFF, HS)
    attended = attention(
        slot_of, (HALF * c).reshape(1), query.reshape(2, 32, HALF, HS), kv_all
    )
    mixed = out_exchange(attended, out_half, rows)
    return mixed.reshape(tok_rows, part)


def solution(mesh):
    in_specs = (
        P("ctx", "tp"),
        P(("ctx", "tp"), None),
        P(("ctx", "tp")),
        P(),
        P(),
        P("tp"),
        P(None, "tp"),
        P(),
        P(),
        P("tp", None),
    )
    out_specs = P("ctx", "tp")
    return jax.shard_map(
        per_device, mesh=mesh, in_specs=in_specs, out_specs=out_specs, check_vma=False
    )
```

time: 685 us -> 433 us (0.63); the launches traced: 678 us -> 433 us
  Pallas kernels: 0 us -> 182 us
  matrix products: 173 us -> 8.61 us
  other arithmetic: 119 us -> 3.92 us
  local copies, waits for them, and re-layouts: 86.7 us -> 28.3 us
  waiting for transfers between devices: 227 us -> 186 us
  blocking collectives: 36.7 us -> 0 us
  starting transfers between devices: 20.7 us -> 10.7 us
    pallas_call x0 -> x4, Pallas kernels: none -> 182 us  [the longest x1 60 us: rows_exchange(): pl.pallas_call(rows_kernel, out_shape=(jax.ShapeDtypeStruct((2, N_TP, 2,...]
    dot_general x35 -> x2, matrix products: 173 us -> 8.61 us  [the longest x1 7.37 us: place_frames(): jnp.dot(sorted_features, projector, preferred_element_type=jnp.float32)]
    reduce_scatter x1 -> x0, waiting for transfers between devices: 102 us -> none  [per_device(): lax.psum_scatter(partial_sum.astype(jnp.bfloat16), 'tp', scatter_dimensio...]
    reduce_sum x18 -> x4, other arithmetic: 74 us -> 0.48 us  [the longest x1 0.17 us: place_frames(): place = jnp.sum(earlier.astype(jnp.int32), axis=1)]
    all_gather x3, waiting for transfers between devices: 113 us -> 170 us  [the longest x1 75.9 us: per_device(): out_half = lax.all_gather(out_half, 'tp')]
    while x113 -> x0, local copies, waits for them, and re-layouts: 40 us -> none
    all_gather x1 -> x0, blocking collectives: 21.5 us -> none  [per_device(): pos_piece = lax.all_gather(positions, 'ctx', axis=0, tiled=True)]
    convert_element_type x6 -> x3, other arithmetic: 19.3 us -> 0.11 us  [the longest x1 0.07 us: per_device(): angles = positions.astype(jnp.float32)[:, None] * freqs[None, :]]
  transfers between devices with their start and end apart: 6 -> 4, of which waited for: 5 -> 4; matrix products, arithmetic and copies ran while one was open for 8% -> 7% of each run, Pallas kernels for 0% -> 20%
where the time goes in v1:
time: 433 us
  waiting for transfers between devices  186 us (43%)
  Pallas kernels  182 us (42%)
  local copies, waits for them, and re-layouts  28.3 us (7%)
  between operations  13.4 us (3%)
  starting transfers between devices  10.7 us (2%)
  matrix products  8.61 us (2%)
    all_gather x1, waiting for transfers between devices, per_device(): out_half = lax.all_gather(out_half, 'tp')  75.9 us
    pallas_call x1, Pallas kernels, rows_exchange(): pl.pallas_call(rows_kernel, out_shape=(jax.ShapeDtypeStruct((2, N_TP, 2,...  60 us
    pallas_call x1, Pallas kernels, out_exchange(): pl.pallas_call(out_kernel, out_shape=jax.ShapeDtypeStruct((2, CH, part),...  49.5 us
    all_gather x1, waiting for transfers between devices, per_device(): lax.all_gather(lax.dynamic_slice_in_dim(query_weight, core * HS, HS, 1),...  47.9 us
    all_gather x1, waiting for transfers between devices, per_device(): lax.all_gather(kv.reshape(32, OFF, HS), 'ctx')  46.1 us
    pallas_call x1, Pallas kernels, attention(): pl.pallas_call(attention_kernel, out_shape=jax.ShapeDtypeStruct((32, HALF...  45 us
    pallas_call x1, Pallas kernels, qkv_exchange(): pl.pallas_call(qkv_kernel, out_shape=(jax.ShapeDtypeStruct((2, N_TP, 4, H...  27.8 us
    all_to_all x1, waiting for transfers between devices, place_frames(): lax.all_to_all(outgoing.reshape(N_CTX * N_TP, CAP, part + 64), ('ctx', 't...  15.8 us
  transfers between devices with their start and end apart: 4, of which 4 were waited for; matrix products, arithmetic and copies ran while one was open for 7% of the time, Pallas kernels for 20%

profile of v1, /device:TPU:29, one launch (start us, length us, event | category | flops | bytes accessed | tf_op | source)
XLA Modules:
  0.0 432.9 jit_solution(59528832121053432)
XLA Ops:
  6.5 0.0 copy-start
  6.5 0.0 all-gather.8.cloned.1.call-start
  6.5 1.5 copy-done
  8.0 1.0 constant_dynamic-slice_fusion
  9.0 0.0 all-gather.8.cloned.1.call-update
  9.0 0.0 all-gather.10.cloned.1.call-start
  9.1 1.2 constant_dynamic-slice_fusion.1
  10.3 0.0 copy-start.10
  10.4 0.0 copy-start.9
  10.4 0.0 copy-start.12
  10.4 1.3 copy.36
  11.7 0.0 all-gather.10.cloned.1.call-update
  11.7 0.0 copy-done.10
  11.7 0.1 select_reduce_fusion.2.slot_of
  11.9 0.0 copy-done.9
  11.9 0.1 select_reduce_fusion.1
  12.0 0.2 convert_reduce_fusion
  12.2 0.1 select_reduce_fusion
  12.3 0.1 sub.29
  12.4 0.0 copy-done.12
  12.4 7.4 %fusion.5 = bf16[128,3584]{1,0:T(8,128)(2,1)S(1)} fusion(bf16[1152,3584]{1,0:T(8,128)(2,1)} %param.14, bf16[64,1152]{1,0:T(8,128)(2,1)S(1)} %copy-done.12, s32[64]{0:T(128)S(1)} %multiply_add_fusion.1), kind=kOutput, calls=%fused_computation.8 | convolution fusion | flops 1105813504 | bytes 9322752 | tf_op jit(solution)/shard_map/dot_general | solution.py:531
  19.8 1.2 reshape.210
  21.0 0.4 copy.38
  21.4 0.1 broadcast_in_dim.96
  21.5 0.1 broadcast_in_dim.97
  21.6 1.3 pad_maximum_fusion
  22.9 10.6 %all-to-all-start = ((bf16[128,8,512]{2,1,0:T(8,128)(2,1)}), bf16[128,8,512]{2,1,0:T(8,128)(2,1)S(1)}, u32[]{:S(2)}, u32[]{:S(2)}) async-start(bf16[128,8,512]{2,1,0:T(8,128)(2,1)} %bitcast.2), calls=%async_computation | async-start | bytes 2097152 | tf_op jit(solution)/shard_map/all_to_all | solution.py:542
  33.5 0.0 copy-start.11
  33.5 0.0 all-gather.6.cloned.1.call-start
  33.6 0.1 multiply_add_fusion
  33.7 0.1 add_convert_fusion.1
  33.8 0.1 convert_element_type.69
  33.9 0.5 fusion.17
  34.4 0.8 broadcast_select_fusion
  35.2 15.8 %all-to-all-done = bf16[128,8,512]{2,1,0:T(8,128)(2,1)S(1)} async-done(((bf16[128,8,512]{2,1,0:T(8,128)(2,1)}), bf16[128,8,512]{2,1,0:T(8,128)(2,1)S(1)}, u32[]{:S(2)}, u32[]{:S(2)}) %all-to-all-start) | async-done | bytes 1048608 | tf_op jit(solution)/shard_map/all_to_all | solution.py:542
  51.0 0.2 fusion.30
  51.2 0.1 copy.34
  51.3 0.1 copy.35
  51.5 0.6 fusion.1
  52.1 0.0 copy-done.11
  52.1 1.2 fusion.14
  53.3 0.0 copy-start.8
  53.3 0.5 copy.30
  53.9 0.1 copy-done.8
  54.0 60.0 %rows.1 = (bf16[2,8,2,64,448]{4,3,2,1,0:T(8,128)(2,1)S(1)}, bf16[8,2,128,448]{3,2,1,0:T(8,128)(2,1)S(1)}) custom-call(bf16[2,8,64,448]{3,2,1,0:T(8,128)(2,1)S(1)} %bitcast.21, bf16[16,448]{1,0:T(8,128)(2,1)S(1)} %broadcast_in_dim.99.gain), custom_call_target="tpu_custom_call" | custom-call | tf_op jit(solution)/shard_map/rows/pallas_call | solution.py:123
  114.0 0.0 copy-start.5
  114.1 1.4 copy-done.5
  115.4 47.9 %all-gather.8.cloned.1.call-done = bf16[28672,128]{1,0:T(8,128)(2,1)} async-done(((bf16[3584,128]{1,0:T(8,128)(2,1)}), bf16[28672,128]{1,0:T(8,128)(2,1)}) %all-gather.8.cloned.1.call-update) | async-done | bytes 7340048 | tf_op jit(solution)/shard_map/all_gather | solution.py:576
  163.3 0.0 copy-start.3
  163.3 2.0 copy-done.3
  165.4 2.0 copy-done.4
  167.4 0.9 copy-done.7
  168.3 27.8 %qkv.1 = (bf16[2,8,4,32,128]{4,3,2,1,0:T(8,128)(2,1)S(1)}, bf16[8,4,64,128]{3,2,1,0:T(8,128)(2,1)}) custom-call(bf16[8,2,128,448]{3,2,1,0:T(8,128)(2,1)S(1)} %get-tuple-element.9.normed, bf16[8,3584,128]{2,1,0:T(8,128)(2,1)} %bitcast.24, bf16[3584,512]{1,0:T(8,128)(2,1)S(1)} %copy-done.3, bf16[3584,512]{1,0:T(8,128)(2,1)S(1)} %copy-done.4, ...), custom_call_target="tpu_custom_call" | custom-call | tf_op jit(solution)/shard_map/qkv/pallas_call | solution.py:273
  196.1 0.0 all-gather.6.cloned.1.call-update
  196.1 75.9 %all-gather.10.cloned.1.call-done = bf16[32,256,448]{1,2,0:T(8,128)(2,1)} async-done(((bf16[4,256,448]{1,2,0:T(8,128)(2,1)}), bf16[32,256,448]{1,2,0:T(8,128)(2,1)}) %all-gather.10.cloned.1.call-update) | async-done | bytes 7340048 | tf_op jit(solution)/shard_map/all_gather | solution.py:584
  272.0 10.9 %copy.32 = bf16[32,256,448]{2,1,0:T(8,128)(2,1)} copy(bf16[32,256,448]{1,2,0:T(8,128)(2,1)} %all-gather.10.cloned.1.call-done) | data formatting | bytes 14680064 | tf_op jit(solution)/shard_map/all_gather | solution.py:584
  282.9 46.1 %all-gather.6.cloned.1.call-done = bf16[16,32,64,128]{3,2,1,0:T(8,128)(2,1)} async-done(((bf16[1,32,64,128]{3,2,1,0:T(8,128)(2,1)}), bf16[16,32,64,128]{3,2,1,0:T(8,128)(2,1)}) %all-gather.6.cloned.1.call-update) | async-done | bytes 8388624 | tf_op jit(solution)/shard_map/all_gather | solution.py:611
  328.9 45.0 %attention.1.attended = bf16[32,32,256]{2,1,0:T(8,128)(2,1)S(1)} custom-call(s32[32]{0:T(128)S(1)} %select_reduce_fusion.2.slot_of, s32[1]{0:T(128)} %bitcast.offset, bf16[2,32,32,128]{3,2,1,0:T(8,128)(2,1)S(1)} %bitcast.22, bf16[8,2,32,64,128]{4,3,2,1,0:T(8,128)(2,1)} %bitcast.23), custom_call_target="tpu_custom_call" | custom-call | tf_op jit(solution)/shard_map/attention/pallas_call | solution.py:352
  373.9 0.0 copy-done.2
  373.9 0.0 copy-start.6
  373.9 1.6 copy-done.6
  375.5 49.5 %out.1 = bf16[2,512,448]{2,1,0:T(8,128)(2,1)S(1)} custom-call(bf16[32,32,256]{2,1,0:T(8,128)(2,1)S(1)} %attention.1.attended, bf16[8,4,256,448]{3,2,1,0:T(8,128)(2,1)S(1)} %bitcast.19, bf16[2,8,2,64,448]{4,3,2,1,0:T(8,128)(2,1)S(1)} %copy-done.6), custom_call_target="tpu_custom_call" | custom-call | tf_op jit(solution)/shard_map/out/pallas_call | solution.py:487
  425.1 1.3 copy.33
  426.3 0.0 copy-done.1
  (12 shorter events, 0.1 us)
Async XLA Ops:
  6.5 1.5 copy-start
  6.5 156.8 %all-gather.8.cloned.1.call-start = ((), (), s32[]{:S(2)}) async-start(), calls=%async_computation.2 | async-start | bytes 8257536 | tf_op jit(solution)/shard_map/all_gather | solution.py:576
  9.0 262.9 %all-gather.10.cloned.1.call-start = ((), (), s32[]{:S(2)}) async-start(), calls=%async_computation.3 | async-start | bytes 8257536 | tf_op jit(solution)/shard_map/all_gather | solution.py:584
  10.3 1.4 copy-start.10
  10.4 1.5 copy-start.9
  10.4 2.0 copy-start.12
  22.9 28.1 %all-to-all-start = ((bf16[128,8,512]{2,1,0:T(8,128)(2,1)}), bf16[128,8,512]{2,1,0:T(8,128)(2,1)S(1)}, u32[]{:S(2)}, u32[]{:S(2)}) async-start(bf16[128,8,512]{2,1,0:T(8,128)(2,1)} %bitcast.2), calls=%async_computation | async-start | bytes 2097152 | tf_op jit(solution)/shard_map/all_to_all | solution.py:542
  33.5 18.6 %copy-start.11 = (bf16[1024,448]{0,1:T(8,128)(2,1)S(1)}, bf16[1024,448]{0,1:T(8,128)(2,1)}, u32[]{:S(2)}) copy-start(bf16[1024,448]{0,1:T(8,128)(2,1)} %param.10) | copy-start | bytes 2752516
  33.5 295.4 %all-gather.6.cloned.1.call-start = ((), (), s32[]{:S(2)}) async-start(), calls=%async_computation.1 | async-start | bytes 8912896 | tf_op jit(solution)/shard_map/all_gather | solution.py:611
  53.3 0.7 copy-start.8
  114.0 1.4 copy-start.5
  163.3 2.0 copy-start.3
  165.4 2.0 copy-start.4
  167.4 0.9 copy-start.7
  328.9 45.0 %copy-start.2 = (bf16[32,256,448]{2,1,0:T(8,128)(2,1)S(1)}, bf16[32,256,448]{2,1,0:T(8,128)(2,1)}, u32[]{:S(2)}) copy-start(bf16[32,256,448]{2,1,0:T(8,128)(2,1)} %copy.32) | copy-start | bytes 22020100
  373.9 1.6 copy-start.6
  375.5 50.8 %copy-start.1 = (bf16[3584,256]{1,0:T(8,128)(2,1)S(1)}, bf16[3584,256]{1,0:T(8,128)(2,1)}, u32[]{:S(2)}) copy-start(bf16[3584,256]{1,0:T(8,128)(2,1)} %param.16) | copy-start | bytes 5505028
Sparse Core Ops, SparseCore 0:
  9.7 153.6 all-gather.7
  165.6 106.3 all-gather.9
  273.7 55.2 all-gather.5

commit v2 on v1

--- a/solution.py
+++ b/solution.py
@@ -35,40 +35,25 @@
 def rows_kernel(placed, gain, rows, normed, gains, send, recv, fsend, frecv, gsend, grecv):
     c = lax.axis_index("ctx")
     t = lax.axis_index("tp")
-    pair = c // 2
     core = c % 2
-    sibling = pair * 2 + 1 - core
-    own = t == pair
+    sibling = c + 1 - 2 * core
     barrier = pltpu.get_barrier_semaphore()
     signal(barrier, sibling, t)
-    for j in range(N_TP):
-        if_self = jnp.logical_and(own, j == t)
-
-        @pl.when(jnp.logical_not(if_self))
-        def _():
-            signal(barrier, 2 * t + core, j)
-
-    pl.semaphore_wait(barrier, jnp.where(own, PAIRS, PAIRS + 1))
+    for d in range(1, N_TP):
+        signal(barrier, c, lax.rem(t + d, N_TP))
+    pl.semaphore_wait(barrier, N_TP)
 
     def block(d):
-        e = lax.rem(pair + d, PAIRS)
-        return push(placed.at[:, e], rows.at[core, t], send.at[d], recv.at[t], 2 * e + core, pair)
+        j = lax.rem(t + d, N_TP)
+        return push(placed.at[:, j], rows.at[core, t], send.at[d], recv.at[t], c, j)
 
     def gain_block(d):
-        e = lax.rem(pair + d, PAIRS)
-        return push(gain, gains.at[t], gsend.at[d], grecv.at[t], 2 * e + core, pair)
-
-    @pl.when(own)
-    def _():
-        pltpu.make_async_copy(placed.at[:, pair], rows.at[core, t], recv.at[t]).start()
-        pltpu.make_async_copy(gain, gains.at[t], grecv.at[t]).start()
-
-    @pl.when(jnp.logical_not(own))
-    def _():
-        block(0).start()
-        gain_block(0).start()
-
-    for d in range(1, PAIRS):
+        j = lax.rem(t + d, N_TP)
+        return push(gain, gains.at[t], gsend.at[d], grecv.at[t], c, j)
+
+    pltpu.make_async_copy(placed.at[:, t], rows.at[core, t], recv.at[t]).start()
+    pltpu.make_async_copy(gain, gains.at[t], grecv.at[t]).start()
+    for d in range(1, N_TP):
         block(d).start()
         gain_block(d).start()
 
@@ -104,11 +89,6 @@
     for j in range(N_TP):
         receive(j)
     normalise(1 - core)
-
-    @pl.when(jnp.logical_not(own))
-    def _():
-        block(0).wait_send()
-        gain_block(0).wait_send()
 
     for d in range(1, PAIRS):
         block(d).wait_send()
@@ -173,18 +153,20 @@
     for j in range(N_TP):
         load(j).start()
 
+    own = t == pair
     barrier = pltpu.get_barrier_semaphore()
     for k in range(2):
-        for d in range(N_TP):
+        for d in range(PAIRS):
+            e = lax.rem(pair + d, PAIRS)
             if d == 0:
 
-                @pl.when(core != k)
+                @pl.when(jnp.logical_not(jnp.logical_and(own, core == k)))
                 def _():
-                    signal(barrier, 2 * pair + k, t)
+                    signal(barrier, 2 * e + k, pair)
 
             else:
-                signal(barrier, 2 * pair + k, lax.rem(t + d, N_TP))
-    pl.semaphore_wait(barrier, 2 * N_TP - 1)
+                signal(barrier, 2 * e + k, pair)
+    pl.semaphore_wait(barrier, 2 * N_TP - jnp.where(own, 1, 0))
 
     part = normed.shape[-1]
 
@@ -203,13 +185,13 @@
 
     def kv_push(d):
         j = lax.rem(t + d, N_TP)
-        return push(kv.at[j // 2], kv_out.at[t], ksend.at[d], krecv.at[t], c, j)
+        return push(kv.at[j // 2], kv_out.at[pair], ksend.at[d], krecv.at[pair], 2 * t + core, j)
 
     def q_push(d, k):
         j = lax.rem(t + d, N_TP)
         return push(
-            query.at[j, :, pl.ds(k * HALF, HALF), :], query_out.at[core, t],
-            qsend.at[d, k], qrecv.at[core, t], 2 * pair + k, j,
+            query.at[j, :, pl.ds(k * HALF, HALF), :], query_out.at[core, pair],
+            qsend.at[d, k], qrecv.at[core, pair], 2 * t + k, j,
         )
 
     pltpu.make_async_copy(key_weight, kv_slot, wsem.at[N_TP]).wait()
@@ -218,7 +200,15 @@
         kv[h] = rotated(total[:, h * HS : (h + 1) * HS], kv_cosine[...], kv_sine[...]).reshape(
             4, OFF, HS
         )
-    pltpu.make_async_copy(kv.at[t // 2], kv_out.at[t], krecv.at[t]).start()
+
+    @pl.when(own)
+    def _():
+        pltpu.make_async_copy(kv.at[t // 2], kv_out.at[pair], krecv.at[pair]).start()
+
+    @pl.when(jnp.logical_not(own))
+    def _():
+        kv_push(0).start()
+
     for d in range(1, N_TP):
         kv_push(d).start()
     for g in range(2):
@@ -232,33 +222,40 @@
     for d in range(N_TP):
         for k in range(2):
             if d == 0:
-
-                @pl.when(core == k)
+                here = jnp.logical_and(own, core == k)
+
+                @pl.when(here)
                 def _():
                     pltpu.make_async_copy(
-                        query.at[t, :, pl.ds(k * HALF, HALF), :], query_out.at[core, t],
-                        qrecv.at[core, t],
+                        query.at[t, :, pl.ds(k * HALF, HALF), :], query_out.at[core, pair],
+                        qrecv.at[core, pair],
                     ).start()
 
-                @pl.when(core != k)
+                @pl.when(jnp.logical_not(here))
                 def _():
                     q_push(0, k).start()
 
             else:
                 q_push(d, k).start()
-    for j in range(N_TP):
-        push(kv.at[0], kv_out.at[j], ksend.at[0], krecv.at[j], c, t).wait_recv()
+    for e in range(PAIRS):
+        push(kv.at[0], kv_out.at[e], ksend.at[0], krecv.at[e], c, t).wait_recv()
         for k in range(2):
             push(
-                query_out.at[k, j], query_out.at[k, j], qsend.at[0, 0], qrecv.at[k, j], c, t
+                query_out.at[k, e], query_out.at[k, e], qsend.at[0, 0], qrecv.at[k, e], c, t
             ).wait_recv()
     for d in range(N_TP):
-        if d > 0:
+        if d == 0:
+
+            @pl.when(jnp.logical_not(own))
+            def _():
+                kv_push(0).wait_send()
+
+        else:
             kv_push(d).wait_send()
         for k in range(2):
             if d == 0:
 
-                @pl.when(core != k)
+                @pl.when(jnp.logical_not(jnp.logical_and(own, core == k)))
                 def _():
                     q_push(0, k).wait_send()
 
@@ -295,79 +292,174 @@
     )(normed, query_weight, key_weight, value_weight, *tables)
 
 
-def attention_kernel(slot_of, offset, query, kv, out):
+def attention_kernel(
+    slot_of, query, kv_own, out, kv, q, summed, largest, total, send, recv, pass_send,
+):
     scale = LOG2E / math.sqrt(HS)
-    first = offset[0]
-
-    def chunk(i, unused):
-        q = jnp.concatenate(
-            [query[:, slot_of[4 * i + a]].reshape(2 * HALF, HS) for a in range(4)], axis=0
-        )
-
-        def keys_of(j, which):
-            return jnp.concatenate(
-                [kv[:, which, slot_of[4 * j + a]].reshape(CH, HS) for a in range(4)], axis=0
+    c = lax.axis_index("ctx")
+    t = lax.axis_index("tp")
+    pair = c // 2
+    core = c % 2
+    sibling = c + 1 - 2 * core
+    base = pair // 4 * 4
+    other = 4 - base
+    z = pair % 4
+    up = lax.rem(z + 1, 4)
+    down = lax.rem(z + 3, 4)
+    far = lax.rem(z + 2, 4)
+    z_up, z_down, z_far = base + up, base + down, base + far
+    x_own, x_up, x_down, x_far = other + z, other + up, other + down, other + far
+
+    barrier = pltpu.get_barrier_semaphore()
+    signal(barrier, sibling, t)
+    for e in (z_up, z_down, z_far, x_own):
+        signal(barrier, 2 * e + core, t)
+    for j in range(32):
+        kv[pair, core, j * OFF : (j + 1) * OFF] = kv_own[slot_of[j]]
+    pl.semaphore_wait(barrier, 5)
+
+    def transfer(e, to, index):
+        block = kv.at[e, core]
+        return push(block, block, send.at[index], recv.at[e, core], 2 * to + core, t)
+
+    def share(e):
+        block = kv.at[e, core]
+        return push(block, block, pass_send.at[e], recv.at[e, core], sibling, t)
+
+    def arrive(e, which):
+        block = kv.at[e, which]
+        push(block, block, send.at[0], recv.at[e, which], sibling, t).wait_recv()
+
+    share(pair).start()
+    moves = (
+        (pair, x_own), (pair, z_up), (pair, z_down), (pair, z_far),
+        (x_own, z_up), (x_own, z_down), (z_far, x_own),
+    )
+    for index in range(3):
+        transfer(*moves[index], index).start()
+    for j in range(32):
+        q[j * OFF : (j + 1) * OFF] = query[:, slot_of[j]].reshape(2 * HALF, HS)
+
+    rows = 8 * HALF
+    row = lax.broadcasted_iota(jnp.int32, (rows, 1), 0)
+    limit = row // OFF * CH + HALF * c + row % HALF
+    col = lax.broadcasted_iota(jnp.int32, (1, 4 * OFF), 1)
+
+    def update(e, first):
+        at = col // OFF * CH + OFF * e + col % OFF
+        for i in range(8):
+            here = slice(i * rows, (i + 1) * rows)
+            width = 4 * OFF * (i + 1)
+            s = lax.dot_general(
+                q[here], kv[e, 0, :width], (((1,), (1,)), ((), ())),
+                preferred_element_type=jnp.float32,
             )
-
-        def scores_of(j):
-            return lax.dot_general(
-                q, keys_of(j, 0), (((1,), (1,)), ((), ())), preferred_element_type=jnp.float32
+            edge = jnp.where(at <= limit, s[:, width - 4 * OFF :], -1e30)
+            s = edge if i == 0 else jnp.concatenate([s[:, : width - 4 * OFF], edge], axis=1)
+            top = jnp.max(s, axis=1, keepdims=True)
+            if not first:
+                top = jnp.maximum(top, largest[here])
+            weights = jnp.exp2((s - top) * scale)
+            added = jnp.sum(weights, axis=1, keepdims=True)
+            product = jnp.dot(
+                weights.astype(jnp.bfloat16), kv[e, 1, :width], preferred_element_type=jnp.float32
             )
-
-        def update(state, s, j):
-            largest_old, total_old, summed_old = state
-            largest = jnp.maximum(largest_old, jnp.max(s, axis=1, keepdims=True))
-            weights = jnp.exp2((s - largest) * scale)
-            factor = jnp.exp2((largest_old - largest) * scale)
-            total = total_old * factor + jnp.sum(weights, axis=1, keepdims=True)
-            summed = summed_old * factor + jnp.dot(
-                weights.astype(jnp.bfloat16), keys_of(j, 1), preferred_element_type=jnp.float32
-            )
-            return largest, total, summed
-
-        rows = 8 * HALF
-        initial = (
-            jnp.full((rows, 1), -1e30, jnp.float32),
-            jnp.zeros((rows, 1), jnp.float32),
-            jnp.zeros((rows, HS), jnp.float32),
-        )
-        s = scores_of(i)
-        row = lax.broadcasted_iota(jnp.int32, (rows, 1), 0)
-        limit = row // (2 * HALF) * CH + first + row % HALF
-        col = lax.broadcasted_iota(jnp.int32, s.shape, 1)
-        s = jnp.where(col <= limit, s, -1e30)
-        state = update(initial, s, i)
-        state = lax.fori_loop(0, i, lambda j, st: update(st, scores_of(j), j), state)
-        attended = (state[2] / state[1]).astype(jnp.bfloat16).reshape(4, 2, HALF, HS)
+            if not first:
+                factor = jnp.exp2((largest[here] - top) * scale)
+                added = added + total[here] * factor
+                product = product + summed[here] * factor
+            largest[here] = top
+            total[here] = added
+            summed[here] = product
+
+    arrive(pair, 1 - core)
+    update(pair, True)
+    transfer(*moves[3], 3).start()
+    arrive(x_own, core)
+    transfer(*moves[4], 4).start()
+    transfer(*moves[5], 5).start()
+    share(x_own).start()
+    arrive(z_up, core)
+    share(z_up).start()
+    arrive(z_down, core)
+    share(z_down).start()
+
+    order = (x_own, z_up, z_down, x_up, x_down, z_far, x_far)
+
+    def step(n, unused):
+        e = order[6]
+        for index in range(6):
+            e = jnp.where(n == index, order[index], e)
+
+        @pl.when(n == 2)
+        def _():
+            arrive(x_up, core)
+            share(x_up).start()
+
+        @pl.when(n == 3)
+        def _():
+            arrive(x_down, core)
+            share(x_down).start()
+            arrive(z_far, core)
+            transfer(*moves[6], 6).start()
+            share(z_far).start()
+
+        @pl.when(n == 6)
+        def _():
+            arrive(x_far, core)
+            share(x_far).start()
+
+        arrive(e, 1 - core)
+        update(e, False)
+        return unused
+
+    lax.fori_loop(0, 7, step, 0)
+    for i in range(8):
+        here = slice(i * rows, (i + 1) * rows)
+        attended = (summed[here] / total[here]).astype(jnp.bfloat16).reshape(4, 2, HALF, HS)
         for a in range(4):
-            out[slot_of[4 * i + a]] = jnp.concatenate([attended[a, 0], attended[a, 1]], axis=1)
-        return unused
-
-    lax.fori_loop(0, 8, chunk, 0)
-
-
-def attention(slot_of, offset, query, kv):
+            out[4 * i + a] = jnp.concatenate([attended[a, 0], attended[a, 1]], axis=1)
+    for index in range(7):
+        transfer(*moves[index], index).wait_send()
+    for e in range(PAIRS):
+        share(e).wait_send()
+
+
+def attention(slot_of, query, kv):
     vm = pl.BlockSpec(memory_space=pltpu.VMEM)
     sm = pl.BlockSpec(memory_space=pltpu.SMEM)
+    keys = 32 * OFF
     return pl.pallas_call(
         attention_kernel,
         out_shape=jax.ShapeDtypeStruct((32, HALF, 2 * HS), jnp.bfloat16),
-        in_specs=[sm, sm, vm, vm],
+        in_specs=[sm, vm, vm],
         out_specs=vm,
-        compiler_params=pltpu.CompilerParams(vmem_limit_bytes=48 * 2**20),
+        scratch_shapes=[
+            pltpu.VMEM((PAIRS, 2, keys, HS), jnp.bfloat16),
+            pltpu.VMEM((keys, HS), jnp.bfloat16),
+            pltpu.VMEM((keys, HS), jnp.float32),
+            pltpu.VMEM((keys, 1), jnp.float32),
+            pltpu.VMEM((keys, 1), jnp.float32),
+            pltpu.SemaphoreType.DMA((7,)),
+            pltpu.SemaphoreType.DMA((PAIRS, 2)),
+            pltpu.SemaphoreType.DMA((PAIRS,)),
+        ],
+        compiler_params=pltpu.CompilerParams(
+            collective_id=4, has_side_effects=True, vmem_limit_bytes=48 * 2**20
+        ),
         name="attention",
-    )(slot_of, offset, query, kv)
+    )(slot_of, query, kv)
 
 
 def out_kernel(
-    attended, out_weight, rows, out, heads, weight, result,
+    span_order, attended, out_weight, rows, out, sorted_heads, heads, weight, result,
     wsem, hsend, hrecv, fsend, frecv, rsend, rrecv,
 ):
     c = lax.axis_index("ctx")
     t = lax.axis_index("tp")
     pair = c // 2
     core = c % 2
-    sibling = pair * 2 + 1 - core
+    sibling = c + 1 - 2 * core
     side = t // 4
     parts = out_weight.shape[1]
 
@@ -377,36 +469,52 @@
     for g in range(N_TP):
         load(g).start()
 
+    own = t == pair
+    home = side == core
     barrier = pltpu.get_barrier_semaphore()
     signal(barrier, sibling, t)
-    for d in range(1, N_TP):
-        signal(barrier, c, lax.rem(t + d, N_TP))
-    home = jnp.logical_and(t == pair, side == core)
-    for d in range(PAIRS):
-        e = lax.rem(pair + d, PAIRS)
+    for d in range(N_TP):
+        j = lax.rem(t + d, N_TP)
         if d == 0:
+
+            @pl.when(jnp.logical_not(own))
+            def _():
+                signal(barrier, 2 * t + core, j)
 
             @pl.when(jnp.logical_not(home))
             def _():
-                signal(barrier, 2 * e + side, pair)
+                signal(barrier, 2 * pair + side, j)
 
         else:
-            signal(barrier, 2 * e + side, pair)
-    pl.semaphore_wait(barrier, 1 + N_TP - 1 + 2 * parts - jnp.where(home, 1, 0))
+            signal(barrier, 2 * t + core, j)
+            signal(barrier, 2 * pair + side, j)
+    for j in range(32):
+        sorted_heads[j] = attended[span_order[j]]
+    pl.semaphore_wait(
+        barrier, 1 + PAIRS - jnp.where(own, 1, 0) + 2 * parts - jnp.where(home, 1, 0)
+    )
 
     mine = pl.ds(core * HALF, HALF)
     theirs = pl.ds((1 - core) * HALF, HALF)
 
     def gather(d):
-        j = lax.rem(t + d, N_TP)
+        e = lax.rem(pair + d, PAIRS)
         return push(
-            attended.at[pl.ds(4 * j, 4)], heads.at[t, :, mine, :], hsend.at[d], hrecv.at[t], c, j
+            sorted_heads.at[pl.ds(4 * e, 4)], heads.at[t, :, mine, :], hsend.at[d], hrecv.at[t],
+            2 * e + core, pair,
         )
 
-    pltpu.make_async_copy(
-        attended.at[pl.ds(4 * t, 4)], heads.at[t, :, mine, :], hrecv.at[t]
-    ).start()
-    for d in range(1, N_TP):
+    @pl.when(own)
+    def _():
+        pltpu.make_async_copy(
+            sorted_heads.at[pl.ds(4 * pair, 4)], heads.at[t, :, mine, :], hrecv.at[t]
+        ).start()
+
+    @pl.when(jnp.logical_not(own))
+    def _():
+        gather(0).start()
+
+    for d in range(1, PAIRS):
         gather(d).start()
 
     def forward(j):
@@ -415,7 +523,7 @@
         )
 
     for d in range(N_TP):
-        j = lax.rem(t + N_TP - d, N_TP)
+        j = lax.rem(t + d, N_TP)
         push(
             heads.at[j, :, mine, :], heads.at[j, :, mine, :], hsend.at[0], hrecv.at[j], sibling, t
         ).wait_recv()
@@ -432,8 +540,8 @@
 
     def send_home(j, a):
         return push(
-            result.at[j, a], out.at[:, pl.ds(OFF * pair, OFF), :], rsend.at[j, a], rrecv.at[pair],
-            2 * t + a, parts * core + j,
+            result.at[j, a], out.at[:, pl.ds(OFF * t, OFF), :], rsend.at[j, a], rrecv.at[t],
+            2 * pair + a, parts * core + j,
         )
 
     def is_home(j, a):
@@ -455,7 +563,7 @@
             @pl.when(is_home(j, a))
             def _():
                 pltpu.make_async_copy(
-                    result.at[j, a], out.at[:, pl.ds(OFF * pair, OFF), :], rrecv.at[pair]
+                    result.at[j, a], out.at[:, pl.ds(OFF * t, OFF), :], rrecv.at[t]
                 ).start()
 
             @pl.when(jnp.logical_not(is_home(j, a)))
@@ -467,7 +575,12 @@
             result.at[0, 0], out.at[:, pl.ds(OFF * e, OFF), :], rsend.at[0, 0], rrecv.at[e],
             sibling, t,
         ).wait_recv()
-    for d in range(1, N_TP):
+
+    @pl.when(jnp.logical_not(own))
+    def _():
+        gather(0).wait_send()
+
+    for d in range(1, PAIRS):
         gather(d).wait_send()
     for j in range(N_TP):
         forward(j).wait_send()
@@ -479,7 +592,7 @@
                 send_home(j, a).wait_send()
 
 
-def out_exchange(attended, out_weight, rows):
+def out_exchange(span_order, attended, out_weight, rows):
     part = rows.shape[-1]
     parts = out_weight.shape[1]
     vm = pl.BlockSpec(memory_space=pltpu.VMEM)
@@ -487,9 +600,10 @@
     return pl.pallas_call(
         out_kernel,
         out_shape=jax.ShapeDtypeStruct((2, CH, part), jnp.bfloat16),
-        in_specs=[vm, anywhere, vm],
+        in_specs=[pl.BlockSpec(memory_space=pltpu.SMEM), vm, anywhere, vm],
         out_specs=vm,
         scratch_shapes=[
+            pltpu.VMEM((32, HALF, 2 * HS), jnp.bfloat16),
             pltpu.VMEM((N_TP, 4, OFF, 2 * HS), jnp.bfloat16),
             pltpu.VMEM((N_TP, parts, 2 * HS, part), jnp.bfloat16),
             pltpu.VMEM((parts, 2, 2, OFF, part), jnp.bfloat16),
@@ -505,7 +619,7 @@
             collective_id=3, has_side_effects=True, vmem_limit_bytes=40 * 2**20
         ),
         name="out",
-    )(attended, out_weight, rows)
+    )(span_order, attended, out_weight, rows)
 
 
 def place_frames(text_embed, frame_features, frame_positions, slot_of, projector):
@@ -581,8 +695,6 @@
         ),
         (1, 0, 2),
     )
-    out_half = lax.all_gather(out_half, "tp")
-
     slots = span_order.shape[0]
     index = jnp.arange(slots, dtype=jnp.int32)
     slot_of = jnp.sum(
@@ -592,9 +704,9 @@
     gain = jnp.broadcast_to(norm_gain[None, :], (16, part))
     rows, normed = rows_exchange(placed.reshape(2, PAIRS, OFF, part), gain)
 
-    spans = lax.dynamic_slice_in_dim(span_order, 4 * t, 4, 0)
+    spans = lax.dynamic_slice_in_dim(span_order, 4 * pair, 4, 0)
     positions = (
-        spans[:, None] * CH + OFF * pair + jnp.arange(OFF, dtype=jnp.int32)[None, :]
+        spans[:, None] * CH + OFF * t + jnp.arange(OFF, dtype=jnp.int32)[None, :]
     ).reshape(-1)
     half = HS // 2
     freqs = 1000000.0 ** (-(jnp.arange(half, dtype=jnp.float32) * 2.0 / HS))
@@ -608,11 +720,12 @@
     query, kv = qkv_exchange(
         normed, q_half, key_weight, value_weight, (cosine, sine, kv_cosine, kv_sine)
     )
-    kv_all = lax.all_gather(kv.reshape(32, OFF, HS), "ctx").reshape(PAIRS, 2, 32, OFF, HS)
+    kv, out_half = lax.optimization_barrier((kv, out_half))
+    out_half = lax.all_gather(out_half, "tp")
     attended = attention(
-        slot_of, (HALF * c).reshape(1), query.reshape(2, 32, HALF, HS), kv_all
-    )
-    mixed = out_exchange(attended, out_half, rows)
+        slot_of, query.reshape(2, 32, HALF, HS), kv.reshape(32, OFF, HS)
+    )
+    mixed = out_exchange(span_order, attended, out_half, rows)
     return mixed.reshape(tok_rows, part)
 
 

time: 433 us -> 356 us (0.82); the launches traced: 433 us -> 349 us
  waiting for transfers between devices: 186 us -> 75.8 us
  Pallas kernels: 182 us -> 197 us
  local copies, waits for them, and re-layouts: 28.3 us -> 36.8 us
    all_gather x1 -> x0, waiting for transfers between devices: 46.1 us -> none  [per_device(): lax.all_gather(kv.reshape(32, OFF, HS), 'ctx')]
    all_gather x1, waiting for transfers between devices: 75.9 us -> 31.3 us  [per_device(): out_half = lax.all_gather(out_half, 'tp')]
    pallas_call x1, Pallas kernels: 45 us -> 74.7 us  [attention(): pl.pallas_call(attention_kernel, out_shape=jax.ShapeDtypeStruct((32, HALF...]
    pallas_call x1, Pallas kernels: 60 us -> 36 us  [rows_exchange(): pl.pallas_call(rows_kernel, out_shape=(jax.ShapeDtypeStruct((2, N_TP, 2,...]
    all_gather x1, waiting for transfers between devices: 47.9 us -> 31.1 us  [per_device(): lax.all_gather(lax.dynamic_slice_in_dim(query_weight, core * HS, HS, 1),...]
    pallas_call x1, Pallas kernels: 27.8 us -> 34.5 us  [qkv_exchange(): pl.pallas_call(qkv_kernel, out_shape=(jax.ShapeDtypeStruct((2, N_TP, 4, H...]
    unnamed x29 -> x27, local copies, waits for them, and re-layouts: 11.2 us -> 16.5 us
  transfers between devices with their start and end apart: 4 -> 3, of which waited for: 4 -> 3; matrix products, arithmetic and copies ran while one was open for 7% -> 7% of each run, Pallas kernels for 20% -> 32%
where the time goes in v2:
time: 356 us; the launch traced here: 349 us
  Pallas kernels  197 us (55%)
  waiting for transfers between devices  75.8 us (21%)
  local copies, waits for them, and re-layouts  36.8 us (10%)
  between operations  13.6 us (4%)
  matrix products  11.8 us (3%)
  starting transfers between devices  11.1 us (3%)
    pallas_call x1, Pallas kernels, attention(): pl.pallas_call(attention_kernel, out_shape=jax.ShapeDtypeStruct((32, HALF...  74.7 us
    pallas_call x1, Pallas kernels, out_exchange(): pl.pallas_call(out_kernel, out_shape=jax.ShapeDtypeStruct((2, CH, part),...  51.5 us
    pallas_call x1, Pallas kernels, rows_exchange(): pl.pallas_call(rows_kernel, out_shape=(jax.ShapeDtypeStruct((2, N_TP, 2,...  36 us
    pallas_call x1, Pallas kernels, qkv_exchange(): pl.pallas_call(qkv_kernel, out_shape=(jax.ShapeDtypeStruct((2, N_TP, 4, H...  34.5 us
    all_gather x1, waiting for transfers between devices, per_device(): out_half = lax.all_gather(out_half, 'tp')  31.3 us
    all_gather x1, waiting for transfers between devices, per_device(): lax.all_gather(lax.dynamic_slice_in_dim(query_weight, core * HS, HS, 1),...  31.1 us
    unnamed x27, local copies, waits for them, and re-layouts  16.5 us
    all_to_all x1, waiting for transfers between devices, place_frames(): lax.all_to_all(outgoing.reshape(N_CTX * N_TP, CAP, part + 64), ('ctx', 't...  13.5 us
  transfers between devices with their start and end apart: 3, of which 3 were waited for; matrix products, arithmetic and copies ran while one was open for 7% of the time, Pallas kernels for 32%

profile of v2, /device:TPU:29, one launch (start us, length us, event | category | flops | bytes accessed | tf_op | source)
XLA Modules:
  0.0 349.2 jit_solution(15842283740703437433)
XLA Ops:
  6.5 0.0 copy-start
  6.5 0.0 copy-start.8
  6.5 0.0 copy-start.10
  6.5 0.0 copy-start.11
  6.5 0.0 all-gather.5.cloned.1.call-start
  6.6 1.4 copy-done
  8.0 1.0 constant_dynamic-slice_fusion
  9.0 0.0 all-gather.5.cloned.1.call-update
  9.0 0.0 copy-done.8
  9.0 0.1 select_reduce_fusion.2.slot_of
  9.2 0.0 copy-done.10
  9.2 0.1 select_reduce_fusion.1
  9.3 0.2 convert_reduce_fusion
  9.5 0.1 select_reduce_fusion
  9.6 0.1 sub.29
  9.7 0.0 copy-done.11
  9.7 8.1 %fusion.5 = bf16[128,3584]{1,0:T(8,128)(2,1)} fusion(bf16[1152,3584]{1,0:T(8,128)(2,1)} %param.14, bf16[64,1152]{1,0:T(8,128)(2,1)S(1)} %copy-done.11, s32[64]{0:T(128)S(1)} %multiply_add_fusion.1), kind=kOutput, calls=%fused_computation.8 | convolution fusion | flops 1105813504 | bytes 9322752 | tf_op jit(solution)/shard_map/dot_general | solution.py:645
  17.8 2.3 reshape.206
  20.1 0.4 copy.38
  20.6 0.1 broadcast_in_dim.96
  20.7 0.1 broadcast_in_dim.97
  20.8 1.3 pad_maximum_fusion
  22.1 11.0 %all-to-all-start = ((bf16[128,8,512]{2,1,0:T(8,128)(2,1)}), bf16[128,8,512]{2,1,0:T(8,128)(2,1)}, u32[]{:S(2)}, u32[]{:S(2)}) async-start(bf16[128,8,512]{2,1,0:T(8,128)(2,1)} %bitcast.1), calls=%async_computation | async-start | bytes 2097152 | tf_op jit(solution)/shard_map/all_to_all | solution.py:656
  33.1 0.0 all-gather.7.cloned.1.call-start
  33.2 0.1 multiply_add_fusion
  33.3 0.1 add_convert_fusion.1
  33.4 0.1 convert_element_type.69
  33.5 1.2 constant_dynamic-slice_fusion.1
  34.7 1.3 copy.36
  36.0 0.5 fusion.17
  36.6 0.1 broadcast_select_fusion
  36.7 13.5 %all-to-all-done = bf16[128,8,512]{2,1,0:T(8,128)(2,1)} async-done(((bf16[128,8,512]{2,1,0:T(8,128)(2,1)}), bf16[128,8,512]{2,1,0:T(8,128)(2,1)}, u32[]{:S(2)}, u32[]{:S(2)}) %all-to-all-start) | async-done | bytes 1048608 | tf_op jit(solution)/shard_map/all_to_all | solution.py:656
  50.2 1.3 fusion.30
  51.4 0.1 copy.34
  51.5 0.2 copy.35
  51.7 0.6 fusion.1
  52.3 3.7 %fusion.14 = bf16[1024,448]{0,1:T(8,128)(2,1)} fusion(bf16[1024,448]{0,1:T(8,128)(2,1)} %param.10, s32[1024]{0:T(1024)S(1)} %bitcast.26, bf16[1024,512]{1,0:T(8,128)(2,1)} %bitcast.2, pred[1024]{0:T(1024)(128)(4,1)S(1)} %fusion.1), kind=kOutput, calls=%fused_computation.25 | convolution fusion | flops 941490176 | bytes 2888704 | tf_op jit(solution)/shard_map/dot_general | solution.py:667
  55.9 0.0 copy-start.9
  55.9 1.5 copy.30
  57.4 0.0 copy-done.9
  57.4 36.0 %rows.1 = (bf16[2,8,2,64,448]{4,3,2,1,0:T(8,128)(2,1)S(1)}, bf16[8,2,128,448]{3,2,1,0:T(8,128)(2,1)S(1)}) custom-call(bf16[2,8,64,448]{3,2,1,0:T(8,128)(2,1)S(1)} %bitcast.19, bf16[16,448]{1,0:T(8,128)(2,1)S(1)} %broadcast_in_dim.99.gain), custom_call_target="tpu_custom_call" | custom-call | tf_op jit(solution)/shard_map/rows/pallas_call | solution.py:103
  93.5 0.0 copy-start.4
  93.5 1.4 copy-done.4
  94.9 0.0 copy-start.6
  94.9 1.4 copy-done.6
  96.3 31.1 %all-gather.5.cloned.1.call-done = bf16[28672,128]{1,0:T(8,128)(2,1)} async-done(((bf16[3584,128]{1,0:T(8,128)(2,1)}), bf16[28672,128]{1,0:T(8,128)(2,1)}) %all-gather.5.cloned.1.call-update) | async-done | bytes 7340048 | tf_op jit(solution)/shard_map/all_gather | solution.py:690
  127.4 0.0 copy-start.2
  127.4 2.0 copy-done.2
  129.4 0.0 copy-start.3
  129.4 2.0 copy-done.3
  131.4 0.0 copy-start.5
  131.4 1.6 copy-done.5
  133.0 34.5 %qkv.1 = (bf16[2,8,4,32,128]{4,3,2,1,0:T(8,128)(2,1)S(1)}, bf16[8,4,64,128]{3,2,1,0:T(8,128)(2,1)S(1)}) custom-call(bf16[8,2,128,448]{3,2,1,0:T(8,128)(2,1)S(1)} %copy-done.5, bf16[8,3584,128]{2,1,0:T(8,128)(2,1)} %bitcast.22, bf16[3584,512]{1,0:T(8,128)(2,1)S(1)} %copy-done.2, bf16[3584,512]{1,0:T(8,128)(2,1)S(1)} %copy-done.3, ...), custom_call_target="tpu_custom_call" | custom-call | tf_op jit(solution)/shard_map/qkv/pallas_call | solution.py:270
  167.6 0.0 all-gather.7.cloned.1.call-update
  167.6 74.7 %attention.1.attended = bf16[32,32,256]{2,1,0:T(8,128)(2,1)S(1)} custom-call(s32[32]{0:T(128)S(1)} %select_reduce_fusion.2.slot_of, bf16[2,32,32,128]{3,2,1,0:T(8,128)(2,1)S(1)} %bitcast.20, bf16[32,64,128]{2,1,0:T(8,128)(2,1)S(1)} %bitcast.21), custom_call_target="tpu_custom_call" | custom-call | tf_op jit(solution)/shard_map/attention/pallas_call | solution.py:432
  242.3 31.3 %all-gather.7.cloned.1.call-done = bf16[32,256,448]{1,2,0:T(8,128)(2,1)} async-done(((bf16[4,256,448]{1,2,0:T(8,128)(2,1)}), bf16[32,256,448]{1,2,0:T(8,128)(2,1)}) %all-gather.7.cloned.1.call-update) | async-done | bytes 7340048 | tf_op jit(solution)/shard_map/all_gather | solution.py:724
  273.6 11.1 %copy.32 = bf16[32,256,448]{2,1,0:T(8,128)(2,1)} copy(bf16[32,256,448]{1,2,0:T(8,128)(2,1)} %all-gather.7.cloned.1.call-done) | data formatting | bytes 14680064 | tf_op jit(solution)/shard_map/all_gather | solution.py:724
  284.7 0.0 copy-start.1
  284.7 3.4 copy-done.1
  288.0 0.0 copy-start.7
  288.0 1.6 copy-done.7
  289.6 51.5 %out.1 = bf16[2,512,448]{2,1,0:T(8,128)(2,1)S(1)} custom-call(s32[32]{0:T(128)S(1)} %copy-done.8, bf16[32,32,256]{2,1,0:T(8,128)(2,1)S(1)} %attention.1.attended, bf16[8,4,256,448]{3,2,1,0:T(8,128)(2,1)S(1)} %bitcast.17, bf16[2,8,2,64,448]{4,3,2,1,0:T(8,128)(2,1)S(1)} %copy-done.7), custom_call_target="tpu_custom_call" | custom-call | tf_op jit(solution)/shard_map/out/pallas_call | solution.py:600
  341.1 1.3 copy.33
  (8 shorter events, 0.1 us)
Async XLA Ops:
  6.5 1.5 copy-start
  6.5 2.5 copy-start.8
  6.5 2.6 copy-start.10
  6.5 3.1 copy-start.11
  6.5 120.8 %all-gather.5.cloned.1.call-start = ((), (), s32[]{:S(2)}) async-start(), calls=%async_computation.1 | async-start | bytes 8257536 | tf_op jit(solution)/shard_map/all_gather | solution.py:690
  22.1 28.1 %all-to-all-start = ((bf16[128,8,512]{2,1,0:T(8,128)(2,1)}), bf16[128,8,512]{2,1,0:T(8,128)(2,1)}, u32[]{:S(2)}, u32[]{:S(2)}) async-start(bf16[128,8,512]{2,1,0:T(8,128)(2,1)} %bitcast.1), calls=%async_computation | async-start | bytes 2097152 | tf_op jit(solution)/shard_map/all_to_all | solution.py:656
  33.1 240.5 %all-gather.7.cloned.1.call-start = ((), (), s32[]{:S(2)}) async-start(), calls=%async_computation.2 | async-start | bytes 8257536 | tf_op jit(solution)/shard_map/all_gather | solution.py:724
  55.9 1.5 copy-start.9
  93.5 1.4 copy-start.4
  94.9 1.4 copy-start.6
  127.4 2.0 copy-start.2
  129.4 2.0 copy-start.3
  131.4 1.6 copy-start.5
  284.7 3.4 copy-start.1
  288.0 1.6 copy-start.7
Sparse Core Ops, SparseCore 0:
  9.7 117.6 all-gather.4
  167.7 105.8 all-gather.6

commit v3 on v2

--- a/solution.py
+++ b/solution.py
@@ -30,6 +30,18 @@
         src_ref=src, dst_ref=dst, send_sem=send_sem, recv_sem=recv_sem,
         device_id=(ctx, tp), device_id_type=MESH,
     )
+
+
+def add4(a, b):
+    return lax.rem(a + b + 4, 4)
+
+
+def pair_of(e, t):
+    return lax.rem(e // 4 + t // 4, 2) * 4 + add4(lax.rem(e, 4), lax.rem(t, 4))
+
+
+def class_of(e, pair):
+    return lax.rem(e // 4 + pair // 4, 2) * 4 + add4(lax.rem(pair, 4), -lax.rem(e, 4))
 
 
 def rows_kernel(placed, gain, rows, normed, gains, send, recv, fsend, frecv, gsend, grecv):
@@ -153,7 +165,8 @@
     for j in range(N_TP):
         load(j).start()
 
-    own = t == pair
+    goal = pair_of(pair, t)
+    own = t == 0
     barrier = pltpu.get_barrier_semaphore()
     for k in range(2):
         for d in range(PAIRS):
@@ -162,10 +175,10 @@
 
                 @pl.when(jnp.logical_not(jnp.logical_and(own, core == k)))
                 def _():
-                    signal(barrier, 2 * e + k, pair)
+                    signal(barrier, 2 * e + k, 0)
 
             else:
-                signal(barrier, 2 * e + k, pair)
+                signal(barrier, 2 * e + k, class_of(e, pair))
     pl.semaphore_wait(barrier, 2 * N_TP - jnp.where(own, 1, 0))
 
     part = normed.shape[-1]
@@ -185,13 +198,13 @@
 
     def kv_push(d):
         j = lax.rem(t + d, N_TP)
-        return push(kv.at[j // 2], kv_out.at[pair], ksend.at[d], krecv.at[pair], 2 * t + core, j)
+        return push(kv.at[j // 2], kv_out.at[pair], ksend.at[d], krecv.at[pair], 2 * goal + core, j)
 
     def q_push(d, k):
         j = lax.rem(t + d, N_TP)
         return push(
             query.at[j, :, pl.ds(k * HALF, HALF), :], query_out.at[core, pair],
-            qsend.at[d, k], qrecv.at[core, pair], 2 * t + k, j,
+            qsend.at[d, k], qrecv.at[core, pair], 2 * goal + k, j,
         )
 
     pltpu.make_async_copy(key_weight, kv_slot, wsem.at[N_TP]).wait()
@@ -293,7 +306,8 @@
 
 
 def attention_kernel(
-    slot_of, query, kv_own, out, kv, q, summed, largest, total, send, recv, pass_send,
+    slot_of, query, kv_own, out_weight, out, gathered,
+    kv, q, summed, largest, total, limit, send, recv, pass_send, wsend, wrecv, own_sem,
 ):
     scale = LOG2E / math.sqrt(HS)
     c = lax.axis_index("ctx")
@@ -310,13 +324,62 @@
     z_up, z_down, z_far = base + up, base + down, base + far
     x_own, x_up, x_down, x_far = other + z, other + up, other + down, other + far
 
+    y = lax.rem(t, 4)
+    side = t - y
+    across = 4 - side
+    t_up, t_down, t_far = (side + add4(y, n) for n in (1, 3, 2))
+    a_own, a_up, a_down, a_far = (across + add4(y, n) for n in (0, 1, 3, 2))
+    x_next = 2 * x_own + core
+
     barrier = pltpu.get_barrier_semaphore()
     signal(barrier, sibling, t)
     for e in (z_up, z_down, z_far, x_own):
         signal(barrier, 2 * e + core, t)
+    signal(barrier, x_next, a_own)
+    for j in (t_up, t_down, t_far):
+        signal(barrier, c, j)
     for j in range(32):
         kv[pair, core, j * OFF : (j + 1) * OFF] = kv_own[slot_of[j]]
-    pl.semaphore_wait(barrier, 5)
+    pl.semaphore_wait(barrier, 9)
+
+    cols = gathered.shape[-1]
+    quarter_rows = gathered.shape[1] // 4
+    own_weight = out_weight.at[:, pl.ds(pl.multiple_of(cols * core, HS), cols)]
+
+    def quarter(ref, n):
+        return ref.at[pl.ds(quarter_rows * n, quarter_rows)]
+
+    def wmove(m):
+        whole = lambda g: (gathered.at[g], gathered.at[g])
+        part = lambda g: (quarter(gathered.at[g], z), quarter(gathered.at[g], z))
+        src, dst, ctx, tp = (
+            (own_weight, gathered.at[t], x_next, a_own),
+            (own_weight, gathered.at[t], c, t_up),
+            (own_weight, gathered.at[t], c, t_down),
+            (quarter(own_weight, z), quarter(gathered.at[t], z), c, t_far),
+            (*whole(a_own), c, t_up),
+            (*whole(a_own), c, t_down),
+            (*part(a_own), c, t_far),
+            (*part(t_far), 2 * z_up + core, t),
+            (*part(t_far), 2 * z_down + core, t),
+            (*part(t_far), 2 * z_far + core, t),
+            (*part(a_far), 2 * z_up + core, t),
+            (*part(a_far), 2 * z_down + core, t),
+            (*part(a_far), 2 * z_far + core, t),
+        )[m]
+        return push(src, dst, wsend.at[m], wrecv.at[m], ctx, tp)
+
+    def warrive(m):
+        ref = (
+            gathered.at[a_own], gathered.at[t_down], gathered.at[t_up],
+            quarter(gathered.at[t_far], z),
+            gathered.at[a_down], gathered.at[a_up], quarter(gathered.at[a_far], z),
+            quarter(gathered.at[t_far], down), quarter(gathered.at[t_far], up),
+            quarter(gathered.at[t_far], far),
+            quarter(gathered.at[a_far], down), quarter(gathered.at[a_far], up),
+            quarter(gathered.at[a_far], far),
+        )[m]
+        push(ref, ref, wsend.at[m], wrecv.at[m], sibling, t).wait_recv()
 
     def transfer(e, to, index):
         block = kv.at[e, core]
@@ -337,24 +400,39 @@
     )
     for index in range(3):
         transfer(*moves[index], index).start()
+    for m in (0, 3, 1, 2):
+        wmove(m).start()
+    own_copy = pltpu.make_async_copy(own_weight, gathered.at[t], own_sem)
+    own_copy.start()
     for j in range(32):
         q[j * OFF : (j + 1) * OFF] = query[:, slot_of[j]].reshape(2 * HALF, HS)
 
     rows = 8 * HALF
     row = lax.broadcasted_iota(jnp.int32, (rows, 1), 0)
-    limit = row // OFF * CH + HALF * c + row % HALF
     col = lax.broadcasted_iota(jnp.int32, (1, 4 * OFF), 1)
 
+    def starts(index, i, e):
+        value = jnp.zeros(index.shape, jnp.int32)
+        for a in range(4):
+            start = a * CH + OFF * class_of(slot_of[4 * i + a] // 4, e)
+            value = jnp.where(index // OFF == a, start, value)
+        return value
+
+    for i in range(8):
+        limit[i * rows : (i + 1) * rows] = (
+            starts(row, i, pair) + HALF * core + row % HALF
+        )
+
     def update(e, first):
-        at = col // OFF * CH + OFF * e + col % OFF
         for i in range(8):
+            at = starts(col, i, e) + col % OFF
             here = slice(i * rows, (i + 1) * rows)
             width = 4 * OFF * (i + 1)
             s = lax.dot_general(
                 q[here], kv[e, 0, :width], (((1,), (1,)), ((), ())),
                 preferred_element_type=jnp.float32,
             )
-            edge = jnp.where(at <= limit, s[:, width - 4 * OFF :], -1e30)
+            edge = jnp.where(at <= limit[here], s[:, width - 4 * OFF :], -1e30)
             s = edge if i == 0 else jnp.concatenate([s[:, : width - 4 * OFF], edge], axis=1)
             top = jnp.max(s, axis=1, keepdims=True)
             if not first:
@@ -393,6 +471,9 @@
 
         @pl.when(n == 2)
         def _():
+            warrive(3)
+            for m in (7, 8, 9):
+                wmove(m).start()
             arrive(x_up, core)
             share(x_up).start()
 
@@ -404,6 +485,12 @@
             transfer(*moves[6], 6).start()
             share(z_far).start()
 
+        @pl.when(n == 4)
+        def _():
+            warrive(0)
+            for m in (6, 4, 5):
+                wmove(m).start()
+
         @pl.when(n == 6)
         def _():
             arrive(x_far, core)
@@ -419,40 +506,57 @@
         attended = (summed[here] / total[here]).astype(jnp.bfloat16).reshape(4, 2, HALF, HS)
         for a in range(4):
             out[4 * i + a] = jnp.concatenate([attended[a, 0], attended[a, 1]], axis=1)
+    warrive(6)
+    for m in (10, 11, 12):
+        wmove(m).start()
+    for m in (1, 2, 4, 5, 7, 8, 9, 10, 11, 12):
+        warrive(m)
+    own_copy.wait()
     for index in range(7):
         transfer(*moves[index], index).wait_send()
     for e in range(PAIRS):
         share(e).wait_send()
-
-
-def attention(slot_of, query, kv):
+    for m in range(13):
+        wmove(m).wait_send()
+
+
+def attention(slot_of, query, kv, out_weight):
+    anywhere = pl.BlockSpec(memory_space=pl.ANY)
+    depth, width = out_weight.shape
     vm = pl.BlockSpec(memory_space=pltpu.VMEM)
     sm = pl.BlockSpec(memory_space=pltpu.SMEM)
     keys = 32 * OFF
     return pl.pallas_call(
         attention_kernel,
-        out_shape=jax.ShapeDtypeStruct((32, HALF, 2 * HS), jnp.bfloat16),
-        in_specs=[sm, vm, vm],
-        out_specs=vm,
+        out_shape=(
+            jax.ShapeDtypeStruct((32, HALF, 2 * HS), jnp.bfloat16),
+            jax.ShapeDtypeStruct((N_TP, depth, width // 2), jnp.bfloat16),
+        ),
+        in_specs=[sm, vm, vm, anywhere],
+        out_specs=(vm, anywhere),
         scratch_shapes=[
             pltpu.VMEM((PAIRS, 2, keys, HS), jnp.bfloat16),
             pltpu.VMEM((keys, HS), jnp.bfloat16),
             pltpu.VMEM((keys, HS), jnp.float32),
             pltpu.VMEM((keys, 1), jnp.float32),
             pltpu.VMEM((keys, 1), jnp.float32),
+            pltpu.VMEM((keys, 1), jnp.int32),
             pltpu.SemaphoreType.DMA((7,)),
             pltpu.SemaphoreType.DMA((PAIRS, 2)),
             pltpu.SemaphoreType.DMA((PAIRS,)),
+            pltpu.SemaphoreType.DMA((13,)),
+            pltpu.SemaphoreType.DMA((13,)),
+            pltpu.SemaphoreType.DMA,
         ],
         compiler_params=pltpu.CompilerParams(
             collective_id=4, has_side_effects=True, vmem_limit_bytes=48 * 2**20
         ),
         name="attention",
-    )(slot_of, query, kv)
+    )(slot_of, query, kv, out_weight)
 
 
 def out_kernel(
-    span_order, attended, out_weight, rows, out, sorted_heads, heads, weight, result,
+    span_order, attended, out_weight, rows, out, sorted_heads, heads, weight, product, result,
     wsem, hsend, hrecv, fsend, frecv, rsend, rrecv,
 ):
     c = lax.axis_index("ctx")
@@ -461,7 +565,7 @@
     core = c % 2
     sibling = c + 1 - 2 * core
     side = t // 4
-    parts = out_weight.shape[1]
+    parts = N_TP // 2
 
     def load(g):
         return pltpu.make_async_copy(out_weight.at[g], weight.at[g], wsem.at[g])
@@ -469,8 +573,9 @@
     for g in range(N_TP):
         load(g).start()
 
-    own = t == pair
+    own = t == 0
     home = side == core
+    origin = pair_of(pair, t)
     barrier = pltpu.get_barrier_semaphore()
     signal(barrier, sibling, t)
     for d in range(N_TP):
@@ -479,14 +584,14 @@
 
             @pl.when(jnp.logical_not(own))
             def _():
-                signal(barrier, 2 * t + core, j)
+                signal(barrier, 2 * origin + core, j)
 
             @pl.when(jnp.logical_not(home))
             def _():
                 signal(barrier, 2 * pair + side, j)
 
         else:
-            signal(barrier, 2 * t + core, j)
+            signal(barrier, 2 * origin + core, j)
             signal(barrier, 2 * pair + side, j)
     for j in range(32):
         sorted_heads[j] = attended[span_order[j]]
@@ -501,7 +606,7 @@
         e = lax.rem(pair + d, PAIRS)
         return push(
             sorted_heads.at[pl.ds(4 * e, 4)], heads.at[t, :, mine, :], hsend.at[d], hrecv.at[t],
-            2 * e + core, pair,
+            2 * e + core, class_of(e, pair),
         )
 
     @pl.when(own)
@@ -547,13 +652,29 @@
     def is_home(j, a):
         return jnp.logical_and(home, jnp.logical_and(a == core, parts * core + j == t))
 
-    for j in range(parts):
-        total = jnp.zeros((4 * OFF, part), jnp.float32)
+    block = 2 * HS
+
+    def project(n):
+        total = jnp.zeros((4 * OFF, block), jnp.float32)
         for g in range(N_TP):
             x = heads[g].reshape(4 * OFF, 2 * HS)
             total = total + jnp.dot(
-                x, weight[g, j], preferred_element_type=jnp.float32
+                x, weight[g, :, n * block : (n + 1) * block], preferred_element_type=jnp.float32
             ).astype(jnp.bfloat16).astype(jnp.float32)
+        product[:, n * block : (n + 1) * block] = total
+
+    ready = 0
+    for j in range(parts):
+        while ready * block < (j + 1) * part:
+            project(ready)
+            ready += 1
+        start = j * part // HS * HS
+        shift = j * part - start
+        window = -(-(part + shift) // HS) * HS
+        total = product[:, start : start + window]
+        if shift:
+            total = pltpu.roll(total, window - shift, 1)
+        total = total[:, :part]
         for a in range(2):
             placed = rows[a, parts * core + j].reshape(2 * OFF, part).astype(jnp.float32)
             result[j, a] = (placed + total[a * 2 * OFF : (a + 1) * 2 * OFF]).astype(
@@ -594,7 +715,7 @@
 
 def out_exchange(span_order, attended, out_weight, rows):
     part = rows.shape[-1]
-    parts = out_weight.shape[1]
+    parts = N_TP // 2
     vm = pl.BlockSpec(memory_space=pltpu.VMEM)
     anywhere = pl.BlockSpec(memory_space=pl.ANY)
     return pl.pallas_call(
@@ -605,7 +726,8 @@
         scratch_shapes=[
             pltpu.VMEM((32, HALF, 2 * HS), jnp.bfloat16),
             pltpu.VMEM((N_TP, 4, OFF, 2 * HS), jnp.bfloat16),
-            pltpu.VMEM((N_TP, parts, 2 * HS, part), jnp.bfloat16),
+            pltpu.VMEM(out_weight.shape, jnp.bfloat16),
+            pltpu.VMEM((4 * OFF, parts * part), jnp.float32),
             pltpu.VMEM((parts, 2, 2, OFF, part), jnp.bfloat16),
             pltpu.SemaphoreType.DMA((N_TP,)),
             pltpu.SemaphoreType.DMA((N_TP,)),
@@ -688,13 +810,6 @@
     pair = c // 2
     core = c % 2
     q_half = lax.all_gather(lax.dynamic_slice_in_dim(query_weight, core * HS, HS, 1), "tp")
-    out_cols = out_weight.shape[1] // 2
-    out_half = jnp.transpose(
-        lax.dynamic_slice_in_dim(out_weight, core * out_cols, out_cols, 1).reshape(
-            2 * HS, N_TP // 2, part
-        ),
-        (1, 0, 2),
-    )
     slots = span_order.shape[0]
     index = jnp.arange(slots, dtype=jnp.int32)
     slot_of = jnp.sum(
@@ -720,12 +835,10 @@
     query, kv = qkv_exchange(
         normed, q_half, key_weight, value_weight, (cosine, sine, kv_cosine, kv_sine)
     )
-    kv, out_half = lax.optimization_barrier((kv, out_half))
-    out_half = lax.all_gather(out_half, "tp")
-    attended = attention(
-        slot_of, query.reshape(2, 32, HALF, HS), kv.reshape(32, OFF, HS)
-    )
-    mixed = out_exchange(span_order, attended, out_half, rows)
+    attended, gathered = attention(
+        slot_of, query.reshape(2, 32, HALF, HS), kv.reshape(32, OFF, HS), out_weight
+    )
+    mixed = out_exchange(span_order, attended, gathered, rows)
     return mixed.reshape(tok_rows, part)
 
 

time: 356 us -> 300 us (0.84); the launches traced: 349 us -> 299 us
  waiting for transfers between devices: 75.8 us -> 46.2 us
  local copies, waits for them, and re-layouts: 36.8 us -> 22.9 us
  Pallas kernels: 197 us -> 191 us
    all_gather x1 -> x0, waiting for transfers between devices: 31.3 us -> none  [per_device(): out_half = lax.all_gather(out_half, 'tp')]
    pallas_call x1, Pallas kernels: 74.7 us -> 86.2 us  [attention(): pl.pallas_call(attention_kernel, out_shape=(jax.ShapeDtypeStruct((32, HAL...]
    all_gather x1 -> x0, local copies, waits for them, and re-layouts: 11.1 us -> none  [per_device(): out_half = lax.all_gather(out_half, 'tp')]
    pallas_call x1, Pallas kernels: 51.5 us -> 43 us  [out_exchange(): pl.pallas_call(out_kernel, out_shape=jax.ShapeDtypeStruct((2, CH, part),...]
    pallas_call x1, Pallas kernels: 34.5 us -> 26.3 us  [qkv_exchange(): pl.pallas_call(qkv_kernel, out_shape=(jax.ShapeDtypeStruct((2, N_TP, 4, H...]
    unnamed x27 -> x28, local copies, waits for them, and re-layouts: 16.5 us -> 15.1 us
  transfers between devices with their start and end apart: 3 -> 2, of which waited for: 3 -> 2; matrix products, arithmetic and copies ran while one was open for 7% -> 7% of each run, Pallas kernels for 32% -> 12%
where the time goes in v3:
time: 300 us; the launch traced here: 299 us
  Pallas kernels  191 us (64%)
  waiting for transfers between devices  46.2 us (15%)
  local copies, waits for them, and re-layouts  22.9 us (8%)
  between operations  13.7 us (5%)
  matrix products  11.5 us (4%)
  starting transfers between devices  10.6 us (4%)
  other arithmetic  3.25 us (1%)
    pallas_call x1, Pallas kernels, attention(): pl.pallas_call(attention_kernel, out_shape=(jax.ShapeDtypeStruct((32, HAL...  86.2 us
    pallas_call x1, Pallas kernels, out_exchange(): pl.pallas_call(out_kernel, out_shape=jax.ShapeDtypeStruct((2, CH, part),...  43 us
    pallas_call x1, Pallas kernels, rows_exchange(): pl.pallas_call(rows_kernel, out_shape=(jax.ShapeDtypeStruct((2, N_TP, 2,...  36.1 us
    all_gather x1, waiting for transfers between devices, per_device(): lax.all_gather(lax.dynamic_slice_in_dim(query_weight, core * HS, HS, 1),...  29.7 us
    pallas_call x1, Pallas kernels, qkv_exchange(): pl.pallas_call(qkv_kernel, out_shape=(jax.ShapeDtypeStruct((2, N_TP, 4, H...  26.3 us
    all_to_all x1, waiting for transfers between devices, place_frames(): lax.all_to_all(outgoing.reshape(N_CTX * N_TP, CAP, part + 64), ('ctx', 't...  16.4 us
    unnamed x28, local copies, waits for them, and re-layouts  15.1 us
    all_to_all x1, starting transfers between devices, place_frames(): lax.all_to_all(outgoing.reshape(N_CTX * N_TP, CAP, part + 64), ('ctx', 't...  10.6 us
  transfers between devices with their start and end apart: 2, of which 2 were waited for; matrix products, arithmetic and copies ran while one was open for 7% of the time, Pallas kernels for 12%

profile of v3, /device:TPU:29, one launch (start us, length us, event | category | flops | bytes accessed | tf_op | source)
XLA Modules:
  0.0 299.5 jit_solution(16496581804727358755)
XLA Ops:
  6.5 0.0 copy-start
  6.5 0.0 copy-start.9
  6.5 0.0 copy-start.11
  6.5 0.0 copy-start.12
  6.5 0.0 all-gather.3.cloned.1.call-start
  6.6 1.4 copy-done
  8.0 1.0 constant_dynamic-slice_fusion
  9.0 0.0 all-gather.3.cloned.1.call-update
  9.1 0.0 copy-done.9
  9.1 0.1 select_reduce_fusion.2.slot_of
  9.2 0.0 copy-done.11
  9.2 0.1 select_reduce_fusion.1
  9.3 0.2 convert_reduce_fusion
  9.5 0.1 select_reduce_fusion
  9.6 0.1 sub.29
  9.7 0.0 copy-done.12
  9.7 8.1 %fusion.5 = bf16[128,3584]{1,0:T(8,128)(2,1)} fusion(bf16[1152,3584]{1,0:T(8,128)(2,1)} %param.14, bf16[64,1152]{1,0:T(8,128)(2,1)S(1)} %copy-done.12, s32[64]{0:T(128)S(1)} %multiply_add_fusion.1), kind=kOutput, calls=%fused_computation.8 | convolution fusion | flops 1105813504 | bytes 9322752 | tf_op jit(solution)/shard_map/dot_general | solution.py:767
  17.8 2.3 reshape.203
  20.2 0.4 copy.26
  20.6 0.1 broadcast_in_dim.96
  20.7 0.1 broadcast_in_dim.97
  20.8 1.3 pad_maximum_fusion
  22.1 10.6 %all-to-all-start = ((bf16[128,8,512]{2,1,0:T(8,128)(2,1)}), bf16[128,8,512]{2,1,0:T(8,128)(2,1)S(1)}, u32[]{:S(2)}, u32[]{:S(2)}) async-start(bf16[128,8,512]{2,1,0:T(8,128)(2,1)} %bitcast.1), calls=%async_computation | async-start | bytes 2097152 | tf_op jit(solution)/shard_map/all_to_all | solution.py:778
  32.7 0.1 multiply_add_fusion
  32.8 0.1 add_convert_fusion.1
  32.8 0.1 convert_element_type.69
  32.9 0.5 fusion.17
  33.5 0.1 broadcast_select_fusion
  33.6 16.4 %all-to-all-done = bf16[128,8,512]{2,1,0:T(8,128)(2,1)S(1)} async-done(((bf16[128,8,512]{2,1,0:T(8,128)(2,1)}), bf16[128,8,512]{2,1,0:T(8,128)(2,1)S(1)}, u32[]{:S(2)}, u32[]{:S(2)}) %all-to-all-start) | async-done | bytes 1048608 | tf_op jit(solution)/shard_map/all_to_all | solution.py:778
  50.0 1.0 fusion.30
  51.0 1.1 copy.23
  52.1 1.1 copy.24
  53.2 0.6 fusion.1
  53.8 3.3 %fusion.14 = bf16[1024,448]{0,1:T(8,128)(2,1)} fusion(bf16[1024,448]{0,1:T(8,128)(2,1)} %param.10, s32[1024]{0:T(1024)S(1)} %bitcast.22, bf16[1024,512]{1,0:T(8,128)(2,1)S(1)} %bitcast.20, pred[1024]{0:T(1024)(128)(4,1)S(1)} %fusion.1), kind=kOutput, calls=%fused_computation.25 | convolution fusion | flops 941490176 | bytes 2888704 | tf_op jit(solution)/shard_map/dot_general | solution.py:789
  57.1 0.0 copy-start.10
  57.1 1.5 copy.21
  58.6 0.0 copy-done.10
  58.6 36.1 %rows.1 = (bf16[2,8,2,64,448]{4,3,2,1,0:T(8,128)(2,1)S(1)}, bf16[8,2,128,448]{3,2,1,0:T(8,128)(2,1)S(1)}) custom-call(bf16[2,8,64,448]{3,2,1,0:T(8,128)(2,1)S(1)} %bitcast.13, bf16[16,448]{1,0:T(8,128)(2,1)S(1)} %broadcast_in_dim.99.gain), custom_call_target="tpu_custom_call" | custom-call | tf_op jit(solution)/shard_map/rows/pallas_call | solution.py:115
  94.7 0.0 copy-start.4
  94.7 1.3 copy-done.4
  96.0 0.0 copy-start.6
  96.0 1.4 copy-done.6
  97.4 29.7 %all-gather.3.cloned.1.call-done = bf16[28672,128]{1,0:T(8,128)(2,1)} async-done(((bf16[3584,128]{1,0:T(8,128)(2,1)}), bf16[28672,128]{1,0:T(8,128)(2,1)}) %all-gather.3.cloned.1.call-update) | async-done | bytes 7340048 | tf_op jit(solution)/shard_map/all_gather | solution.py:812
  127.1 0.0 copy-start.2
  127.1 2.0 copy-done.2
  129.2 0.0 copy-start.3
  129.2 2.0 copy-done.3
  131.2 0.0 copy-start.5
  131.2 1.6 copy-done.5
  132.8 0.0 copy-start.8
  132.8 26.3 %qkv.1 = (bf16[2,8,4,32,128]{4,3,2,1,0:T(8,128)(2,1)S(1)}, bf16[8,4,64,128]{3,2,1,0:T(8,128)(2,1)S(1)}) custom-call(bf16[8,2,128,448]{3,2,1,0:T(8,128)(2,1)S(1)} %copy-done.5, bf16[8,3584,128]{2,1,0:T(8,128)(2,1)} %bitcast.17, bf16[3584,512]{1,0:T(8,128)(2,1)S(1)} %copy-done.2, bf16[3584,512]{1,0:T(8,128)(2,1)S(1)} %copy-done.3, ...), custom_call_target="tpu_custom_call" | custom-call | tf_op jit(solution)/shard_map/qkv/pallas_call | solution.py:283
  159.1 0.0 copy-start.7
  159.1 0.0 copy-done.8
  159.1 86.2 %attention.1 = (bf16[32,32,256]{2,1,0:T(8,128)(2,1)S(1)}, bf16[8,256,1792]{2,1,0:T(8,128)(2,1)}) custom-call(s32[32]{0:T(128)S(1)} %select_reduce_fusion.2.slot_of, bf16[2,32,32,128]{3,2,1,0:T(8,128)(2,1)S(1)} %bitcast.15, bf16[32,64,128]{2,1,0:T(8,128)(2,1)S(1)} %bitcast.16, bf16[256,3584]{1,0:T(8,128)(2,1)S(1)} %copy-done.8), custom_call_target="tpu_custom_call" | custom-call | tf_op jit(solution)/shard_map/attention/pallas_call | solution.py:529
  245.3 0.0 copy-done.7
  245.3 0.0 copy-start.1
  245.3 3.1 %copy-done.1 = bf16[8,256,1792]{2,1,0:T(8,128)(2,1)S(1)} copy-done((bf16[8,256,1792]{2,1,0:T(8,128)(2,1)S(1)}, bf16[8,256,1792]{2,1,0:T(8,128)(2,1)}, u32[]{:S(2)}) %copy-start.1) | copy-done | bytes 7340056
  248.4 43.0 %out.1 = bf16[2,512,448]{2,1,0:T(8,128)(2,1)S(1)} custom-call(s32[32]{0:T(128)S(1)} %copy-done.9, bf16[32,32,256]{2,1,0:T(8,128)(2,1)S(1)} %get-tuple-element.14.attended, bf16[8,256,1792]{2,1,0:T(8,128)(2,1)S(1)} %copy-done.1, bf16[2,8,2,64,448]{4,3,2,1,0:T(8,128)(2,1)S(1)} %copy-done.7), custom_call_target="tpu_custom_call" | custom-call | tf_op jit(solution)/shard_map/out/pallas_call | solution.py:721
  291.4 1.3 copy.22
  (8 shorter events, 0.1 us)
Async XLA Ops:
  6.5 1.5 copy-start
  6.5 2.5 copy-start.9
  6.5 2.6 copy-start.11
  6.5 3.2 %copy-start.12 = (bf16[64,1152]{1,0:T(8,128)(2,1)S(1)}, bf16[64,1152]{1,0:T(8,128)(2,1)}, u32[]{:S(2)}) copy-start(bf16[64,1152]{1,0:T(8,128)(2,1)} %param.11) | copy-start | bytes 442372
  6.5 120.6 %all-gather.3.cloned.1.call-start = ((), (), s32[]{:S(2)}) async-start(), calls=%async_computation.1 | async-start | bytes 8257536 | tf_op jit(solution)/shard_map/all_gather | solution.py:812
  22.1 28.0 %all-to-all-start = ((bf16[128,8,512]{2,1,0:T(8,128)(2,1)}), bf16[128,8,512]{2,1,0:T(8,128)(2,1)S(1)}, u32[]{:S(2)}, u32[]{:S(2)}) async-start(bf16[128,8,512]{2,1,0:T(8,128)(2,1)} %bitcast.1), calls=%async_computation | async-start | bytes 2097152 | tf_op jit(solution)/shard_map/all_to_all | solution.py:778
  57.1 1.5 copy-start.10
  94.7 1.3 copy-start.4
  96.0 1.4 copy-start.6
  127.1 2.0 copy-start.2
  129.2 2.0 copy-start.3
  131.2 1.6 copy-start.5
  132.8 26.3 %copy-start.8 = (bf16[256,3584]{1,0:T(8,128)(2,1)S(1)}, bf16[256,3584]{1,0:T(8,128)(2,1)}, u32[]{:S(2)}) copy-start(bf16[256,3584]{1,0:T(8,128)(2,1)} %out_weight.1) | copy-start | bytes 5505028
  159.1 86.2 %copy-start.7 = (bf16[2,8,2,64,448]{4,3,2,1,0:T(8,128)(2,1)S(1)}, bf16[2,8,2,64,448]{4,3,2,1,0:T(8,128)(2,1)}, u32[]{:S(2)}) copy-start(bf16[2,8,2,64,448]{4,3,2,1,0:T(8,128)(2,1)} %copy-done.6) | copy-start | bytes 5505028
  245.3 3.1 %copy-start.1 = (bf16[8,256,1792]{2,1,0:T(8,128)(2,1)S(1)}, bf16[8,256,1792]{2,1,0:T(8,128)(2,1)}, u32[]{:S(2)}) copy-start(bf16[8,256,1792]{2,1,0:T(8,128)(2,1)} %get-tuple-element.15.out_weight) | copy-start | bytes 22020100
Sparse Core Ops, SparseCore 0:
  9.7 117.4 all-gather.2

commit v4 on v3

--- a/solution.py
+++ b/solution.py
@@ -44,18 +44,214 @@
     return lax.rem(e // 4 + pair // 4, 2) * 4 + add4(lax.rem(pair, 4), -lax.rem(e, 4))
 
 
-def rows_kernel(placed, gain, rows, normed, gains, send, recv, fsend, frecv, gsend, grecv):
+def intake_kernel(
+    text, gain, features, pos_row, pos_col, order_row, order_col, cosine, sine,
+    projector, query_weight, key_weight, value_weight,
+    rows, query_out, kv_out,
+    pweight, projected, outgoing, incoming, placed, gains, normed, weight, kv_weight, query, kv,
+    psem, own_sem, kv_sem, fr_send, fr_recv, wsend, wrecv,
+    send, recv, fsend, frecv, gsend, grecv, qsend, qrecv, ksend, krecv,
+):
     c = lax.axis_index("ctx")
     t = lax.axis_index("tp")
+    pair = c // 2
     core = c % 2
     sibling = c + 1 - 2 * core
+    devices = N_CTX * N_TP
+    me = c * N_TP + t
+    part = text.shape[-1]
+    width = N_TP * part
+    base = pair // 4 * 4
+    z = pair % 4
+    z_up, z_down, z_far = (base + add4(z, n) for n in (1, 3, 2))
+    y = lax.rem(t, 4)
+    side = t - y
+    across = 4 - side
+    t_up, t_down, t_far = (side + add4(y, n) for n in (1, 3, 2))
+    a_own, a_up, a_down, a_far = (across + add4(y, n) for n in (0, 1, 3, 2))
+    x_next = 2 * (4 - base + z) + core
+
+    own_copy = pltpu.make_async_copy(
+        query_weight.at[:, pl.ds(pl.multiple_of(HS * core, HS), HS)], weight.at[t], own_sem
+    )
+    own_copy.start()
+    block = 4 * HS
+    blocks = width // block
+
+    def load(n):
+        cols = pl.ds(n * block, block)
+        return pltpu.make_async_copy(projector.at[:, cols], pweight.at[:, cols], psem.at[n])
+
+    for n in range(blocks):
+        load(n).start()
+
+    @pl.when(core == 0)
+    def _():
+        pltpu.make_async_copy(key_weight, kv_weight, kv_sem).start()
+
+    @pl.when(core == 1)
+    def _():
+        pltpu.make_async_copy(value_weight, kv_weight, kv_sem).start()
+
     barrier = pltpu.get_barrier_semaphore()
-    signal(barrier, sibling, t)
-    for d in range(1, N_TP):
-        signal(barrier, c, lax.rem(t + d, N_TP))
-    pl.semaphore_wait(barrier, N_TP)
-
-    def block(d):
+
+    def greet(d, unused):
+        other = lax.rem(me + d, devices)
+        signal(barrier, other // N_TP, lax.rem(other, N_TP))
+        return unused
+
+    lax.fori_loop(1, devices, greet, 0)
+
+    f32 = jnp.float32
+    spans = order_row.shape[1]
+    tokens = pos_row.shape[1]
+    entries = N_CTX * CAP
+    slot_row = jnp.sum(
+        jnp.where(
+            order_col[...] == pos_row[...] // CH,
+            lax.broadcasted_iota(jnp.int32, (spans, tokens), 0).astype(f32), 0.0,
+        ),
+        axis=0, keepdims=True,
+    ).astype(jnp.int32)
+    slot_col = jnp.sum(
+        jnp.where(
+            order_row[...] == pos_col[...] // CH,
+            lax.broadcasted_iota(jnp.int32, (tokens, spans), 1).astype(f32), 0.0,
+        ),
+        axis=1, keepdims=True,
+    ).astype(jnp.int32)
+    first = lax.broadcasted_iota(jnp.int32, (tokens, tokens), 0)
+    second = lax.broadcasted_iota(jnp.int32, (tokens, tokens), 1)
+    earlier = jnp.logical_and(slot_col // 2 == slot_row // 2, first < second)
+    place = jnp.sum(jnp.where(earlier, 1.0, 0.0), axis=0, keepdims=True).astype(jnp.int32)
+    entry = slot_row // 2 * CAP + place
+    chosen = lax.broadcasted_iota(jnp.int32, (entries, tokens), 0) == entry
+    ordered = jnp.dot(
+        jnp.where(chosen, 1.0, 0.0).astype(jnp.bfloat16), features[...],
+        preferred_element_type=f32,
+    ).astype(jnp.bfloat16)
+    token_row = (slot_row % 2 * CH + pos_row[...] % CH + 1).astype(f32)
+    row_at = jnp.sum(jnp.where(chosen, token_row, 0.0), axis=1, keepdims=True) - 1.0
+    row_at = row_at.astype(jnp.int32)
+    high = (row_at >> 5).astype(f32)
+    low = (row_at & 31).astype(f32)
+
+    pl.semaphore_wait(barrier, devices - 1)
+
+    depth = weight.shape[1]
+    direct = pl.ds(0, depth // 2)
+
+    def eighth(n):
+        return pl.ds(depth // 2 + depth // 8 * n, depth // 8)
+
+    def quarter(n):
+        return pl.ds(depth // 4 * n, depth // 4)
+
+    def wmove(m):
+        if m == 0:
+            ref, ctx, tp = weight.at[t], x_next, a_own
+        elif m < 11:
+            shard = t if m < 6 else a_own
+            cut, tp = (
+                (direct, t_up), (direct, t_down), (eighth(z), t_up), (eighth(z), t_down),
+                (quarter(z), t_far),
+            )[(m - 1) % 5]
+            ref, ctx = weight.at[shard, cut], c
+        else:
+            n = m - 11
+            shard = (t_up, t_down, t_far, a_up, a_down, a_far)[n // 3]
+            cut = quarter(z) if n // 3 % 3 == 2 else eighth(z)
+            ref, tp = weight.at[shard, cut], t
+            ctx = 2 * (z_up, z_down, z_far)[n % 3] + core
+        return push(ref, ref, wsend.at[m], wrecv.at[m], ctx, tp)
+
+    def warrive(m):
+        if m == 0:
+            ref = weight.at[a_own]
+        elif m < 11:
+            n = (m - 1) % 5
+            shard = ((t_down, t_up, t_down, t_up, t_far), (a_down, a_up, a_down, a_up, a_far))[
+                (m - 1) // 5
+            ][n]
+            cut = (direct, direct, eighth(z), eighth(z), quarter(z))[n]
+            ref = weight.at[shard, cut]
+        else:
+            n = m - 11
+            shard = (t_up, t_down, t_far, a_up, a_down, a_far)[n // 3]
+            origin = (add4(z, 3), add4(z, 1), add4(z, 2))[n % 3]
+            cut = quarter(origin) if n // 3 % 3 == 2 else eighth(origin)
+            ref = weight.at[shard, cut]
+        push(ref, ref, wsend.at[m], wrecv.at[m], sibling, t).wait_recv()
+
+    own_copy.wait()
+    for m in (0, 5, 3, 4, 1, 2):
+        wmove(m).start()
+
+    for n in range(blocks):
+        load(n).wait()
+        cols = slice(n * block, (n + 1) * block)
+        x = jnp.dot(ordered, pweight[:, cols], preferred_element_type=f32)
+        projected[:, cols] = 0.5 * x * (1.0 + lax.erf(x * math.sqrt(0.5)))
+    lane = lax.broadcasted_iota(jnp.int32, (entries, block), 1)
+    tail = jnp.where(lane < part + 32, high, jnp.where(lane < part + 48, low, 1.0))
+    for j in range(N_TP):
+        start = j * part // HS * HS
+        shift = j * part - start
+        x = projected[:, start : start + block]
+        if shift:
+            x = pltpu.roll(x, block - shift, 1)
+        x = jnp.where(lane < part, x, tail)
+        halves = [
+            x[:, n * 2 * HS : (n + 1) * 2 * HS].reshape(N_CTX, CAP, 2 * HS) for n in range(2)
+        ]
+        outgoing[:, j] = jnp.concatenate(halves, axis=1).astype(jnp.bfloat16)
+
+    here = pltpu.make_async_copy(outgoing.at[c, t], incoming.at[me], fr_recv)
+    here.start()
+
+    def deliver(d, unused):
+        other = lax.rem(me + d, devices)
+        oc = other // N_TP
+        ot = lax.rem(other, N_TP)
+        push(outgoing.at[oc, ot], incoming.at[me], fr_send, fr_recv, oc, ot).start()
+        return unused
+
+    lax.fori_loop(1, devices, deliver, 0)
+    for m in (3, 4, 5):
+        warrive(m)
+    for m in range(11, 20):
+        wmove(m).start()
+    warrive(0)
+    for m in (10, 8, 9, 6, 7):
+        wmove(m).start()
+    pltpu.make_async_copy(incoming, incoming, fr_recv).wait()
+
+    arrived = incoming[...].astype(f32)
+    slots = devices * CAP
+    left = arrived[:, :CAP].reshape(slots, 2 * HS)
+    right = arrived[:, CAP:].reshape(slots, 2 * HS)
+    edge = part - 2 * HS
+    at = right[:, edge : edge + 1] * 32.0 + right[:, edge + 32 : edge + 33]
+    at = jnp.transpose(jnp.broadcast_to(at, (slots, HS)))[0:1, :]
+    left = left.astype(jnp.bfloat16)
+    right = right.astype(jnp.bfloat16)
+    group = CH // 2
+    for n in range(4):
+        a, b = n // 2, n % 2 * 4
+        row = lax.broadcasted_iota(jnp.int32, (group, 1), 0) + n * group
+        hit = jnp.where(row.astype(f32) == at, 1.0, 0.0).astype(jnp.bfloat16)
+        new_left = jnp.dot(hit, left, preferred_element_type=f32)
+        new_right = jnp.dot(hit, right, preferred_element_type=f32)
+        framed = new_right[:, 2 * HS - 1 :] > 0.5
+        old = text[a, b : b + 4].reshape(group, part).astype(f32)
+        placed[a, b : b + 4, :, : 2 * HS] = (
+            jnp.where(framed, new_left, old[:, : 2 * HS]).astype(jnp.bfloat16)
+        ).reshape(4, OFF, 2 * HS)
+        placed[a, b : b + 4, :, 2 * HS :] = (
+            jnp.where(framed, new_right[:, :edge], old[:, 2 * HS :]).astype(jnp.bfloat16)
+        ).reshape(4, OFF, edge)
+
+    def row_block(d):
         j = lax.rem(t + d, N_TP)
         return push(placed.at[:, j], rows.at[core, t], send.at[d], recv.at[t], c, j)
 
@@ -66,7 +262,7 @@
     pltpu.make_async_copy(placed.at[:, t], rows.at[core, t], recv.at[t]).start()
     pltpu.make_async_copy(gain, gains.at[t], grecv.at[t]).start()
     for d in range(1, N_TP):
-        block(d).start()
+        row_block(d).start()
         gain_block(d).start()
 
     def forward(j):
@@ -78,141 +274,62 @@
         forward(j).start()
     for j in range(N_TP):
         push(gain, gains.at[j], gsend.at[0], grecv.at[j], sibling, t).wait_recv()
-
-    def receive(j):
+    for m in (8, 9, 10):
+        warrive(m)
+    for m in range(20, 29):
+        wmove(m).start()
+
+    def normalise(a):
+        total = jnp.zeros((2 * OFF, 1), f32)
+        for j in range(N_TP):
+            x = rows[a, j].reshape(2 * OFF, part).astype(f32)
+            total = total + jnp.sum(x * x, axis=1, keepdims=True)
+        inverse = lax.rsqrt(total / width + 1e-06)
+        for j in range(N_TP):
+            x = rows[a, j].reshape(2 * OFF, part).astype(f32)
+            g = gains[j, 0:1, :].astype(f32)
+            normed[j, a] = (x * inverse * g).astype(jnp.bfloat16)
+
+    normalise(core)
+    for j in range(N_TP):
         push(
             rows.at[1 - core, j], rows.at[1 - core, j], fsend.at[j], frecv.at[j], sibling, t
         ).wait_recv()
-
-    width = N_TP * placed.shape[-1]
-
-    def normalise(a):
-        total = jnp.zeros((2 * OFF, 1), jnp.float32)
+    normalise(1 - core)
+
+    def product(piece):
+        total = None
         for j in range(N_TP):
-            x = rows[a, j].reshape(2 * OFF, -1).astype(jnp.float32)
-            total = total + jnp.sum(x * x, axis=1, keepdims=True)
-        inverse = lax.rsqrt(total / width + 1e-06)
-        for j in range(N_TP):
-            x = rows[a, j].reshape(2 * OFF, -1).astype(jnp.float32)
-            g = gains[j, 0:1, :].astype(jnp.float32)
-            normed[j, a] = (x * inverse * g).astype(jnp.bfloat16)
-
-    normalise(core)
-    for j in range(N_TP):
-        receive(j)
-    normalise(1 - core)
-
-    for d in range(1, PAIRS):
-        block(d).wait_send()
-        gain_block(d).wait_send()
-    for j in range(N_TP):
-        forward(j).wait_send()
-
-
-def rows_exchange(placed, gain):
-    part = placed.shape[-1]
-    vm = pl.BlockSpec(memory_space=pltpu.VMEM)
-    return pl.pallas_call(
-        rows_kernel,
-        out_shape=(
-            jax.ShapeDtypeStruct((2, N_TP, 2, OFF, part), jnp.bfloat16),
-            jax.ShapeDtypeStruct((N_TP, 2, 2 * OFF, part), jnp.bfloat16),
-        ),
-        in_specs=[vm, vm],
-        out_specs=(vm, vm),
-        scratch_shapes=[
-            pltpu.VMEM((N_TP, 16, part), jnp.bfloat16),
-            pltpu.SemaphoreType.DMA((PAIRS,)),
-            pltpu.SemaphoreType.DMA((N_TP,)),
-            pltpu.SemaphoreType.DMA((N_TP,)),
-            pltpu.SemaphoreType.DMA((N_TP,)),
-            pltpu.SemaphoreType.DMA((PAIRS,)),
-            pltpu.SemaphoreType.DMA((N_TP,)),
-        ],
-        compiler_params=pltpu.CompilerParams(
-            collective_id=1, has_side_effects=True, vmem_limit_bytes=24 * 2**20
-        ),
-        name="rows",
-    )(placed, gain)
-
-
-def qkv_kernel(
-    normed, query_weight, key_weight, value_weight, cosine, sine, kv_cosine, kv_sine,
-    query_out, kv_out, weight, query, kv, wsem, qsend, qrecv, ksend, krecv,
-):
-    c = lax.axis_index("ctx")
-    t = lax.axis_index("tp")
-    pair = c // 2
-    core = c % 2
-    q_cols = N_TP * HS
-    kv_cols = KVH * HS
-
-    def load(j):
-        return pltpu.make_async_copy(
-            query_weight.at[j], weight.at[:, pl.ds(j * HS, HS)], wsem.at[j]
-        )
-
-    kv_slot = weight.at[:, pl.ds(q_cols, kv_cols)]
-
-    @pl.when(core == 0)
-    def _():
-        pltpu.make_async_copy(key_weight, kv_slot, wsem.at[N_TP]).start()
-
-    @pl.when(core == 1)
-    def _():
-        pltpu.make_async_copy(value_weight, kv_slot, wsem.at[N_TP]).start()
-
-    for j in range(N_TP):
-        load(j).start()
+            x = normed[j].reshape(4 * OFF, part)
+            term = jnp.dot(x, piece(slice(j * part, (j + 1) * part)), preferred_element_type=f32)
+            total = term if total is None else total + term
+        return total
+
+    def rotated(x, cos, sin):
+        return (x * cos + pltpu.roll(x, HS // 2, 1) * sin).astype(jnp.bfloat16).reshape(4, OFF, HS)
 
     goal = pair_of(pair, t)
     own = t == 0
-    barrier = pltpu.get_barrier_semaphore()
-    for k in range(2):
-        for d in range(PAIRS):
-            e = lax.rem(pair + d, PAIRS)
-            if d == 0:
-
-                @pl.when(jnp.logical_not(jnp.logical_and(own, core == k)))
-                def _():
-                    signal(barrier, 2 * e + k, 0)
-
-            else:
-                signal(barrier, 2 * e + k, class_of(e, pair))
-    pl.semaphore_wait(barrier, 2 * N_TP - jnp.where(own, 1, 0))
-
-    part = normed.shape[-1]
-
-    def product(start, cols):
-        total = jnp.zeros((4 * OFF, cols), jnp.float32)
-        for j in range(N_TP):
-            x = normed[j].reshape(4 * OFF, part)
-            total = total + jnp.dot(
-                x, weight[j * part : (j + 1) * part, start : start + cols],
-                preferred_element_type=jnp.float32,
-            )
-        return total
-
-    def rotated(x, cos, sin):
-        return (x * cos + pltpu.roll(x, HS // 2, 1) * sin).astype(jnp.bfloat16)
 
     def kv_push(d):
         j = lax.rem(t + d, N_TP)
         return push(kv.at[j // 2], kv_out.at[pair], ksend.at[d], krecv.at[pair], 2 * goal + core, j)
 
-    def q_push(d, k):
-        j = lax.rem(t + d, N_TP)
+    def q_push(j, k):
         return push(
             query.at[j, :, pl.ds(k * HALF, HALF), :], query_out.at[core, pair],
-            qsend.at[d, k], qrecv.at[core, pair], 2 * goal + k, j,
+            qsend.at[j, k], qrecv.at[core, pair], 2 * goal + k, j,
         )
 
-    pltpu.make_async_copy(key_weight, kv_slot, wsem.at[N_TP]).wait()
-    total = product(q_cols, kv_cols)
-    for h in range(KVH):
-        kv[h] = rotated(total[:, h * HS : (h + 1) * HS], kv_cosine[...], kv_sine[...]).reshape(
-            4, OFF, HS
-        )
+    pltpu.make_async_copy(key_weight, kv_weight, kv_sem).wait()
+    cos = cosine[...]
+    sin = sine[...]
+    kv_cos = jnp.where(core == 0, cos, 1.0)
+    kv_sin = jnp.where(core == 0, sin, 0.0)
+    for h in range(0, KVH, 2):
+        total = product(lambda cut: kv_weight[cut, h * HS : (h + 2) * HS])
+        for n in range(2):
+            kv[h + n] = rotated(total[:, n * HS : (n + 1) * HS], kv_cos, kv_sin)
 
     @pl.when(own)
     def _():
@@ -224,85 +341,138 @@
 
     for d in range(1, N_TP):
         kv_push(d).start()
-    for g in range(2):
-        for j in range(4 * g, 4 * g + 4):
-            load(j).wait()
-        total = product(g * 4 * HS, 4 * HS)
-        for h in range(4):
-            query[4 * g + h] = rotated(
-                total[:, h * HS : (h + 1) * HS], cosine[...], sine[...]
-            ).reshape(4, OFF, HS)
-    for d in range(N_TP):
-        for k in range(2):
-            if d == 0:
-                here = jnp.logical_and(own, core == k)
-
-                @pl.when(here)
-                def _():
-                    pltpu.make_async_copy(
-                        query.at[t, :, pl.ds(k * HALF, HALF), :], query_out.at[core, pair],
-                        qrecv.at[core, pair],
-                    ).start()
-
-                @pl.when(jnp.logical_not(here))
-                def _():
-                    q_push(0, k).start()
-
-            else:
-                q_push(d, k).start()
+
+    def is_here(j, k):
+        return jnp.logical_and(own, jnp.logical_and(j == t, core == k))
+
+    def heads(begin):
+        for h in range(0, 4, 2):
+            j0, j1 = begin + h, begin + h + 1
+            total = product(
+                lambda cut: jnp.concatenate([weight[j0, cut], weight[j1, cut]], axis=1)
+            )
+            for n, j in enumerate((j0, j1)):
+                query[j] = rotated(total[:, n * HS : (n + 1) * HS], cos, sin)
+                for k in range(2):
+
+                    @pl.when(is_here(j, k))
+                    def _():
+                        pltpu.make_async_copy(
+                            query.at[j, :, pl.ds(k * HALF, HALF), :], query_out.at[core, pair],
+                            qrecv.at[core, pair],
+                        ).start()
+
+                    @pl.when(jnp.logical_not(is_here(j, k)))
+                    def _():
+                        q_push(j, k).start()
+
+    for m in (1, 2, *range(11, 20)):
+        warrive(m)
+    heads(side)
+    for m in (6, 7, *range(20, 29)):
+        warrive(m)
+    heads(across)
+
     for e in range(PAIRS):
         push(kv.at[0], kv_out.at[e], ksend.at[0], krecv.at[e], c, t).wait_recv()
         for k in range(2):
             push(
                 query_out.at[k, e], query_out.at[k, e], qsend.at[0, 0], qrecv.at[k, e], c, t
             ).wait_recv()
-    for d in range(N_TP):
-        if d == 0:
-
-            @pl.when(jnp.logical_not(own))
+    pltpu.make_async_copy(
+        incoming.at[pl.ds(0, devices - 1)], incoming.at[pl.ds(0, devices - 1)], fr_send
+    ).wait()
+    for m in range(29):
+        wmove(m).wait_send()
+    for d in range(1, N_TP):
+        row_block(d).wait_send()
+        gain_block(d).wait_send()
+    for j in range(N_TP):
+        forward(j).wait_send()
+
+    @pl.when(jnp.logical_not(own))
+    def _():
+        kv_push(0).wait_send()
+
+    for d in range(1, N_TP):
+        kv_push(d).wait_send()
+    for j in range(N_TP):
+        for k in range(2):
+
+            @pl.when(jnp.logical_not(is_here(j, k)))
             def _():
-                kv_push(0).wait_send()
-
-        else:
-            kv_push(d).wait_send()
-        for k in range(2):
-            if d == 0:
-
-                @pl.when(jnp.logical_not(jnp.logical_and(own, core == k)))
-                def _():
-                    q_push(0, k).wait_send()
-
-            else:
-                q_push(d, k).wait_send()
-
-
-def qkv_exchange(normed, query_weight, key_weight, value_weight, tables):
-    width = key_weight.shape[0]
+                q_push(j, k).wait_send()
+
+
+def intake(
+    text_embed, norm_gain, frame_features, frame_positions, span_order, tables,
+    projector, query_weight, key_weight, value_weight,
+):
+    tok_rows, part = text_embed.shape
+    depth = query_weight.shape[0]
+    entries = N_CTX * CAP
+    devices = N_CTX * N_TP
     vm = pl.BlockSpec(memory_space=pltpu.VMEM)
     anywhere = pl.BlockSpec(memory_space=pl.ANY)
+    dma = pltpu.SemaphoreType.DMA
+    bf16 = jnp.bfloat16
     return pl.pallas_call(
-        qkv_kernel,
+        intake_kernel,
         out_shape=(
-            jax.ShapeDtypeStruct((2, N_TP, 4, HALF, HS), jnp.bfloat16),
-            jax.ShapeDtypeStruct((N_TP, 4, OFF, HS), jnp.bfloat16),
+            jax.ShapeDtypeStruct((2, N_TP, 2, OFF, part), bf16),
+            jax.ShapeDtypeStruct((2, N_TP, 4, HALF, HS), bf16),
+            jax.ShapeDtypeStruct((N_TP, 4, OFF, HS), bf16),
         ),
-        in_specs=[vm, anywhere, anywhere, anywhere, vm, vm, vm, vm],
-        out_specs=(vm, vm),
+        in_specs=[vm] * 9 + [anywhere] * 4,
+        out_specs=(vm, vm, vm),
         scratch_shapes=[
-            pltpu.VMEM((width, (N_TP + KVH) * HS), jnp.bfloat16),
-            pltpu.VMEM((N_TP, 4, OFF, HS), jnp.bfloat16),
-            pltpu.VMEM((KVH, 4, OFF, HS), jnp.bfloat16),
-            pltpu.SemaphoreType.DMA((N_TP + 1,)),
-            pltpu.SemaphoreType.DMA((N_TP, 2)),
-            pltpu.SemaphoreType.DMA((2, N_TP)),
-            pltpu.SemaphoreType.DMA((N_TP,)),
-            pltpu.SemaphoreType.DMA((N_TP,)),
+            pltpu.VMEM(projector.shape, bf16),
+            pltpu.VMEM((entries, depth), jnp.float32),
+            pltpu.VMEM((N_CTX, N_TP, 2 * CAP, 2 * HS), bf16),
+            pltpu.VMEM((devices, 2 * CAP, 2 * HS), bf16),
+            pltpu.VMEM((2, PAIRS, OFF, part), bf16),
+            pltpu.VMEM((N_TP, 16, part), bf16),
+            pltpu.VMEM((N_TP, 2, 2 * OFF, part), bf16),
+            pltpu.VMEM((N_TP, depth, HS), bf16),
+            pltpu.VMEM(key_weight.shape, bf16),
+            pltpu.VMEM((N_TP, 4, OFF, HS), bf16),
+            pltpu.VMEM((KVH, 4, OFF, HS), bf16),
+            dma((depth // (4 * HS),)),
+            dma,
+            dma,
+            dma,
+            dma,
+            dma((29,)),
+            dma((29,)),
+            dma((N_TP,)),
+            dma((N_TP,)),
+            dma((N_TP,)),
+            dma((N_TP,)),
+            dma((N_TP,)),
+            dma((N_TP,)),
+            dma((N_TP, 2)),
+            dma((2, N_TP)),
+            dma((N_TP,)),
+            dma((N_TP,)),
         ],
         compiler_params=pltpu.CompilerParams(
-            collective_id=2, has_side_effects=True, vmem_limit_bytes=40 * 2**20
+            collective_id=1, has_side_effects=True, vmem_limit_bytes=48 * 2**20
         ),
-        name="qkv",
-    )(normed, query_weight, key_weight, value_weight, *tables)
+        name="intake",
+    )(
+        text_embed.reshape(2, PAIRS, OFF, part),
+        jnp.broadcast_to(norm_gain[None, :], (16, part)),
+        frame_features,
+        frame_positions.reshape(1, -1),
+        frame_positions.reshape(-1, 1),
+        span_order.reshape(1, -1),
+        span_order.reshape(-1, 1),
+        *tables,
+        projector,
+        query_weight,
+        key_weight,
+        value_weight,
+    )
 
 
 def attention_kernel(
@@ -744,54 +914,6 @@
     )(span_order, attended, out_weight, rows)
 
 
-def place_frames(text_embed, frame_features, frame_positions, slot_of, projector):
-    tok_rows, part = text_embed.shape
-    tokens = frame_positions.shape[0]
-    spans = jnp.arange(slot_of.shape[0], dtype=jnp.int32)
-    slot = jnp.sum(
-        jnp.where((frame_positions // CH)[:, None] == spans[None, :], slot_of[None, :], 0), axis=1
-    )
-    target = slot // 2
-    target_row = slot % 2 * CH + frame_positions % CH
-    index = jnp.arange(tokens, dtype=jnp.int32)
-    earlier = jnp.logical_and(target[None, :] == target[:, None], index[None, :] < index[:, None])
-    place = jnp.sum(earlier.astype(jnp.int32), axis=1)
-    entry = target * CAP + place
-    entries = N_CTX * CAP
-    chosen = jnp.arange(entries, dtype=jnp.int32)[:, None] == entry[None, :]
-    sorted_features = jnp.dot(
-        chosen.astype(jnp.bfloat16), frame_features, preferred_element_type=jnp.float32
-    ).astype(jnp.bfloat16)
-    row = jnp.sum(jnp.where(chosen, target_row[None, :] + 1, 0), axis=1) - 1
-    projected = jax.nn.gelu(
-        jnp.dot(sorted_features, projector, preferred_element_type=jnp.float32), approximate=False
-    ).astype(jnp.bfloat16)
-    outgoing = jnp.transpose(
-        projected.reshape(N_CTX, CAP, N_TP, part), (0, 2, 1, 3)
-    )
-    row = row.reshape(N_CTX, 1, CAP, 1)
-    high = jnp.broadcast_to(jnp.where(row < 0, -1, row // 32), (N_CTX, N_TP, CAP, 32))
-    low = jnp.broadcast_to(jnp.where(row < 0, 0, row % 32), (N_CTX, N_TP, CAP, 32))
-    outgoing = jnp.concatenate(
-        [outgoing, high.astype(jnp.bfloat16), low.astype(jnp.bfloat16)], axis=3
-    )
-    arrived = lax.all_to_all(
-        outgoing.reshape(N_CTX * N_TP, CAP, part + 64),
-        ("ctx", "tp"),
-        split_axis=0,
-        concat_axis=0,
-        tiled=True,
-    ).reshape(N_CTX * N_TP * CAP, part + 64)
-    at = (
-        arrived[:, part].astype(jnp.float32) * 32.0 + arrived[:, part + 32].astype(jnp.float32)
-    ).astype(jnp.int32)
-    hit = jnp.arange(tok_rows, dtype=jnp.int32)[:, None] == at[None, :]
-    inserted = jnp.dot(
-        hit.astype(jnp.bfloat16), arrived[:, :part], preferred_element_type=jnp.float32
-    ).astype(jnp.bfloat16)
-    return jnp.where(jnp.any(hit, axis=1)[:, None], inserted, text_embed)
-
-
 def per_device(
     text_embed,
     frame_features,
@@ -808,17 +930,11 @@
     c = lax.axis_index("ctx")
     t = lax.axis_index("tp")
     pair = c // 2
-    core = c % 2
-    q_half = lax.all_gather(lax.dynamic_slice_in_dim(query_weight, core * HS, HS, 1), "tp")
     slots = span_order.shape[0]
     index = jnp.arange(slots, dtype=jnp.int32)
     slot_of = jnp.sum(
         jnp.where(span_order[None, :] == index[:, None], index[None, :], 0), axis=1
     )
-    placed = place_frames(text_embed, frame_features, frame_positions, slot_of, projector)
-    gain = jnp.broadcast_to(norm_gain[None, :], (16, part))
-    rows, normed = rows_exchange(placed.reshape(2, PAIRS, OFF, part), gain)
-
     spans = lax.dynamic_slice_in_dim(span_order, 4 * pair, 4, 0)
     positions = (
         spans[:, None] * CH + OFF * t + jnp.arange(OFF, dtype=jnp.int32)[None, :]
@@ -830,10 +946,9 @@
     sin = jnp.sin(angles)
     cosine = jnp.concatenate([cos, cos], axis=1)
     sine = jnp.concatenate([-sin, sin], axis=1)
-    kv_cosine = jnp.where(core == 0, cosine, 1.0)
-    kv_sine = jnp.where(core == 0, sine, 0.0)
-    query, kv = qkv_exchange(
-        normed, q_half, key_weight, value_weight, (cosine, sine, kv_cosine, kv_sine)
+    rows, query, kv = intake(
+        text_embed, norm_gain, frame_features, frame_positions, span_order, (cosine, sine),
+        projector, query_weight, key_weight, value_weight,
     )
     attended, gathered = attention(
         slot_of, query.reshape(2, 32, HALF, HS), kv.reshape(32, OFF, HS), out_weight

time: 300 us -> 260 us (0.87)
  Pallas kernels: 191 us -> 247 us
  waiting for transfers between devices: 46.2 us -> 0 us
  between operations: 13.7 us -> 0.11 us
  local copies, waits for them, and re-layouts: 22.9 us -> 10.3 us
  matrix products: 11.5 us -> 0 us
  starting transfers between devices: 10.6 us -> 0 us
    pallas_call x2 -> x1, Pallas kernels: 62.3 us -> 115 us  [intake(): pl.pallas_call(intake_kernel, out_shape=(jax.ShapeDtypeStruct((2, N_TP, 2...]
    all_gather x1 -> x0, waiting for transfers between devices: 29.7 us -> none  [per_device(): lax.all_gather(lax.dynamic_slice_in_dim(query_weight, core * HS, HS, 1),...]
    all_to_all x1 -> x0, waiting for transfers between devices: 16.4 us -> none  [place_frames(): lax.all_to_all(outgoing.reshape(N_CTX * N_TP, CAP, part + 64), ('ctx', 't...]
    dot_general x2 -> x0, matrix products: 11.5 us -> none  [the longest x1 8.12 us: place_frames(): jnp.dot(sorted_features, projector, preferred_element_type=jnp.float32)]
    all_to_all x1 -> x0, starting transfers between devices: 10.6 us -> none  [place_frames(): lax.all_to_all(outgoing.reshape(N_CTX * N_TP, CAP, part + 64), ('ctx', 't...]
    unnamed x28 -> x17, local copies, waits for them, and re-layouts: 15.1 us -> 6.77 us
    pallas_call x1, Pallas kernels: 43 us -> 46.7 us  [out_exchange(): pl.pallas_call(out_kernel, out_shape=jax.ShapeDtypeStruct((2, CH, part),...]
  transfers between devices with their start and end apart: 2 -> 0, of which waited for: 2 -> 0; matrix products, arithmetic and copies ran while one was open for 7% -> 0% of each run, Pallas kernels for 12% -> 0%
where the time goes in v4:
time: 260 us
  Pallas kernels  247 us (95%)
  local copies, waits for them, and re-layouts  10.3 us (4%)
    pallas_call x1, Pallas kernels, intake(): pl.pallas_call(intake_kernel, out_shape=(jax.ShapeDtypeStruct((2, N_TP, 2...  115 us
    pallas_call x1, Pallas kernels, attention(): pl.pallas_call(attention_kernel, out_shape=(jax.ShapeDtypeStruct((32, HAL...  85.7 us
    pallas_call x1, Pallas kernels, out_exchange(): pl.pallas_call(out_kernel, out_shape=jax.ShapeDtypeStruct((2, CH, part),...  46.7 us
    unnamed x17, local copies, waits for them, and re-layouts  6.77 us

profile of v4, /device:TPU:29, one launch (start us, length us, event | category | flops | bytes accessed | tf_op | source)
XLA Modules:
  0.0 259.9 jit_solution(7210472161721738788)
XLA Ops:
  0.0 0.0 copy-start.3
  0.0 0.9 multiply_add_fusion
  0.9 0.8 select_reduce_fusion.slot_of
  1.6 0.1 add_convert_fusion
  1.7 0.1 convert_element_type.11
  1.8 0.7 broadcast_in_dim.18.gain
  2.5 0.7 copy.17.order_col
  3.2 0.7 copy.16.pos_col
  4.0 0.5 fusion
  4.5 0.1 pad_maximum_fusion
  4.7 1.5 copy.15
  6.1 0.0 copy-done.3
  6.1 0.0 copy-start.4
  6.2 0.9 copy-done.4
  7.1 0.0 copy-start.5
  7.1 0.7 copy-done.5
  7.7 0.0 copy-start.7
  7.7 0.7 copy-done.7
  8.4 0.0 copy-start.2
  8.4 0.0 copy-start.6
  8.4 114.7 %intake.1 = (bf16[2,8,2,64,448]{4,3,2,1,0:T(8,128)(2,1)}, bf16[2,8,4,32,128]{4,3,2,1,0:T(8,128)(2,1)S(1)}, bf16[8,4,64,128]{3,2,1,0:T(8,128)(2,1)S(1)}) custom-call(bf16[2,8,64,448]{3,2,1,0:T(8,128)(2,1)S(1)} %bitcast.8, bf16[16,448]{1,0:T(8,128)(2,1)S(1)} %broadcast_in_dim.18.gain, bf16[64,1152]{1,0:T(8,128)(2,1)S(1)} %copy-done.4, s32[1,64]{1,0:T(1,128)S(1)} %bitcast.15, ...), custom_call_target="tpu_custom_call" | custom-call | tf_op jit(solution)/shard_map/intake/pallas_call | solution.py:419
  123.1 0.0 copy-start.1
  123.1 0.0 copy-done.2
  123.1 85.7 %attention.1 = (bf16[32,32,256]{2,1,0:T(8,128)(2,1)S(1)}, bf16[8,256,1792]{2,1,0:T(8,128)(2,1)}) custom-call(s32[32]{0:T(128)S(1)} %select_reduce_fusion.slot_of, bf16[2,32,32,128]{3,2,1,0:T(8,128)(2,1)S(1)} %bitcast.10, bf16[32,64,128]{2,1,0:T(8,128)(2,1)S(1)} %bitcast.11, bf16[256,3584]{1,0:T(8,128)(2,1)S(1)} %copy-done.2), custom_call_target="tpu_custom_call" | custom-call | tf_op jit(solution)/shard_map/attention/pallas_call | solution.py:699
  208.8 0.0 copy-done.6
  208.8 0.0 copy-done.1
  208.8 0.0 copy-start
  208.8 3.1 %copy-done = bf16[8,256,1792]{2,1,0:T(8,128)(2,1)S(1)} copy-done((bf16[8,256,1792]{2,1,0:T(8,128)(2,1)S(1)}, bf16[8,256,1792]{2,1,0:T(8,128)(2,1)}, u32[]{:S(2)}) %copy-start) | copy-done | bytes 7340056
  211.9 46.7 %out.1 = bf16[2,512,448]{2,1,0:T(8,128)(2,1)S(1)} custom-call(s32[32]{0:T(128)S(1)} %copy-done.6, bf16[32,32,256]{2,1,0:T(8,128)(2,1)S(1)} %get-tuple-element.12.attended, bf16[8,256,1792]{2,1,0:T(8,128)(2,1)S(1)} %copy-done, bf16[2,8,2,64,448]{4,3,2,1,0:T(8,128)(2,1)S(1)} %copy-done.1), custom_call_target="tpu_custom_call" | custom-call | tf_op jit(solution)/shard_map/out/pallas_call | solution.py:891
  258.6 1.3 copy.18
  (1 shorter events, 0.0 us)
Async XLA Ops:
  0.0 6.1 %copy-start.3 = (bf16[3584,256]{1,0:T(8,128)(2,1)S(1)}, bf16[3584,256]{1,0:T(8,128)(2,1)}, u32[]{:S(2)}) copy-start(bf16[3584,256]{1,0:T(8,128)(2,1)} %query_weight.1) | copy-start | bytes 5505028
  6.1 0.9 copy-start.4
  7.1 0.7 copy-start.5
  7.7 0.7 copy-start.7
  8.4 114.7 %copy-start.2 = (bf16[256,3584]{1,0:T(8,128)(2,1)S(1)}, bf16[256,3584]{1,0:T(8,128)(2,1)}, u32[]{:S(2)}) copy-start(bf16[256,3584]{1,0:T(8,128)(2,1)} %out_weight.1) | copy-start | bytes 5505028
  8.4 200.4 %copy-start.6 = (s32[32]{0:T(128)S(1)}, s32[32]{0:T(128)}, u32[]{:S(2)}) copy-start(s32[32]{0:T(128)} %span_order.1) | copy-start | bytes 388
  123.1 85.7 %copy-start.1 = (bf16[2,8,2,64,448]{4,3,2,1,0:T(8,128)(2,1)S(1)}, bf16[2,8,2,64,448]{4,3,2,1,0:T(8,128)(2,1)}, u32[]{:S(2)}) copy-start(bf16[2,8,2,64,448]{4,3,2,1,0:T(8,128)(2,1)} %get-tuple-element.14.rows) | copy-start | bytes 5505028
  208.8 3.1 %copy-start = (bf16[8,256,1792]{2,1,0:T(8,128)(2,1)S(1)}, bf16[8,256,1792]{2,1,0:T(8,128)(2,1)}, u32[]{:S(2)}) copy-start(bf16[8,256,1792]{2,1,0:T(8,128)(2,1)} %get-tuple-element.13.out_weight) | copy-start | bytes 22020100

commit v5 on v4

--- a/solution.py
+++ b/solution.py
@@ -47,10 +47,10 @@
 def intake_kernel(
     text, gain, features, pos_row, pos_col, order_row, order_col, cosine, sine,
     projector, query_weight, key_weight, value_weight,
-    rows, query_out, kv_out,
-    pweight, projected, outgoing, incoming, placed, gains, normed, weight, kv_weight, query, kv,
-    psem, own_sem, kv_sem, fr_send, fr_recv, wsend, wrecv,
-    send, recv, fsend, frecv, gsend, grecv, qsend, qrecv, ksend, krecv,
+    rows_out, query_out, kv_out,
+    pweight, outgoing, incoming, placed, rows, gains, normed, weight, kv_weight, query, kv,
+    psem, own_sem, kv_sem, fr_send, fr_recv, wsend, wrecv, csend, crecv,
+    send, recv, gsend, grecv, osem, osend, orecv, qsend, qrecv, ksend, krecv,
 ):
     c = lax.axis_index("ctx")
     t = lax.axis_index("tp")
@@ -66,32 +66,31 @@
     z_up, z_down, z_far = (base + add4(z, n) for n in (1, 3, 2))
     y = lax.rem(t, 4)
     side = t - y
-    across = 4 - side
-    t_up, t_down, t_far = (side + add4(y, n) for n in (1, 3, 2))
-    a_own, a_up, a_down, a_far = (across + add4(y, n) for n in (0, 1, 3, 2))
-    x_next = 2 * (4 - base + z) + core
+    half = t // 4
+    y_up, y_down, y_far = (add4(y, n) for n in (1, 3, 2))
 
     own_copy = pltpu.make_async_copy(
-        query_weight.at[:, pl.ds(pl.multiple_of(HS * core, HS), HS)], weight.at[t], own_sem
+        query_weight.at[:, pl.ds(pl.multiple_of(HS * core, HS), HS)], weight.at[core, y], own_sem
     )
     own_copy.start()
     block = 4 * HS
-    blocks = width // block
-
-    def load(n):
-        cols = pl.ds(n * block, block)
-        return pltpu.make_async_copy(projector.at[:, cols], pweight.at[:, cols], psem.at[n])
-
-    for n in range(blocks):
-        load(n).start()
-
-    @pl.when(core == 0)
-    def _():
-        pltpu.make_async_copy(key_weight, kv_weight, kv_sem).start()
-
-    @pl.when(core == 1)
-    def _():
-        pltpu.make_async_copy(value_weight, kv_weight, kv_sem).start()
+
+    def load(d):
+        j = lax.rem(t + d, N_TP)
+        start = pl.multiple_of((j * part) // HS * HS, HS)
+        return pltpu.make_async_copy(
+            projector.at[:, pl.ds(start, block)], pweight.at[d], psem.at[d]
+        )
+
+    for d in range(N_TP):
+        load(d).start()
+    kv_cols = pl.ds(pl.multiple_of(2 * HS * half, HS), 2 * HS)
+    kv_loads = [
+        pltpu.make_async_copy(ref.at[:, kv_cols], kv_weight.at[n], kv_sem.at[n])
+        for n, ref in enumerate((key_weight, value_weight))
+    ]
+    for one in kv_loads:
+        one.start()
 
     barrier = pltpu.get_barrier_semaphore()
 
@@ -135,10 +134,12 @@
     row_at = row_at.astype(jnp.int32)
     high = (row_at >> 5).astype(f32)
     low = (row_at & 31).astype(f32)
+    lane = lax.broadcasted_iota(jnp.int32, (entries, block), 1)
+    tail = jnp.where(lane < part + 32, high, jnp.where(lane < part + 48, low, 1.0))
 
     pl.semaphore_wait(barrier, devices - 1)
 
-    depth = weight.shape[1]
+    depth = weight.shape[2]
     direct = pl.ds(0, depth // 2)
 
     def eighth(n):
@@ -148,84 +149,87 @@
         return pl.ds(depth // 4 * n, depth // 4)
 
     def wmove(m):
-        if m == 0:
-            ref, ctx, tp = weight.at[t], x_next, a_own
-        elif m < 11:
-            shard = t if m < 6 else a_own
+        if m < 5:
             cut, tp = (
-                (direct, t_up), (direct, t_down), (eighth(z), t_up), (eighth(z), t_down),
-                (quarter(z), t_far),
-            )[(m - 1) % 5]
-            ref, ctx = weight.at[shard, cut], c
+                (direct, y_up), (direct, y_down), (eighth(z), y_up), (eighth(z), y_down),
+                (quarter(z), y_far),
+            )[m]
+            ref, ctx, tp = weight.at[core, y, cut], c, side + tp
         else:
-            n = m - 11
-            shard = (t_up, t_down, t_far, a_up, a_down, a_far)[n // 3]
-            cut = quarter(z) if n // 3 % 3 == 2 else eighth(z)
-            ref, tp = weight.at[shard, cut], t
+            n = m - 5
+            cut = quarter(z) if n // 3 == 2 else eighth(z)
+            ref, tp = weight.at[core, (y_up, y_down, y_far)[n // 3], cut], t
             ctx = 2 * (z_up, z_down, z_far)[n % 3] + core
         return push(ref, ref, wsend.at[m], wrecv.at[m], ctx, tp)
 
     def warrive(m):
-        if m == 0:
-            ref = weight.at[a_own]
-        elif m < 11:
-            n = (m - 1) % 5
-            shard = ((t_down, t_up, t_down, t_up, t_far), (a_down, a_up, a_down, a_up, a_far))[
-                (m - 1) // 5
-            ][n]
-            cut = (direct, direct, eighth(z), eighth(z), quarter(z))[n]
-            ref = weight.at[shard, cut]
+        if m < 5:
+            shard = (y_down, y_up, y_down, y_up, y_far)[m]
+            cut = (direct, direct, eighth(z), eighth(z), quarter(z))[m]
         else:
-            n = m - 11
-            shard = (t_up, t_down, t_far, a_up, a_down, a_far)[n // 3]
+            n = m - 5
+            shard = (y_up, y_down, y_far)[n // 3]
             origin = (add4(z, 3), add4(z, 1), add4(z, 2))[n % 3]
-            cut = quarter(origin) if n // 3 % 3 == 2 else eighth(origin)
-            ref = weight.at[shard, cut]
+            cut = quarter(origin) if n // 3 == 2 else eighth(origin)
+        ref = weight.at[core, shard, cut]
         push(ref, ref, wsend.at[m], wrecv.at[m], sibling, t).wait_recv()
 
+    def share(n):
+        ref = weight.at[core, add4(y, n)]
+        return push(ref, ref, csend.at[n], crecv.at[n], sibling, t)
+
+    def shared(n):
+        ref = weight.at[1 - core, add4(y, n)]
+        push(ref, ref, csend.at[n], crecv.at[n], sibling, t).wait_recv()
+
     own_copy.wait()
-    for m in (0, 5, 3, 4, 1, 2):
+    for m in (4, 2, 3, 0, 1):
         wmove(m).start()
-
-    for n in range(blocks):
-        load(n).wait()
-        cols = slice(n * block, (n + 1) * block)
-        x = jnp.dot(ordered, pweight[:, cols], preferred_element_type=f32)
-        projected[:, cols] = 0.5 * x * (1.0 + lax.erf(x * math.sqrt(0.5)))
-    lane = lax.broadcasted_iota(jnp.int32, (entries, block), 1)
-    tail = jnp.where(lane < part + 32, high, jnp.where(lane < part + 48, low, 1.0))
-    for j in range(N_TP):
-        start = j * part // HS * HS
-        shift = j * part - start
-        x = projected[:, start : start + block]
-        if shift:
-            x = pltpu.roll(x, block - shift, 1)
+    share(0).start()
+
+    for d in range(N_TP):
+        j = lax.rem(t + d, N_TP)
+        load(d).wait()
+        x = jnp.dot(ordered, pweight[d], preferred_element_type=f32)
+        x = 0.5 * x * (1.0 + lax.erf(x * math.sqrt(0.5)))
+        shift = j * part - (j * part) // HS * HS
+        x = jnp.where(shift > 0, pltpu.roll(x, block - HS // 2, 1), x)
         x = jnp.where(lane < part, x, tail)
         halves = [
             x[:, n * 2 * HS : (n + 1) * 2 * HS].reshape(N_CTX, CAP, 2 * HS) for n in range(2)
         ]
-        outgoing[:, j] = jnp.concatenate(halves, axis=1).astype(jnp.bfloat16)
-
-    here = pltpu.make_async_copy(outgoing.at[c, t], incoming.at[me], fr_recv)
-    here.start()
-
-    def deliver(d, unused):
-        other = lax.rem(me + d, devices)
-        oc = other // N_TP
-        ot = lax.rem(other, N_TP)
-        push(outgoing.at[oc, ot], incoming.at[me], fr_send, fr_recv, oc, ot).start()
-        return unused
-
-    lax.fori_loop(1, devices, deliver, 0)
-    for m in (3, 4, 5):
+        outgoing[d] = jnp.concatenate(halves, axis=1).astype(jnp.bfloat16)
+
+        def deliver(n, unused):
+            oc = lax.rem(c + n, N_CTX)
+            push(outgoing.at[d, oc], incoming.at[me], fr_send, fr_recv, oc, j).start()
+            return unused
+
+        if d == 0:
+            pltpu.make_async_copy(outgoing.at[0, c], incoming.at[me], fr_recv).start()
+        else:
+            push(outgoing.at[d, c], incoming.at[me], fr_send, fr_recv, c, j).start()
+        lax.fori_loop(1, N_CTX, deliver, 0)
+
+    for m in (2, 3, 4):
         warrive(m)
-    for m in range(11, 20):
-        wmove(m).start()
-    warrive(0)
-    for m in (10, 8, 9, 6, 7):
+    for m in range(5, 14):
         wmove(m).start()
     pltpu.make_async_copy(incoming, incoming, fr_recv).wait()
 
+    def row_block(n, across):
+        j = add4(y, n)
+        tp = j + (4 - side if across else side)
+        return push(
+            placed.at[:, j], rows.at[t], send.at[n, across], recv.at[t], c, tp
+        )
+
+    def gain_block(d):
+        return push(gain, gains.at[t], gsend.at[d], grecv.at[t], c, lax.rem(t + d, N_TP))
+
+    pltpu.make_async_copy(gain, gains.at[t], grecv.at[t]).start()
+    for d in range(1, N_TP):
+        gain_block(d).start()
     arrived = incoming[...].astype(f32)
     slots = devices * CAP
     left = arrived[:, :CAP].reshape(slots, 2 * HS)
@@ -235,173 +239,177 @@
     at = jnp.transpose(jnp.broadcast_to(at, (slots, HS)))[0:1, :]
     left = left.astype(jnp.bfloat16)
     right = right.astype(jnp.bfloat16)
-    group = CH // 2
+    group = 2 * HS
+    offset = lax.broadcasted_iota(jnp.int32, (group, 1), 0)
+    offset = offset // HS * CH + offset % HS
     for n in range(4):
-        a, b = n // 2, n % 2 * 4
-        row = lax.broadcasted_iota(jnp.int32, (group, 1), 0) + n * group
+        j = add4(y, n)
+        row = offset + j * HS
         hit = jnp.where(row.astype(f32) == at, 1.0, 0.0).astype(jnp.bfloat16)
         new_left = jnp.dot(hit, left, preferred_element_type=f32)
         new_right = jnp.dot(hit, right, preferred_element_type=f32)
         framed = new_right[:, 2 * HS - 1 :] > 0.5
-        old = text[a, b : b + 4].reshape(group, part).astype(f32)
-        placed[a, b : b + 4, :, : 2 * HS] = (
+        old = text[:, j].reshape(group, part).astype(f32)
+        placed[:, j, :, : 2 * HS] = (
             jnp.where(framed, new_left, old[:, : 2 * HS]).astype(jnp.bfloat16)
-        ).reshape(4, OFF, 2 * HS)
-        placed[a, b : b + 4, :, 2 * HS :] = (
+        ).reshape(2, HS, 2 * HS)
+        placed[:, j, :, 2 * HS :] = (
             jnp.where(framed, new_right[:, :edge], old[:, 2 * HS :]).astype(jnp.bfloat16)
-        ).reshape(4, OFF, edge)
-
-    def row_block(d):
-        j = lax.rem(t + d, N_TP)
-        return push(placed.at[:, j], rows.at[core, t], send.at[d], recv.at[t], c, j)
-
-    def gain_block(d):
-        j = lax.rem(t + d, N_TP)
-        return push(gain, gains.at[t], gsend.at[d], grecv.at[t], c, j)
-
-    pltpu.make_async_copy(placed.at[:, t], rows.at[core, t], recv.at[t]).start()
-    pltpu.make_async_copy(gain, gains.at[t], grecv.at[t]).start()
-    for d in range(1, N_TP):
-        row_block(d).start()
-        gain_block(d).start()
-
-    def forward(j):
-        return push(rows.at[core, j], rows.at[core, j], fsend.at[j], frecv.at[j], sibling, t)
-
+        ).reshape(2, HS, edge)
+        row_block(n, 1).start()
+        if n == 0:
+            pltpu.make_async_copy(placed.at[:, y], rows.at[t], recv.at[t]).start()
+        else:
+            row_block(n, 0).start()
+
+    for m in (0, 1, *range(5, 14)):
+        warrive(m)
+    for n in range(1, 4):
+        share(n).start()
+    for one in kv_loads:
+        one.wait()
+
+    total = jnp.zeros((group, 1), f32)
     for d in range(N_TP):
         j = lax.rem(t + d, N_TP)
-        push(rows.at[core, j], rows.at[core, j], send.at[0], recv.at[j], sibling, t).wait_recv()
-        forward(j).start()
+        push(gain, gains.at[j], gsend.at[0], grecv.at[j], sibling, t).wait_recv()
+        push(rows.at[j], rows.at[j], send.at[0, 0], recv.at[j], sibling, t).wait_recv()
+        x = rows[j].reshape(group, part).astype(f32)
+        total = total + jnp.sum(x * x, axis=1, keepdims=True)
+
+    def keep(n):
+        return pltpu.make_async_copy(
+            rows.at[4 * core + n, :, pl.ds(OFF * half, OFF)], rows_out.at[core, n], osem.at[n]
+        )
+
+    def give(n):
+        return push(
+            rows.at[4 * (1 - core) + n, :, pl.ds(OFF * half, OFF)], rows_out.at[core, n],
+            osend.at[n], orecv.at[n], sibling, t,
+        )
+
+    for n in range(4):
+        keep(n).start()
+        give(n).start()
+
+    inverse = lax.rsqrt(total / width + 1e-06)
     for j in range(N_TP):
-        push(gain, gains.at[j], gsend.at[0], grecv.at[j], sibling, t).wait_recv()
-    for m in (8, 9, 10):
-        warrive(m)
-    for m in range(20, 29):
-        wmove(m).start()
-
-    def normalise(a):
-        total = jnp.zeros((2 * OFF, 1), f32)
-        for j in range(N_TP):
-            x = rows[a, j].reshape(2 * OFF, part).astype(f32)
-            total = total + jnp.sum(x * x, axis=1, keepdims=True)
-        inverse = lax.rsqrt(total / width + 1e-06)
-        for j in range(N_TP):
-            x = rows[a, j].reshape(2 * OFF, part).astype(f32)
-            g = gains[j, 0:1, :].astype(f32)
-            normed[j, a] = (x * inverse * g).astype(jnp.bfloat16)
-
-    normalise(core)
-    for j in range(N_TP):
-        push(
-            rows.at[1 - core, j], rows.at[1 - core, j], fsend.at[j], frecv.at[j], sibling, t
-        ).wait_recv()
-    normalise(1 - core)
+        x = rows[j].reshape(group, part).astype(f32)
+        normed[j] = (x * inverse * gains[j, 0:1, :].astype(f32)).astype(jnp.bfloat16)
 
     def product(piece):
         total = None
         for j in range(N_TP):
-            x = normed[j].reshape(4 * OFF, part)
-            term = jnp.dot(x, piece(slice(j * part, (j + 1) * part)), preferred_element_type=f32)
+            term = jnp.dot(
+                normed[j], piece(slice(j * part, (j + 1) * part)), preferred_element_type=f32
+            )
             total = term if total is None else total + term
         return total
 
     def rotated(x, cos, sin):
-        return (x * cos + pltpu.roll(x, HS // 2, 1) * sin).astype(jnp.bfloat16).reshape(4, OFF, HS)
-
-    goal = pair_of(pair, t)
-    own = t == 0
-
-    def kv_push(d):
-        j = lax.rem(t + d, N_TP)
-        return push(kv.at[j // 2], kv_out.at[pair], ksend.at[d], krecv.at[pair], 2 * goal + core, j)
-
-    def q_push(j, k):
+        return (x * cos + pltpu.roll(x, HS // 2, 1) * sin).astype(jnp.bfloat16).reshape(2, HS, HS)
+
+    goal = [pair_of(pair, 4 * n + y) for n in range(2)]
+    mine = pl.ds(2 * core, 2)
+
+    def kv_push(n, which, m):
         return push(
-            query.at[j, :, pl.ds(k * HALF, HALF), :], query_out.at[core, pair],
-            qsend.at[j, k], qrecv.at[core, pair], 2 * goal + k, j,
-        )
-
-    pltpu.make_async_copy(key_weight, kv_weight, kv_sem).wait()
+            kv.at[which, m // 2, :, pl.ds(OFF * n, OFF), :], kv_out.at[pair, mine],
+            ksend.at[n, which, m], krecv.at[pair, core], 2 * goal[n] + which, side + m,
+        )
+
+    def q_push(n, k, m):
+        return push(
+            query.at[m, :, :, pl.ds(OFF * n + HALF * k, HALF), :], query_out.at[:, pair, mine],
+            qsend.at[n, k, m], qrecv.at[pair, core], 2 * goal[n] + k, side + m,
+        )
+
+    def is_here(n, k, m):
+        return jnp.logical_and(goal[n] == pair, jnp.logical_and(core == k, y == m))
+
     cos = cosine[...]
     sin = sine[...]
-    kv_cos = jnp.where(core == 0, cos, 1.0)
-    kv_sin = jnp.where(core == 0, sin, 0.0)
-    for h in range(0, KVH, 2):
-        total = product(lambda cut: kv_weight[cut, h * HS : (h + 2) * HS])
+    for which in range(2):
+        out = product(lambda cut: kv_weight[which, cut, :])
+        for h in range(2):
+            x = out[:, h * HS : (h + 1) * HS]
+            kv[which, h] = rotated(x, cos, sin) if which == 0 else x.astype(
+                jnp.bfloat16
+            ).reshape(2, HS, HS)
+        for m in range(4):
+            for n in range(2):
+
+                @pl.when(is_here(n, which, m))
+                def _():
+                    pltpu.make_async_copy(
+                        kv.at[which, m // 2, :, pl.ds(OFF * n, OFF), :], kv_out.at[pair, mine],
+                        krecv.at[pair, core],
+                    ).start()
+
+                @pl.when(jnp.logical_not(is_here(n, which, m)))
+                def _():
+                    kv_push(n, which, m).start()
+
+    for m0 in range(4):
+        m = add4(y, m0)
+        shared(m0)
+        out = product(
+            lambda cut: jnp.concatenate([weight[0, m, cut], weight[1, m, cut]], axis=1)
+        )
+        for h in range(2):
+            query[m, h] = rotated(out[:, h * HS : (h + 1) * HS], cos, sin)
         for n in range(2):
-            kv[h + n] = rotated(total[:, n * HS : (n + 1) * HS], kv_cos, kv_sin)
-
-    @pl.when(own)
-    def _():
-        pltpu.make_async_copy(kv.at[t // 2], kv_out.at[pair], krecv.at[pair]).start()
-
-    @pl.when(jnp.logical_not(own))
-    def _():
-        kv_push(0).start()
-
-    for d in range(1, N_TP):
-        kv_push(d).start()
-
-    def is_here(j, k):
-        return jnp.logical_and(own, jnp.logical_and(j == t, core == k))
-
-    def heads(begin):
-        for h in range(0, 4, 2):
-            j0, j1 = begin + h, begin + h + 1
-            total = product(
-                lambda cut: jnp.concatenate([weight[j0, cut], weight[j1, cut]], axis=1)
-            )
-            for n, j in enumerate((j0, j1)):
-                query[j] = rotated(total[:, n * HS : (n + 1) * HS], cos, sin)
-                for k in range(2):
-
-                    @pl.when(is_here(j, k))
+            for k in range(2):
+                if m0 == 0:
+                    here = jnp.logical_and(goal[n] == pair, core == k)
+
+                    @pl.when(here)
                     def _():
                         pltpu.make_async_copy(
-                            query.at[j, :, pl.ds(k * HALF, HALF), :], query_out.at[core, pair],
-                            qrecv.at[core, pair],
+                            query.at[m, :, :, pl.ds(OFF * n + HALF * k, HALF), :],
+                            query_out.at[:, pair, mine], qrecv.at[pair, core],
                         ).start()
 
-                    @pl.when(jnp.logical_not(is_here(j, k)))
+                    @pl.when(jnp.logical_not(here))
                     def _():
-                        q_push(j, k).start()
-
-    for m in (1, 2, *range(11, 20)):
-        warrive(m)
-    heads(side)
-    for m in (6, 7, *range(20, 29)):
-        warrive(m)
-    heads(across)
+                        q_push(n, k, m).start()
+
+                else:
+                    q_push(n, k, m).start()
 
     for e in range(PAIRS):
-        push(kv.at[0], kv_out.at[e], ksend.at[0], krecv.at[e], c, t).wait_recv()
-        for k in range(2):
-            push(
-                query_out.at[k, e], query_out.at[k, e], qsend.at[0, 0], qrecv.at[k, e], c, t
-            ).wait_recv()
+        for a in range(2):
+            two = pl.ds(2 * a, 2)
+            ref = kv_out.at[e, two]
+            push(ref, ref, ksend.at[0, 0, 0], krecv.at[e, a], sibling, t).wait_recv()
+            ref = query_out.at[:, e, two]
+            push(ref, ref, qsend.at[0, 0, 0], qrecv.at[e, a], sibling, t).wait_recv()
+    for n in range(4):
+        keep(n).wait()
+        push(
+            rows_out.at[1 - core, n], rows_out.at[1 - core, n], osend.at[n], orecv.at[n], sibling, t
+        ).wait_recv()
+        give(n).wait_send()
     pltpu.make_async_copy(
         incoming.at[pl.ds(0, devices - 1)], incoming.at[pl.ds(0, devices - 1)], fr_send
     ).wait()
-    for m in range(29):
+    for m in range(14):
         wmove(m).wait_send()
+    for n in range(4):
+        share(n).wait_send()
+        row_block(n, 1).wait_send()
+        if n:
+            row_block(n, 0).wait_send()
     for d in range(1, N_TP):
-        row_block(d).wait_send()
         gain_block(d).wait_send()
-    for j in range(N_TP):
-        forward(j).wait_send()
-
-    @pl.when(jnp.logical_not(own))
-    def _():
-        kv_push(0).wait_send()
-
-    for d in range(1, N_TP):
-        kv_push(d).wait_send()
-    for j in range(N_TP):
+    for n in range(2):
         for k in range(2):
-
-            @pl.when(jnp.logical_not(is_here(j, k)))
-            def _():
-                q_push(j, k).wait_send()
+            for m in range(4):
+
+                @pl.when(jnp.logical_not(is_here(n, k, m)))
+                def _():
+                    kv_push(n, k, m).wait_send()
+                    q_push(n, k, m).wait_send()
 
 
 def intake(
@@ -410,7 +418,6 @@
 ):
     tok_rows, part = text_embed.shape
     depth = query_weight.shape[0]
-    entries = N_CTX * CAP
     devices = N_CTX * N_TP
     vm = pl.BlockSpec(memory_space=pltpu.VMEM)
     anywhere = pl.BlockSpec(memory_space=pl.ANY)
@@ -419,48 +426,51 @@
     return pl.pallas_call(
         intake_kernel,
         out_shape=(
-            jax.ShapeDtypeStruct((2, N_TP, 2, OFF, part), bf16),
-            jax.ShapeDtypeStruct((2, N_TP, 4, HALF, HS), bf16),
-            jax.ShapeDtypeStruct((N_TP, 4, OFF, HS), bf16),
+            jax.ShapeDtypeStruct((2, 4, 2, OFF, part), bf16),
+            jax.ShapeDtypeStruct((2, PAIRS, 4, HALF, HS), bf16),
+            jax.ShapeDtypeStruct((PAIRS, 4, OFF, HS), bf16),
         ),
         in_specs=[vm] * 9 + [anywhere] * 4,
         out_specs=(vm, vm, vm),
         scratch_shapes=[
-            pltpu.VMEM(projector.shape, bf16),
-            pltpu.VMEM((entries, depth), jnp.float32),
-            pltpu.VMEM((N_CTX, N_TP, 2 * CAP, 2 * HS), bf16),
+            pltpu.VMEM((N_TP, projector.shape[0], 4 * HS), bf16),
+            pltpu.VMEM((N_TP, N_CTX, 2 * CAP, 2 * HS), bf16),
             pltpu.VMEM((devices, 2 * CAP, 2 * HS), bf16),
-            pltpu.VMEM((2, PAIRS, OFF, part), bf16),
+            pltpu.VMEM((2, 4, HS, part), bf16),
+            pltpu.VMEM((N_TP, 2, HS, part), bf16),
             pltpu.VMEM((N_TP, 16, part), bf16),
-            pltpu.VMEM((N_TP, 2, 2 * OFF, part), bf16),
-            pltpu.VMEM((N_TP, depth, HS), bf16),
-            pltpu.VMEM(key_weight.shape, bf16),
-            pltpu.VMEM((N_TP, 4, OFF, HS), bf16),
-            pltpu.VMEM((KVH, 4, OFF, HS), bf16),
-            dma((depth // (4 * HS),)),
+            pltpu.VMEM((N_TP, 2 * HS, part), bf16),
+            pltpu.VMEM((2, 4, depth, HS), bf16),
+            pltpu.VMEM((2, depth, 2 * HS), bf16),
+            pltpu.VMEM((4, 2, 2, HS, HS), bf16),
+            pltpu.VMEM((2, 2, 2, HS, HS), bf16),
+            dma((N_TP,)),
+            dma,
+            dma((2,)),
             dma,
             dma,
-            dma,
-            dma,
-            dma((29,)),
-            dma((29,)),
+            dma((14,)),
+            dma((14,)),
+            dma((4,)),
+            dma((4,)),
+            dma((4, 2)),
             dma((N_TP,)),
             dma((N_TP,)),
             dma((N_TP,)),
-            dma((N_TP,)),
-            dma((N_TP,)),
-            dma((N_TP,)),
-            dma((N_TP, 2)),
-            dma((2, N_TP)),
-            dma((N_TP,)),
-            dma((N_TP,)),
+            dma((4,)),
+            dma((4,)),
+            dma((4,)),
+            dma((2, 2, 4)),
+            dma((PAIRS, 2)),
+            dma((2, 2, 4)),
+            dma((PAIRS, 2)),
         ],
         compiler_params=pltpu.CompilerParams(
             collective_id=1, has_side_effects=True, vmem_limit_bytes=48 * 2**20
         ),
         name="intake",
     )(
-        text_embed.reshape(2, PAIRS, OFF, part),
+        text_embed.reshape(2, 4, HS, part),
         jnp.broadcast_to(norm_gain[None, :], (16, part)),
         frame_features,
         frame_positions.reshape(1, -1),
@@ -584,7 +594,8 @@
     def starts(index, i, e):
         value = jnp.zeros(index.shape, jnp.int32)
         for a in range(4):
-            start = a * CH + OFF * class_of(slot_of[4 * i + a] // 4, e)
+            kind = class_of(slot_of[4 * i + a] // 4, e)
+            start = a * CH + HS * lax.rem(kind, 4) + OFF * (kind // 4)
             value = jnp.where(index // OFF == a, start, value)
         return value
 
@@ -813,9 +824,11 @@
 
     part = out.shape[-1]
 
+    place = HS * lax.rem(t, 4) + OFF * side
+
     def send_home(j, a):
         return push(
-            result.at[j, a], out.at[:, pl.ds(OFF * t, OFF), :], rsend.at[j, a], rrecv.at[t],
+            result.at[j, a], out.at[:, pl.ds(place, OFF), :], rsend.at[j, a], rrecv.at[t],
             2 * pair + a, parts * core + j,
         )
 
@@ -846,7 +859,7 @@
             total = pltpu.roll(total, window - shift, 1)
         total = total[:, :part]
         for a in range(2):
-            placed = rows[a, parts * core + j].reshape(2 * OFF, part).astype(jnp.float32)
+            placed = rows[a, j].reshape(2 * OFF, part).astype(jnp.float32)
             result[j, a] = (placed + total[a * 2 * OFF : (a + 1) * 2 * OFF]).astype(
                 jnp.bfloat16
             ).reshape(2, OFF, part)
@@ -854,7 +867,7 @@
             @pl.when(is_home(j, a))
             def _():
                 pltpu.make_async_copy(
-                    result.at[j, a], out.at[:, pl.ds(OFF * t, OFF), :], rrecv.at[t]
+                    result.at[j, a], out.at[:, pl.ds(place, OFF), :], rrecv.at[t]
                 ).start()
 
             @pl.when(jnp.logical_not(is_home(j, a)))
@@ -929,15 +942,14 @@
     tok_rows, part = text_embed.shape
     c = lax.axis_index("ctx")
     t = lax.axis_index("tp")
-    pair = c // 2
     slots = span_order.shape[0]
     index = jnp.arange(slots, dtype=jnp.int32)
     slot_of = jnp.sum(
         jnp.where(span_order[None, :] == index[:, None], index[None, :], 0), axis=1
     )
-    spans = lax.dynamic_slice_in_dim(span_order, 4 * pair, 4, 0)
+    spans = lax.dynamic_slice_in_dim(span_order, 2 * c, 2, 0)
     positions = (
-        spans[:, None] * CH + OFF * t + jnp.arange(OFF, dtype=jnp.int32)[None, :]
+        spans[:, None] * CH + HS * (t % 4) + jnp.arange(HS, dtype=jnp.int32)[None, :]
     ).reshape(-1)
     half = HS // 2
     freqs = 1000000.0 ** (-(jnp.arange(half, dtype=jnp.float32) * 2.0 / HS))

time: 260 us -> 233 us (0.90)
  Pallas kernels: 247 us -> 220 us
    pallas_call x1, Pallas kernels: 115 us -> 88 us  [intake(): pl.pallas_call(intake_kernel, out_shape=(jax.ShapeDtypeStruct((2, 4, 2, O...]
    unnamed x17 -> x15, local copies, waits for them, and re-layouts: 6.77 us -> 6.77 us
where the time goes in v5:
time: 233 us; the launch traced here: 232 us
  Pallas kernels  220 us (94%)
  local copies, waits for them, and re-layouts  10.2 us (4%)
  other arithmetic  2.38 us (1%)
    pallas_call x1, Pallas kernels, intake(): pl.pallas_call(intake_kernel, out_shape=(jax.ShapeDtypeStruct((2, 4, 2, O...  88 us
    pallas_call x1, Pallas kernels, attention(): pl.pallas_call(attention_kernel, out_shape=(jax.ShapeDtypeStruct((32, HAL...  85.5 us
    pallas_call x1, Pallas kernels, out_exchange(): pl.pallas_call(out_kernel, out_shape=jax.ShapeDtypeStruct((2, CH, part),...  46.2 us
    unnamed x15, local copies, waits for them, and re-layouts  6.77 us

profile of v5, /device:TPU:29, one launch (start us, length us, event | category | flops | bytes accessed | tf_op | source)
XLA Modules:
  0.0 232.4 jit_solution(17431623765295411885)
XLA Ops:
  0.0 0.0 copy-start.2
  0.0 0.9 multiply_add_fusion
  0.9 0.1 convert_bitcast_fusion
  0.9 0.8 select_reduce_fusion.slot_of
  1.7 0.7 broadcast_in_dim.18.gain
  2.4 0.7 copy.17.order_col
  3.1 0.7 copy.16.pos_col
  3.9 0.5 fusion
  4.4 0.1 pad_maximum_fusion
  4.6 1.5 copy.15
  6.0 0.0 copy-done.2
  6.1 0.0 copy-start.3
  6.1 0.9 copy-done.3
  7.0 0.0 copy-start.4
  7.0 0.7 copy-done.4
  7.6 0.0 copy-start.6
  7.6 0.7 copy-done.6
  8.3 0.0 copy-start.1
  8.3 0.0 copy-start.5
  8.3 88.0 %intake.1 = (bf16[2,4,2,64,448]{4,3,2,1,0:T(8,128)(2,1)S(1)}, bf16[2,8,4,32,128]{4,3,2,1,0:T(8,128)(2,1)S(1)}, bf16[8,4,64,128]{3,2,1,0:T(8,128)(2,1)S(1)}) custom-call(bf16[2,4,128,448]{3,2,1,0:T(8,128)(2,1)S(1)} %bitcast.10, bf16[16,448]{1,0:T(8,128)(2,1)S(1)} %broadcast_in_dim.18.gain, bf16[64,1152]{1,0:T(8,128)(2,1)S(1)} %copy-done.3, ...), custom_call_target="tpu_custom_call" | custom-call | tf_op jit(solution)/shard_map/intake/pallas_call | solution.py:426
  96.2 0.0 copy-done.1
  96.3 85.5 %attention.1 = (bf16[32,32,256]{2,1,0:T(8,128)(2,1)S(1)}, bf16[8,256,1792]{2,1,0:T(8,128)(2,1)}) custom-call(s32[32]{0:T(128)S(1)} %select_reduce_fusion.slot_of, bf16[2,32,32,128]{3,2,1,0:T(8,128)(2,1)S(1)} %bitcast.12, bf16[32,64,128]{2,1,0:T(8,128)(2,1)S(1)} %bitcast.13, bf16[256,3584]{1,0:T(8,128)(2,1)S(1)} %copy-done.1), custom_call_target="tpu_custom_call" | custom-call | tf_op jit(solution)/shard_map/attention/pallas_call | solution.py:710
  181.8 0.0 copy-done.5
  181.8 0.0 copy-start
  181.8 3.1 %copy-done = bf16[8,256,1792]{2,1,0:T(8,128)(2,1)S(1)} copy-done((bf16[8,256,1792]{2,1,0:T(8,128)(2,1)S(1)}, bf16[8,256,1792]{2,1,0:T(8,128)(2,1)}, u32[]{:S(2)}) %copy-start) | copy-done | bytes 7340056
  184.9 46.2 %out.1 = bf16[2,512,448]{2,1,0:T(8,128)(2,1)S(1)} custom-call(s32[32]{0:T(128)S(1)} %copy-done.5, bf16[32,32,256]{2,1,0:T(8,128)(2,1)S(1)} %get-tuple-element.12.attended, bf16[8,256,1792]{2,1,0:T(8,128)(2,1)S(1)} %copy-done, bf16[2,4,2,64,448]{4,3,2,1,0:T(8,128)(2,1)S(1)} %get-tuple-element.14.rows), custom_call_target="tpu_custom_call" | custom-call | tf_op jit(solution)/shard_map/out/pallas_call | solution.py:904
  231.1 1.3 copy.18
  (1 shorter events, 0.0 us)
Async XLA Ops:
  0.0 6.0 %copy-start.2 = (bf16[3584,256]{1,0:T(8,128)(2,1)S(1)}, bf16[3584,256]{1,0:T(8,128)(2,1)}, u32[]{:S(2)}) copy-start(bf16[3584,256]{1,0:T(8,128)(2,1)} %query_weight.1) | copy-start | bytes 5505028
  6.1 0.9 copy-start.3
  7.0 0.7 copy-start.4
  7.6 0.7 copy-start.6
  8.3 88.0 %copy-start.1 = (bf16[256,3584]{1,0:T(8,128)(2,1)S(1)}, bf16[256,3584]{1,0:T(8,128)(2,1)}, u32[]{:S(2)}) copy-start(bf16[256,3584]{1,0:T(8,128)(2,1)} %out_weight.1) | copy-start | bytes 5505028
  8.3 173.5 %copy-start.5 = (s32[32]{0:T(128)S(1)}, s32[32]{0:T(128)}, u32[]{:S(2)}) copy-start(s32[32]{0:T(128)} %span_order.1) | copy-start | bytes 388
  181.8 3.1 %copy-start = (bf16[8,256,1792]{2,1,0:T(8,128)(2,1)S(1)}, bf16[8,256,1792]{2,1,0:T(8,128)(2,1)}, u32[]{:S(2)}) copy-start(bf16[8,256,1792]{2,1,0:T(8,128)(2,1)} %get-tuple-element.13.out_weight) | copy-start | bytes 22020100

commit v6 on v5

--- a/solution.py
+++ b/solution.py
@@ -50,7 +50,7 @@
     rows_out, query_out, kv_out,
     pweight, outgoing, incoming, placed, rows, gains, normed, weight, kv_weight, query, kv,
     psem, own_sem, kv_sem, fr_send, fr_recv, wsend, wrecv, csend, crecv,
-    send, recv, gsend, grecv, osem, osend, orecv, qsend, qrecv, ksend, krecv,
+    send, recv, gsend, grecv, osem, qsend, qrecv, ksend, krecv,
 ):
     c = lax.axis_index("ctx")
     t = lax.axis_index("tp")
@@ -277,20 +277,8 @@
         x = rows[j].reshape(group, part).astype(f32)
         total = total + jnp.sum(x * x, axis=1, keepdims=True)
 
-    def keep(n):
-        return pltpu.make_async_copy(
-            rows.at[4 * core + n, :, pl.ds(OFF * half, OFF)], rows_out.at[core, n], osem.at[n]
-        )
-
-    def give(n):
-        return push(
-            rows.at[4 * (1 - core) + n, :, pl.ds(OFF * half, OFF)], rows_out.at[core, n],
-            osend.at[n], orecv.at[n], sibling, t,
-        )
-
-    for n in range(4):
-        keep(n).start()
-        give(n).start()
+    keep = pltpu.make_async_copy(rows.at[pl.ds(side, 4)], rows_out, osem)
+    keep.start()
 
     inverse = lax.rsqrt(total / width + 1e-06)
     for j in range(N_TP):
@@ -384,12 +372,7 @@
             push(ref, ref, ksend.at[0, 0, 0], krecv.at[e, a], sibling, t).wait_recv()
             ref = query_out.at[:, e, two]
             push(ref, ref, qsend.at[0, 0, 0], qrecv.at[e, a], sibling, t).wait_recv()
-    for n in range(4):
-        keep(n).wait()
-        push(
-            rows_out.at[1 - core, n], rows_out.at[1 - core, n], osend.at[n], orecv.at[n], sibling, t
-        ).wait_recv()
-        give(n).wait_send()
+    keep.wait()
     pltpu.make_async_copy(
         incoming.at[pl.ds(0, devices - 1)], incoming.at[pl.ds(0, devices - 1)], fr_send
     ).wait()
@@ -426,7 +409,7 @@
     return pl.pallas_call(
         intake_kernel,
         out_shape=(
-            jax.ShapeDtypeStruct((2, 4, 2, OFF, part), bf16),
+            jax.ShapeDtypeStruct((4, 2, HS, part), bf16),
             jax.ShapeDtypeStruct((2, PAIRS, 4, HALF, HS), bf16),
             jax.ShapeDtypeStruct((PAIRS, 4, OFF, HS), bf16),
         ),
@@ -457,9 +440,7 @@
             dma((N_TP,)),
             dma((N_TP,)),
             dma((N_TP,)),
-            dma((4,)),
-            dma((4,)),
-            dma((4,)),
+            dma,
             dma((2, 2, 4)),
             dma((PAIRS, 2)),
             dma((2, 2, 4)),
@@ -486,9 +467,12 @@
 
 
 def attention_kernel(
-    slot_of, query, kv_own, out_weight, out, gathered,
-    kv, q, summed, largest, total, limit, send, recv, pass_send, wsend, wrecv, own_sem,
+    slot_of, span_order, query, kv_own, out_weight, rows, out,
+    kv, q, summed, largest, limit, attended, heads, weight, product, result,
+    send, recv, pass_send, wsend, wrecv, csend, crecv, own_sem,
+    hsend, hrecv, rsend, rrecv,
 ):
+    f32 = jnp.float32
     scale = LOG2E / math.sqrt(HS)
     c = lax.axis_index("ctx")
     t = lax.axis_index("tp")
@@ -498,19 +482,23 @@
     base = pair // 4 * 4
     other = 4 - base
     z = pair % 4
-    up = lax.rem(z + 1, 4)
-    down = lax.rem(z + 3, 4)
-    far = lax.rem(z + 2, 4)
+    up, down, far = (add4(z, n) for n in (1, 3, 2))
     z_up, z_down, z_far = base + up, base + down, base + far
     x_own, x_up, x_down, x_far = other + z, other + up, other + down, other + far
-
     y = lax.rem(t, 4)
     side = t - y
+    half = t // 4
     across = 4 - side
     t_up, t_down, t_far = (side + add4(y, n) for n in (1, 3, 2))
     a_own, a_up, a_down, a_far = (across + add4(y, n) for n in (0, 1, 3, 2))
     x_next = 2 * x_own + core
-
+    depth, cols = weight.shape[2:]
+
+    def columns(of_half):
+        return out_weight.at[:, pl.ds(pl.multiple_of(cols * (2 * of_half + core), HS), cols)]
+
+    own_copy = pltpu.make_async_copy(columns(half), weight.at[core, t], own_sem)
+    own_copy.start()
     barrier = pltpu.get_barrier_semaphore()
     signal(barrier, sibling, t)
     for e in (z_up, z_down, z_far, x_own):
@@ -518,48 +506,57 @@
     signal(barrier, x_next, a_own)
     for j in (t_up, t_down, t_far):
         signal(barrier, c, j)
+    first = y == 0
+    for n in range(2):
+        origin = pair_of(pair, 4 * n + y)
+        for k in range(2):
+            for d in range(N_TP):
+                j = lax.rem(t + d, N_TP)
+                if n == 0 and d == 0:
+
+                    @pl.when(jnp.logical_not(jnp.logical_and(first, core == k)))
+                    def _():
+                        signal(barrier, 2 * origin + k, j)
+
+                else:
+                    signal(barrier, 2 * origin + k, j)
     for j in range(32):
         kv[pair, core, j * OFF : (j + 1) * OFF] = kv_own[slot_of[j]]
-    pl.semaphore_wait(barrier, 9)
-
-    cols = gathered.shape[-1]
-    quarter_rows = gathered.shape[1] // 4
-    own_weight = out_weight.at[:, pl.ds(pl.multiple_of(cols * core, HS), cols)]
+    pl.semaphore_wait(barrier, 9 + 32 - jnp.where(first, 1, 0))
 
     def quarter(ref, n):
-        return ref.at[pl.ds(quarter_rows * n, quarter_rows)]
+        return ref.at[pl.ds(depth // 4 * n, depth // 4)]
 
     def wmove(m):
-        whole = lambda g: (gathered.at[g], gathered.at[g])
-        part = lambda g: (quarter(gathered.at[g], z), quarter(gathered.at[g], z))
-        src, dst, ctx, tp = (
-            (own_weight, gathered.at[t], x_next, a_own),
-            (own_weight, gathered.at[t], c, t_up),
-            (own_weight, gathered.at[t], c, t_down),
-            (quarter(own_weight, z), quarter(gathered.at[t], z), c, t_far),
-            (*whole(a_own), c, t_up),
-            (*whole(a_own), c, t_down),
-            (*part(a_own), c, t_far),
-            (*part(t_far), 2 * z_up + core, t),
-            (*part(t_far), 2 * z_down + core, t),
-            (*part(t_far), 2 * z_far + core, t),
-            (*part(a_far), 2 * z_up + core, t),
-            (*part(a_far), 2 * z_down + core, t),
-            (*part(a_far), 2 * z_far + core, t),
-        )[m]
+        own = weight.at[core, t]
+        passed = weight.at[core, a_own]
+        if m == 0:
+            src, dst, ctx, tp = columns(1 - half), own, x_next, a_own
+        elif m < 7:
+            dst, tp = (
+                (own, t_up), (own, t_down), (quarter(own, z), t_far),
+                (passed, t_up), (passed, t_down), (quarter(passed, z), t_far),
+            )[m - 1]
+            src, ctx = dst, c
+        else:
+            n = m - 7
+            dst = quarter(weight.at[core, (t_far, a_far)[n // 3]], z)
+            src, tp, ctx = dst, t, 2 * (z_up, z_down, z_far)[n % 3] + core
         return push(src, dst, wsend.at[m], wrecv.at[m], ctx, tp)
 
     def warrive(m):
-        ref = (
-            gathered.at[a_own], gathered.at[t_down], gathered.at[t_up],
-            quarter(gathered.at[t_far], z),
-            gathered.at[a_down], gathered.at[a_up], quarter(gathered.at[a_far], z),
-            quarter(gathered.at[t_far], down), quarter(gathered.at[t_far], up),
-            quarter(gathered.at[t_far], far),
-            quarter(gathered.at[a_far], down), quarter(gathered.at[a_far], up),
-            quarter(gathered.at[a_far], far),
-        )[m]
+        if m < 7:
+            ref = weight.at[core, (a_own, t_down, t_up, t_far, a_down, a_up, a_far)[m]]
+            if m % 3 == 0 and m:
+                ref = quarter(ref, z)
+        else:
+            n = m - 7
+            ref = quarter(weight.at[core, (t_far, a_far)[n // 3]], (down, up, far)[n % 3])
         push(ref, ref, wsend.at[m], wrecv.at[m], sibling, t).wait_recv()
+
+    def give(g):
+        ref = weight.at[core, g]
+        return push(ref, ref, csend.at[g], crecv.at[g], sibling, t)
 
     def transfer(e, to, index):
         block = kv.at[e, core]
@@ -578,17 +575,16 @@
         (pair, x_own), (pair, z_up), (pair, z_down), (pair, z_far),
         (x_own, z_up), (x_own, z_down), (z_far, x_own),
     )
-    for index in range(3):
+    for index in range(4):
         transfer(*moves[index], index).start()
-    for m in (0, 3, 1, 2):
+    own_copy.wait()
+    for m in (3, 1, 2):
         wmove(m).start()
-    own_copy = pltpu.make_async_copy(own_weight, gathered.at[t], own_sem)
-    own_copy.start()
     for j in range(32):
         q[j * OFF : (j + 1) * OFF] = query[:, slot_of[j]].reshape(2 * HALF, HS)
 
-    rows = 8 * HALF
-    row = lax.broadcasted_iota(jnp.int32, (rows, 1), 0)
+    group = 8 * HALF
+    row = lax.broadcasted_iota(jnp.int32, (group, 1), 0)
     col = lax.broadcasted_iota(jnp.int32, (1, 4 * OFF), 1)
 
     def starts(index, i, e):
@@ -600,331 +596,265 @@
         return value
 
     for i in range(8):
-        limit[i * rows : (i + 1) * rows] = (
-            starts(row, i, pair) + HALF * core + row % HALF
-        )
-
-    def update(e, first):
-        for i in range(8):
+        limit[i * group : (i + 1) * group] = starts(row, i, pair) + HALF * core + row % HALF
+
+    def update(e, first_set):
+        def chunk(i):
+            return slice(i * group, (i + 1) * group), 4 * OFF * (i + 1)
+
+        def scores(i):
+            here, width = chunk(i)
+            return lax.dot_general(
+                q[here], kv[e, 0, :width], (((1,), (1,)), ((), ())), preferred_element_type=f32
+            )
+
+        def soft(i, s):
+            here, width = chunk(i)
             at = starts(col, i, e) + col % OFF
-            here = slice(i * rows, (i + 1) * rows)
-            width = 4 * OFF * (i + 1)
-            s = lax.dot_general(
-                q[here], kv[e, 0, :width], (((1,), (1,)), ((), ())),
-                preferred_element_type=jnp.float32,
-            )
             edge = jnp.where(at <= limit[here], s[:, width - 4 * OFF :], -1e30)
             s = edge if i == 0 else jnp.concatenate([s[:, : width - 4 * OFF], edge], axis=1)
             top = jnp.max(s, axis=1, keepdims=True)
-            if not first:
+            if not first_set:
                 top = jnp.maximum(top, largest[here])
-            weights = jnp.exp2((s - top) * scale)
-            added = jnp.sum(weights, axis=1, keepdims=True)
-            product = jnp.dot(
-                weights.astype(jnp.bfloat16), kv[e, 1, :width], preferred_element_type=jnp.float32
+                summed[here] = summed[here] * jnp.exp2((largest[here] - top) * scale)
+            largest[here] = top
+            return jnp.exp2((s - top) * scale).astype(jnp.bfloat16)
+
+        def gather(i, weights):
+            here, width = chunk(i)
+            beside = jnp.concatenate(
+                [kv[e, 1, :width], jnp.ones((width, HS), jnp.bfloat16)], axis=1
             )
-            if not first:
-                factor = jnp.exp2((largest[here] - top) * scale)
-                added = added + total[here] * factor
-                product = product + summed[here] * factor
-            largest[here] = top
-            total[here] = added
-            summed[here] = product
+            new = jnp.dot(weights, beside, preferred_element_type=f32)
+            summed[here] = new if first_set else summed[here] + new
+
+        s = scores(0)
+        held = None
+        for i in range(8):
+            ahead = scores(i + 1) if i < 7 else None
+            weights = soft(i, s)
+            if held is not None:
+                gather(*held)
+            held = (i, weights)
+            s = ahead
+        gather(*held)
 
     arrive(pair, 1 - core)
     update(pair, True)
-    transfer(*moves[3], 3).start()
     arrive(x_own, core)
     transfer(*moves[4], 4).start()
     transfer(*moves[5], 5).start()
     share(x_own).start()
-    arrive(z_up, core)
-    share(z_up).start()
-    arrive(z_down, core)
-    share(z_down).start()
-
-    order = (x_own, z_up, z_down, x_up, x_down, z_far, x_far)
+    wmove(0).start()
+    give(t).start()
+    order = (x_own, z_up, z_down, z_far, x_up, x_down, x_far)
 
     def step(n, unused):
         e = order[6]
         for index in range(6):
             e = jnp.where(n == index, order[index], e)
 
+        @pl.when(n == 1)
+        def _():
+            arrive(z_up, core)
+            share(z_up).start()
+            arrive(z_down, core)
+            share(z_down).start()
+
         @pl.when(n == 2)
         def _():
+            arrive(z_far, core)
+            transfer(*moves[6], 6).start()
+            share(z_far).start()
             warrive(3)
             for m in (7, 8, 9):
                 wmove(m).start()
-            arrive(x_up, core)
-            share(x_up).start()
-
-        @pl.when(n == 3)
-        def _():
-            arrive(x_down, core)
-            share(x_down).start()
-            arrive(z_far, core)
-            transfer(*moves[6], 6).start()
-            share(z_far).start()
 
         @pl.when(n == 4)
         def _():
             warrive(0)
             for m in (6, 4, 5):
                 wmove(m).start()
+            give(a_own).start()
+            arrive(x_up, core)
+            share(x_up).start()
+            arrive(x_down, core)
+            share(x_down).start()
 
         @pl.when(n == 6)
         def _():
             arrive(x_far, core)
             share(x_far).start()
+            warrive(6)
+            for m in (10, 11, 12):
+                wmove(m).start()
 
         arrive(e, 1 - core)
         update(e, False)
         return unused
 
     lax.fori_loop(0, 7, step, 0)
+
     for i in range(8):
-        here = slice(i * rows, (i + 1) * rows)
-        attended = (summed[here] / total[here]).astype(jnp.bfloat16).reshape(4, 2, HALF, HS)
+        here = slice(i * group, (i + 1) * group)
+        done = (summed[here, :HS] / summed[here, HS : HS + 1]).astype(jnp.bfloat16)
+        done = done.reshape(4, 2, HALF, HS)
         for a in range(4):
-            out[4 * i + a] = jnp.concatenate([attended[a, 0], attended[a, 1]], axis=1)
-    warrive(6)
-    for m in (10, 11, 12):
-        wmove(m).start()
+            attended[0, 4 * i + a] = jnp.concatenate([done[a, 0], done[a, 1]], axis=1)
+
+    def head_push(d, a, n):
+        e = lax.rem(pair + d, PAIRS)
+        kind = class_of(e, pair)
+        at = pl.ds(OFF * (kind // 4) + HALF * core, HALF)
+        return push(
+            attended.at[1, pl.ds(4 * e + 2 * a, 2)], heads.at[t, :, at, :], hsend.at[d, a, n],
+            hrecv.at[t, kind // 4, core], 2 * e + a, lax.rem(4 * n + lax.rem(kind, 4) + side, N_TP),
+        )
+
+    def is_here(d, a, n):
+        if d or n:
+            return jnp.bool_(False)
+        return jnp.logical_and(first, core == a)
+
+    for j in range(32):
+        attended[1, j] = attended[0, span_order[j]]
+    for d in range(PAIRS):
+        for n in range(2):
+            for a in range(2):
+                if d or n:
+                    head_push(d, a, n).start()
+                else:
+
+                    @pl.when(is_here(d, a, n))
+                    def _():
+                        pltpu.make_async_copy(
+                            attended.at[1, pl.ds(4 * pair + 2 * a, 2)],
+                            heads.at[t, :, pl.ds(HALF * core, HALF), :], hrecv.at[t, 0, core],
+                        ).start()
+
+                    @pl.when(jnp.logical_not(is_here(d, a, n)))
+                    def _():
+                        head_push(d, a, n).start()
+
     for m in (1, 2, 4, 5, 7, 8, 9, 10, 11, 12):
         warrive(m)
-    own_copy.wait()
+    for g in (t_up, t_down, t_far, a_up, a_down, a_far):
+        give(g).start()
+    for g in range(N_TP):
+        ref = weight.at[1 - core, g]
+        push(ref, ref, csend.at[g], crecv.at[g], sibling, t).wait_recv()
+    for g in range(N_TP):
+        for n in range(2):
+            for k in range(2):
+                ref = heads.at[g, :, pl.ds(OFF * n + HALF * k, HALF), :]
+                push(ref, ref, hsend.at[0, 0, 0], hrecv.at[g, n, k], sibling, t).wait_recv()
+
+    part = out.shape[-1]
+    place = pl.ds(HS * y, HS)
+
+    def send_home(n):
+        return push(
+            result.at[n], out.at[:, place, :], rsend.at[n], rrecv.at[y], c, side + n
+        )
+
+    for n in range(4):
+        if n % 2 == 0:
+            for begin, end in ((0, 4 * HS), (4 * HS, cols)):
+                total = jnp.zeros((2 * HS, end - begin), f32)
+                for g in range(N_TP):
+                    x = heads[g].reshape(2 * HS, 2 * HS)
+                    total = total + jnp.dot(
+                        x, weight[n // 2, g, :, begin:end], preferred_element_type=f32
+                    ).astype(jnp.bfloat16).astype(f32)
+                product[:, begin:end] = total
+            total = product[:, : 4 * HS][:, :part]
+        else:
+            start = part // HS * HS
+            total = product[:, start : start + 4 * HS]
+            total = pltpu.roll(total, 4 * HS - (part - start), 1)[:, :part]
+        placed = rows[n].reshape(2 * HS, part).astype(f32)
+        result[n] = (placed + total).astype(jnp.bfloat16).reshape(2, HS, part)
+
+        @pl.when(y == n)
+        def _():
+            pltpu.make_async_copy(result.at[n], out.at[:, place, :], rrecv.at[y]).start()
+
+        @pl.when(y != n)
+        def _():
+            send_home(n).start()
+
+    for n in range(4):
+        ref = out.at[:, pl.ds(HS * n, HS), :]
+        push(ref, ref, rsend.at[0], rrecv.at[n], sibling, t).wait_recv()
     for index in range(7):
         transfer(*moves[index], index).wait_send()
     for e in range(PAIRS):
         share(e).wait_send()
     for m in range(13):
         wmove(m).wait_send()
-
-
-def attention(slot_of, query, kv, out_weight):
-    anywhere = pl.BlockSpec(memory_space=pl.ANY)
-    depth, width = out_weight.shape
+    for g in range(N_TP):
+        give(g).wait_send()
+    for d in range(PAIRS):
+        for n in range(2):
+            for a in range(2):
+                if d or n:
+                    head_push(d, a, n).wait_send()
+                else:
+
+                    @pl.when(jnp.logical_not(is_here(d, a, n)))
+                    def _():
+                        head_push(d, a, n).wait_send()
+
+    for n in range(4):
+
+        @pl.when(y != n)
+        def _():
+            send_home(n).wait_send()
+
+
+def attention(slot_of, span_order, query, kv, out_weight, rows):
     vm = pl.BlockSpec(memory_space=pltpu.VMEM)
     sm = pl.BlockSpec(memory_space=pltpu.SMEM)
+    anywhere = pl.BlockSpec(memory_space=pl.ANY)
+    dma = pltpu.SemaphoreType.DMA
+    bf16 = jnp.bfloat16
     keys = 32 * OFF
+    depth, width = out_weight.shape
+    part = rows.shape[-1]
     return pl.pallas_call(
         attention_kernel,
-        out_shape=(
-            jax.ShapeDtypeStruct((32, HALF, 2 * HS), jnp.bfloat16),
-            jax.ShapeDtypeStruct((N_TP, depth, width // 2), jnp.bfloat16),
-        ),
-        in_specs=[sm, vm, vm, anywhere],
-        out_specs=(vm, anywhere),
+        out_shape=jax.ShapeDtypeStruct((2, CH, part), bf16),
+        in_specs=[sm, sm, vm, vm, anywhere, vm],
+        out_specs=vm,
         scratch_shapes=[
-            pltpu.VMEM((PAIRS, 2, keys, HS), jnp.bfloat16),
-            pltpu.VMEM((keys, HS), jnp.bfloat16),
-            pltpu.VMEM((keys, HS), jnp.float32),
-            pltpu.VMEM((keys, 1), jnp.float32),
+            pltpu.VMEM((PAIRS, 2, keys, HS), bf16),
+            pltpu.VMEM((keys, HS), bf16),
+            pltpu.VMEM((keys, 2 * HS), jnp.float32),
             pltpu.VMEM((keys, 1), jnp.float32),
             pltpu.VMEM((keys, 1), jnp.int32),
-            pltpu.SemaphoreType.DMA((7,)),
-            pltpu.SemaphoreType.DMA((PAIRS, 2)),
-            pltpu.SemaphoreType.DMA((PAIRS,)),
-            pltpu.SemaphoreType.DMA((13,)),
-            pltpu.SemaphoreType.DMA((13,)),
-            pltpu.SemaphoreType.DMA,
+            pltpu.VMEM((2, 32, HALF, 2 * HS), bf16),
+            pltpu.VMEM((N_TP, 2, HS, 2 * HS), bf16),
+            pltpu.VMEM((2, N_TP, depth, width // 4), bf16),
+            pltpu.VMEM((2 * HS, width // 4), jnp.float32),
+            pltpu.VMEM((4, 2, HS, part), bf16),
+            dma((7,)),
+            dma((PAIRS, 2)),
+            dma((PAIRS,)),
+            dma((13,)),
+            dma((13,)),
+            dma((N_TP,)),
+            dma((N_TP,)),
+            dma,
+            dma((PAIRS, 2, 2)),
+            dma((N_TP, 2, 2)),
+            dma((4,)),
+            dma((4,)),
         ],
         compiler_params=pltpu.CompilerParams(
-            collective_id=4, has_side_effects=True, vmem_limit_bytes=48 * 2**20
+            collective_id=2, has_side_effects=True, vmem_limit_bytes=52 * 2**20
         ),
         name="attention",
-    )(slot_of, query, kv, out_weight)
-
-
-def out_kernel(
-    span_order, attended, out_weight, rows, out, sorted_heads, heads, weight, product, result,
-    wsem, hsend, hrecv, fsend, frecv, rsend, rrecv,
-):
-    c = lax.axis_index("ctx")
-    t = lax.axis_index("tp")
-    pair = c // 2
-    core = c % 2
-    sibling = c + 1 - 2 * core
-    side = t // 4
-    parts = N_TP // 2
-
-    def load(g):
-        return pltpu.make_async_copy(out_weight.at[g], weight.at[g], wsem.at[g])
-
-    for g in range(N_TP):
-        load(g).start()
-
-    own = t == 0
-    home = side == core
-    origin = pair_of(pair, t)
-    barrier = pltpu.get_barrier_semaphore()
-    signal(barrier, sibling, t)
-    for d in range(N_TP):
-        j = lax.rem(t + d, N_TP)
-        if d == 0:
-
-            @pl.when(jnp.logical_not(own))
-            def _():
-                signal(barrier, 2 * origin + core, j)
-
-            @pl.when(jnp.logical_not(home))
-            def _():
-                signal(barrier, 2 * pair + side, j)
-
-        else:
-            signal(barrier, 2 * origin + core, j)
-            signal(barrier, 2 * pair + side, j)
-    for j in range(32):
-        sorted_heads[j] = attended[span_order[j]]
-    pl.semaphore_wait(
-        barrier, 1 + PAIRS - jnp.where(own, 1, 0) + 2 * parts - jnp.where(home, 1, 0)
-    )
-
-    mine = pl.ds(core * HALF, HALF)
-    theirs = pl.ds((1 - core) * HALF, HALF)
-
-    def gather(d):
-        e = lax.rem(pair + d, PAIRS)
-        return push(
-            sorted_heads.at[pl.ds(4 * e, 4)], heads.at[t, :, mine, :], hsend.at[d], hrecv.at[t],
-            2 * e + core, class_of(e, pair),
-        )
-
-    @pl.when(own)
-    def _():
-        pltpu.make_async_copy(
-            sorted_heads.at[pl.ds(4 * pair, 4)], heads.at[t, :, mine, :], hrecv.at[t]
-        ).start()
-
-    @pl.when(jnp.logical_not(own))
-    def _():
-        gather(0).start()
-
-    for d in range(1, PAIRS):
-        gather(d).start()
-
-    def forward(j):
-        return push(
-            heads.at[j, :, mine, :], heads.at[j, :, mine, :], fsend.at[j], frecv.at[j], sibling, t
-        )
-
-    for d in range(N_TP):
-        j = lax.rem(t + d, N_TP)
-        push(
-            heads.at[j, :, mine, :], heads.at[j, :, mine, :], hsend.at[0], hrecv.at[j], sibling, t
-        ).wait_recv()
-        forward(j).start()
-    for j in range(N_TP):
-        push(
-            heads.at[j, :, theirs, :], heads.at[j, :, theirs, :], fsend.at[j], frecv.at[j],
-            sibling, t,
-        ).wait_recv()
-    for g in range(N_TP):
-        load(g).wait()
-
-    part = out.shape[-1]
-
-    place = HS * lax.rem(t, 4) + OFF * side
-
-    def send_home(j, a):
-        return push(
-            result.at[j, a], out.at[:, pl.ds(place, OFF), :], rsend.at[j, a], rrecv.at[t],
-            2 * pair + a, parts * core + j,
-        )
-
-    def is_home(j, a):
-        return jnp.logical_and(home, jnp.logical_and(a == core, parts * core + j == t))
-
-    block = 2 * HS
-
-    def project(n):
-        total = jnp.zeros((4 * OFF, block), jnp.float32)
-        for g in range(N_TP):
-            x = heads[g].reshape(4 * OFF, 2 * HS)
-            total = total + jnp.dot(
-                x, weight[g, :, n * block : (n + 1) * block], preferred_element_type=jnp.float32
-            ).astype(jnp.bfloat16).astype(jnp.float32)
-        product[:, n * block : (n + 1) * block] = total
-
-    ready = 0
-    for j in range(parts):
-        while ready * block < (j + 1) * part:
-            project(ready)
-            ready += 1
-        start = j * part // HS * HS
-        shift = j * part - start
-        window = -(-(part + shift) // HS) * HS
-        total = product[:, start : start + window]
-        if shift:
-            total = pltpu.roll(total, window - shift, 1)
-        total = total[:, :part]
-        for a in range(2):
-            placed = rows[a, j].reshape(2 * OFF, part).astype(jnp.float32)
-            result[j, a] = (placed + total[a * 2 * OFF : (a + 1) * 2 * OFF]).astype(
-                jnp.bfloat16
-            ).reshape(2, OFF, part)
-
-            @pl.when(is_home(j, a))
-            def _():
-                pltpu.make_async_copy(
-                    result.at[j, a], out.at[:, pl.ds(place, OFF), :], rrecv.at[t]
-                ).start()
-
-            @pl.when(jnp.logical_not(is_home(j, a)))
-            def _():
-                send_home(j, a).start()
-
-    for e in range(PAIRS):
-        push(
-            result.at[0, 0], out.at[:, pl.ds(OFF * e, OFF), :], rsend.at[0, 0], rrecv.at[e],
-            sibling, t,
-        ).wait_recv()
-
-    @pl.when(jnp.logical_not(own))
-    def _():
-        gather(0).wait_send()
-
-    for d in range(1, PAIRS):
-        gather(d).wait_send()
-    for j in range(N_TP):
-        forward(j).wait_send()
-    for j in range(parts):
-        for a in range(2):
-
-            @pl.when(jnp.logical_not(is_home(j, a)))
-            def _():
-                send_home(j, a).wait_send()
-
-
-def out_exchange(span_order, attended, out_weight, rows):
-    part = rows.shape[-1]
-    parts = N_TP // 2
-    vm = pl.BlockSpec(memory_space=pltpu.VMEM)
-    anywhere = pl.BlockSpec(memory_space=pl.ANY)
-    return pl.pallas_call(
-        out_kernel,
-        out_shape=jax.ShapeDtypeStruct((2, CH, part), jnp.bfloat16),
-        in_specs=[pl.BlockSpec(memory_space=pltpu.SMEM), vm, anywhere, vm],
-        out_specs=vm,
-        scratch_shapes=[
-            pltpu.VMEM((32, HALF, 2 * HS), jnp.bfloat16),
-            pltpu.VMEM((N_TP, 4, OFF, 2 * HS), jnp.bfloat16),
-            pltpu.VMEM(out_weight.shape, jnp.bfloat16),
-            pltpu.VMEM((4 * OFF, parts * part), jnp.float32),
-            pltpu.VMEM((parts, 2, 2, OFF, part), jnp.bfloat16),
-            pltpu.SemaphoreType.DMA((N_TP,)),
-            pltpu.SemaphoreType.DMA((N_TP,)),
-            pltpu.SemaphoreType.DMA((N_TP,)),
-            pltpu.SemaphoreType.DMA((N_TP,)),
-            pltpu.SemaphoreType.DMA((N_TP,)),
-            pltpu.SemaphoreType.DMA((parts, 2)),
-            pltpu.SemaphoreType.DMA((PAIRS,)),
-        ],
-        compiler_params=pltpu.CompilerParams(
-            collective_id=3, has_side_effects=True, vmem_limit_bytes=40 * 2**20
-        ),
-        name="out",
-    )(span_order, attended, out_weight, rows)
+    )(slot_of, span_order, query, kv, out_weight, rows)
 
 
 def per_device(
@@ -962,10 +892,10 @@
         text_embed, norm_gain, frame_features, frame_positions, span_order, (cosine, sine),
         projector, query_weight, key_weight, value_weight,
     )
-    attended, gathered = attention(
-        slot_of, query.reshape(2, 32, HALF, HS), kv.reshape(32, OFF, HS), out_weight
+    mixed = attention(
+        slot_of, span_order, query.reshape(2, 32, HALF, HS), kv.reshape(32, OFF, HS),
+        out_weight, rows,
     )
-    mixed = out_exchange(span_order, attended, gathered, rows)
     return mixed.reshape(tok_rows, part)
 
 

time: 233 us -> 205 us (0.88)
  Pallas kernels: 220 us -> 193 us
    pallas_call x3 -> x2, Pallas kernels: 220 us -> 193 us  [the longest x1 105 us: attention(): pl.pallas_call(attention_kernel, out_shape=jax.ShapeDtypeStruct((2, CH, p...]
    unnamed x15 -> x13, local copies, waits for them, and re-layouts: 6.77 us -> 4.66 us
where the time goes in v6:
time: 205 us; the launch traced here: 204 us
  Pallas kernels  193 us (94%)
  local copies, waits for them, and re-layouts  9.04 us (4%)
    pallas_call x1, Pallas kernels, attention(): pl.pallas_call(attention_kernel, out_shape=jax.ShapeDtypeStruct((2, CH, p...  105 us
    pallas_call x1, Pallas kernels, intake(): pl.pallas_call(intake_kernel, out_shape=(jax.ShapeDtypeStruct((4, 2, HS,...  87.4 us
    unnamed x13, local copies, waits for them, and re-layouts  4.66 us

profile of v6, /device:TPU:29, one launch (start us, length us, event | category | flops | bytes accessed | tf_op | source)
XLA Modules:
  0.0 203.7 jit_solution(2687815172883580564)
XLA Ops:
  0.0 0.0 copy-start
  0.0 0.9 multiply_add_fusion
  0.9 0.1 convert_bitcast_fusion
  1.0 0.5 fusion
  1.5 0.1 pad_maximum_fusion
  1.6 1.5 copy.15
  3.1 0.7 copy.16.pos_col
  3.9 0.7 broadcast_in_dim.18.gain
  4.5 0.7 copy.17.order_col
  5.3 0.0 copy-done
  5.3 0.0 copy-start.2
  5.3 0.9 copy-done.2
  6.2 0.0 copy-start.3
  6.2 0.7 copy-done.3
  6.8 0.0 copy-start.5
  6.9 0.7 copy-done.5
  7.5 0.0 copy-start.4
  7.5 87.4 %intake.1 = (bf16[4,2,128,448]{3,2,1,0:T(8,128)(2,1)S(1)}, bf16[2,8,4,32,128]{4,3,2,1,0:T(8,128)(2,1)S(1)}, bf16[8,4,64,128]{3,2,1,0:T(8,128)(2,1)S(1)}) custom-call(bf16[2,4,128,448]{3,2,1,0:T(8,128)(2,1)S(1)} %bitcast.10, bf16[16,448]{1,0:T(8,128)(2,1)S(1)} %broadcast_in_dim.18.gain, bf16[64,1152]{1,0:T(8,128)(2,1)S(1)} %copy-done.2, ...), custom_call_target="tpu_custom_call" | custom-call | tf_op jit(solution)/shard_map/intake/pallas_call | solution.py:409
  95.0 0.0 copy-start.1
  95.0 1.0 copy-done.1
  95.9 0.1 select_reduce_fusion.slot_of
  96.0 0.0 copy-done.4
  96.0 105.4 %attention.1 = bf16[2,512,448]{2,1,0:T(8,128)(2,1)} custom-call(s32[32]{0:T(128)S(1)} %select_reduce_fusion.slot_of, s32[32]{0:T(128)S(1)} %copy-done.4, bf16[2,32,32,128]{3,2,1,0:T(8,128)(2,1)S(1)} %bitcast.11, bf16[32,64,128]{2,1,0:T(8,128)(2,1)S(1)} %bitcast.12, bf16[256,3584]{1,0:T(8,128)(2,1)} %out_weight.1, bf16[4,2,128,448]{3,2,1,0:T(8,128)(2,1)} %copy-done.1), custom_call_target="tpu_custom_call" | custom-call | tf_op jit(solution)/shard_map/attention/pallas_call | solution.py:824
  201.5 2.2 %copy.18 = bf16[1024,448]{0,1:T(8,128)(2,1)} copy(bf16[1024,448]{1,0:T(8,128)(2,1)} %bitcast.17) | data formatting | bytes 1835008 | tf_op jit(solution)/shard_map/reshape | solution.py:899
  (1 shorter events, 0.0 us)
Async XLA Ops:
  0.0 5.3 %copy-start = (bf16[3584,256]{1,0:T(8,128)(2,1)S(1)}, bf16[3584,256]{1,0:T(8,128)(2,1)}, u32[]{:S(2)}) copy-start(bf16[3584,256]{1,0:T(8,128)(2,1)} %query_weight.1) | copy-start | bytes 5505028
  5.3 0.9 copy-start.2
  6.2 0.7 copy-start.3
  6.8 0.7 copy-start.5
  7.5 88.5 %copy-start.4 = (s32[32]{0:T(128)S(1)}, s32[32]{0:T(128)}, u32[]{:S(2)}) copy-start(s32[32]{0:T(128)} %span_order.1) | copy-start | bytes 388
  95.0 1.0 copy-start.1

commit v7 on v6

--- a/solution.py
+++ b/solution.py
@@ -37,19 +37,21 @@
 
 
 def pair_of(e, t):
-    return lax.rem(e // 4 + t // 4, 2) * 4 + add4(lax.rem(e, 4), lax.rem(t, 4))
+    x = lax.rem(e // 4 + t // 4, 2)
+    return x * 4 + lax.rem(lax.rem(e, 4) + lax.rem(t, 4) + 2 * x, 4)
 
 
 def class_of(e, pair):
-    return lax.rem(e // 4 + pair // 4, 2) * 4 + add4(lax.rem(pair, 4), -lax.rem(e, 4))
+    x = pair // 4
+    return lax.rem(e // 4 + x, 2) * 4 + lax.rem(lax.rem(pair, 4) - lax.rem(e, 4) + 2 * x + 4, 4)
 
 
 def intake_kernel(
-    text, gain, features, pos_row, pos_col, order_row, order_col, cosine, sine,
-    projector, query_weight, key_weight, value_weight,
+    norm_gain, pos_row, order_row, cosine, sine,
+    text, frame_features, projector, query_weight, key_weight, value_weight,
     rows_out, query_out, kv_out,
-    pweight, outgoing, incoming, placed, rows, gains, normed, weight, kv_weight, query, kv,
-    psem, own_sem, kv_sem, fr_send, fr_recv, wsend, wrecv, csend, crecv,
+    features, gain, pweight, outgoing, incoming, placed, rows, gains, normed, weight, kv_weight, query, kv,
+    tsem, psem, own_sem, kv_sem, fr_send, fr_recv, wsend, wrecv, csend, crecv,
     send, recv, gsend, grecv, osem, qsend, qrecv, ksend, krecv,
 ):
     c = lax.axis_index("ctx")
@@ -74,6 +76,9 @@
     )
     own_copy.start()
     block = 4 * HS
+    take_features = pltpu.make_async_copy(frame_features, features, tsem.at[0])
+    take_features.start()
+    take_text = pltpu.make_async_copy(text, placed, tsem.at[1])
 
     def load(d):
         j = lax.rem(t + d, N_TP)
@@ -89,6 +94,7 @@
         pltpu.make_async_copy(ref.at[:, kv_cols], kv_weight.at[n], kv_sem.at[n])
         for n, ref in enumerate((key_weight, value_weight))
     ]
+    take_text.start()
     for one in kv_loads:
         one.start()
 
@@ -102,29 +108,35 @@
     lax.fori_loop(1, devices, greet, 0)
 
     f32 = jnp.float32
+    gain[...] = jnp.broadcast_to(norm_gain[...], gain.shape)
     spans = order_row.shape[1]
     tokens = pos_row.shape[1]
     entries = N_CTX * CAP
+
+    def turned(x):
+        size = x.shape[1]
+        same = lax.broadcasted_iota(jnp.int32, (size, size), 0) == lax.broadcasted_iota(
+            jnp.int32, (size, size), 1
+        )
+        return jnp.sum(jnp.where(same, x, 0.0), axis=1, keepdims=True)
+
+    order_col = turned(order_row[...].astype(f32))
     slot_row = jnp.sum(
         jnp.where(
-            order_col[...] == pos_row[...] // CH,
+            order_col == (pos_row[...] // CH).astype(f32),
             lax.broadcasted_iota(jnp.int32, (spans, tokens), 0).astype(f32), 0.0,
         ),
         axis=0, keepdims=True,
-    ).astype(jnp.int32)
-    slot_col = jnp.sum(
-        jnp.where(
-            order_row[...] == pos_col[...] // CH,
-            lax.broadcasted_iota(jnp.int32, (tokens, spans), 1).astype(f32), 0.0,
-        ),
-        axis=1, keepdims=True,
-    ).astype(jnp.int32)
+    )
+    slot_col = turned(slot_row).astype(jnp.int32)
+    slot_row = slot_row.astype(jnp.int32)
     first = lax.broadcasted_iota(jnp.int32, (tokens, tokens), 0)
     second = lax.broadcasted_iota(jnp.int32, (tokens, tokens), 1)
     earlier = jnp.logical_and(slot_col // 2 == slot_row // 2, first < second)
     place = jnp.sum(jnp.where(earlier, 1.0, 0.0), axis=0, keepdims=True).astype(jnp.int32)
     entry = slot_row // 2 * CAP + place
     chosen = lax.broadcasted_iota(jnp.int32, (entries, tokens), 0) == entry
+    take_features.wait()
     ordered = jnp.dot(
         jnp.where(chosen, 1.0, 0.0).astype(jnp.bfloat16), features[...],
         preferred_element_type=f32,
@@ -140,38 +152,25 @@
     pl.semaphore_wait(barrier, devices - 1)
 
     depth = weight.shape[2]
-    direct = pl.ds(0, depth // 2)
-
-    def eighth(n):
-        return pl.ds(depth // 2 + depth // 8 * n, depth // 8)
 
     def quarter(n):
         return pl.ds(depth // 4 * n, depth // 4)
 
     def wmove(m):
-        if m < 5:
-            cut, tp = (
-                (direct, y_up), (direct, y_down), (eighth(z), y_up), (eighth(z), y_down),
-                (quarter(z), y_far),
-            )[m]
-            ref, ctx, tp = weight.at[core, y, cut], c, side + tp
+        n = m - 3
+        shard = y if m < 3 else (y_up, y_down, y_far)[n // 3]
+        ref = weight.at[core, shard, quarter(z)]
+        if m < 3:
+            ctx, tp = c, side + (y_up, y_down, y_far)[m]
         else:
-            n = m - 5
-            cut = quarter(z) if n // 3 == 2 else eighth(z)
-            ref, tp = weight.at[core, (y_up, y_down, y_far)[n // 3], cut], t
-            ctx = 2 * (z_up, z_down, z_far)[n % 3] + core
+            ctx, tp = 2 * (z_up, z_down, z_far)[n % 3] + core, t
         return push(ref, ref, wsend.at[m], wrecv.at[m], ctx, tp)
 
     def warrive(m):
-        if m < 5:
-            shard = (y_down, y_up, y_down, y_up, y_far)[m]
-            cut = (direct, direct, eighth(z), eighth(z), quarter(z))[m]
-        else:
-            n = m - 5
-            shard = (y_up, y_down, y_far)[n // 3]
-            origin = (add4(z, 3), add4(z, 1), add4(z, 2))[n % 3]
-            cut = quarter(origin) if n // 3 == 2 else eighth(origin)
-        ref = weight.at[core, shard, cut]
+        n = m - 3
+        shard = (y_down, y_up, y_far)[m] if m < 3 else (y_up, y_down, y_far)[n // 3]
+        origin = z if m < 3 else add4(z, (3, 1, 2)[n % 3])
+        ref = weight.at[core, shard, quarter(origin)]
         push(ref, ref, wsend.at[m], wrecv.at[m], sibling, t).wait_recv()
 
     def share(n):
@@ -183,7 +182,7 @@
         push(ref, ref, csend.at[n], crecv.at[n], sibling, t).wait_recv()
 
     own_copy.wait()
-    for m in (4, 2, 3, 0, 1):
+    for m in (2, 0, 1):
         wmove(m).start()
     share(0).start()
 
@@ -210,11 +209,12 @@
         else:
             push(outgoing.at[d, c], incoming.at[me], fr_send, fr_recv, c, j).start()
         lax.fori_loop(1, N_CTX, deliver, 0)
-
-    for m in (2, 3, 4):
-        warrive(m)
-    for m in range(5, 14):
-        wmove(m).start()
+        if d == 4:
+            for m in range(3):
+                warrive(m)
+            for m in range(3, 12):
+                wmove(m).start()
+
     pltpu.make_async_copy(incoming, incoming, fr_recv).wait()
 
     def row_block(n, across):
@@ -240,6 +240,7 @@
     left = left.astype(jnp.bfloat16)
     right = right.astype(jnp.bfloat16)
     group = 2 * HS
+    take_text.wait()
     offset = lax.broadcasted_iota(jnp.int32, (group, 1), 0)
     offset = offset // HS * CH + offset % HS
     for n in range(4):
@@ -249,7 +250,7 @@
         new_left = jnp.dot(hit, left, preferred_element_type=f32)
         new_right = jnp.dot(hit, right, preferred_element_type=f32)
         framed = new_right[:, 2 * HS - 1 :] > 0.5
-        old = text[:, j].reshape(group, part).astype(f32)
+        old = placed[:, j].reshape(group, part).astype(f32)
         placed[:, j, :, : 2 * HS] = (
             jnp.where(framed, new_left, old[:, : 2 * HS]).astype(jnp.bfloat16)
         ).reshape(2, HS, 2 * HS)
@@ -262,7 +263,7 @@
         else:
             row_block(n, 0).start()
 
-    for m in (0, 1, *range(5, 14)):
+    for m in range(3, 12):
         warrive(m)
     for n in range(1, 4):
         share(n).start()
@@ -376,7 +377,7 @@
     pltpu.make_async_copy(
         incoming.at[pl.ds(0, devices - 1)], incoming.at[pl.ds(0, devices - 1)], fr_send
     ).wait()
-    for m in range(14):
+    for m in range(12):
         wmove(m).wait_send()
     for n in range(4):
         share(n).wait_send()
@@ -413,9 +414,11 @@
             jax.ShapeDtypeStruct((2, PAIRS, 4, HALF, HS), bf16),
             jax.ShapeDtypeStruct((PAIRS, 4, OFF, HS), bf16),
         ),
-        in_specs=[vm] * 9 + [anywhere] * 4,
+        in_specs=[vm] * 5 + [anywhere] * 6,
         out_specs=(vm, vm, vm),
         scratch_shapes=[
+            pltpu.VMEM(frame_features.shape, bf16),
+            pltpu.VMEM((16, part), bf16),
             pltpu.VMEM((N_TP, projector.shape[0], 4 * HS), bf16),
             pltpu.VMEM((N_TP, N_CTX, 2 * CAP, 2 * HS), bf16),
             pltpu.VMEM((devices, 2 * CAP, 2 * HS), bf16),
@@ -427,13 +430,14 @@
             pltpu.VMEM((2, depth, 2 * HS), bf16),
             pltpu.VMEM((4, 2, 2, HS, HS), bf16),
             pltpu.VMEM((2, 2, 2, HS, HS), bf16),
+            dma((2,)),
             dma((N_TP,)),
             dma,
             dma((2,)),
             dma,
             dma,
-            dma((14,)),
-            dma((14,)),
+            dma((12,)),
+            dma((12,)),
             dma((4,)),
             dma((4,)),
             dma((4, 2)),
@@ -447,18 +451,16 @@
             dma((PAIRS, 2)),
         ],
         compiler_params=pltpu.CompilerParams(
-            collective_id=1, has_side_effects=True, vmem_limit_bytes=48 * 2**20
+            collective_id=1, has_side_effects=True, vmem_limit_bytes=56 * 2**20
         ),
         name="intake",
     )(
+        norm_gain.reshape(1, part),
+        frame_positions.reshape(1, -1),
+        span_order.reshape(1, -1),
+        *tables,
         text_embed.reshape(2, 4, HS, part),
-        jnp.broadcast_to(norm_gain[None, :], (16, part)),
         frame_features,
-        frame_positions.reshape(1, -1),
-        frame_positions.reshape(-1, 1),
-        span_order.reshape(1, -1),
-        span_order.reshape(-1, 1),
-        *tables,
         projector,
         query_weight,
         key_weight,
@@ -506,7 +508,7 @@
     signal(barrier, x_next, a_own)
     for j in (t_up, t_down, t_far):
         signal(barrier, c, j)
-    first = y == 0
+    first = y == 2 * (pair // 4)
     for n in range(2):
         origin = pair_of(pair, 4 * n + y)
         for k in range(2):
@@ -575,7 +577,7 @@
         (pair, x_own), (pair, z_up), (pair, z_down), (pair, z_far),
         (x_own, z_up), (x_own, z_down), (z_far, x_own),
     )
-    for index in range(4):
+    for index in range(3):
         transfer(*moves[index], index).start()
     own_copy.wait()
     for m in (3, 1, 2):
@@ -642,9 +644,10 @@
     arrive(pair, 1 - core)
     update(pair, True)
     arrive(x_own, core)
-    transfer(*moves[4], 4).start()
-    transfer(*moves[5], 5).start()
     share(x_own).start()
+    transfer(*moves[1], 1).wait_send()
+    transfer(*moves[2], 2).wait_send()
+    transfer(*moves[3], 3).start()
     wmove(0).start()
     give(t).start()
     order = (x_own, z_up, z_down, z_far, x_up, x_down, x_far)
@@ -663,6 +666,9 @@
 
         @pl.when(n == 2)
         def _():
+            transfer(*moves[3], 3).wait_send()
+            transfer(*moves[4], 4).start()
+            transfer(*moves[5], 5).start()
             arrive(z_far, core)
             transfer(*moves[6], 6).start()
             share(z_far).start()
@@ -786,7 +792,7 @@
     for n in range(4):
         ref = out.at[:, pl.ds(HS * n, HS), :]
         push(ref, ref, rsend.at[0], rrecv.at[n], sibling, t).wait_recv()
-    for index in range(7):
+    for index in (0, 4, 5, 6):
         transfer(*moves[index], index).wait_send()
     for e in range(PAIRS):
         share(e).wait_send()

time: 205 us -> 200 us (0.976)
  the two profiles are of different devices: /device:TPU:29 before, /device:TPU:22 now
where the time goes in v7:
time: 200 us
  Pallas kernels  190 us (95%)
  local copies, waits for them, and re-layouts  7.8 us (4%)
  other arithmetic  2.29 us (1%)
    pallas_call x1, Pallas kernels, attention(): pl.pallas_call(attention_kernel, out_shape=jax.ShapeDtypeStruct((2, CH, p...  103 us
    pallas_call x1, Pallas kernels, intake(): pl.pallas_call(intake_kernel, out_shape=(jax.ShapeDtypeStruct((4, 2, HS,...  86.7 us
    unnamed x7, local copies, waits for them, and re-layouts  4.33 us

profile of v7, /device:TPU:22, one launch (start us, length us, event | category | flops | bytes accessed | tf_op | source)
XLA Modules:
  0.0 200.0 jit_solution(9724445078425934489)
XLA Ops:
  0.0 0.7 multiply_add_fusion
  0.7 0.1 convert_bitcast_fusion
  0.8 0.5 fusion
  1.4 0.8 pad_maximum_fusion
  2.2 2.2 %copy.13 = bf16[1024,448]{1,0:T(8,128)(2,1)} copy(bf16[1024,448]{0,1:T(8,128)(2,1)} %param.10) | data formatting | bytes 1835008 | tf_op args[0]
  4.4 1.3 reshape.44.norm_gain
  5.7 0.0 copy-start.2
  5.7 86.7 %intake.1 = (bf16[4,2,128,448]{3,2,1,0:T(8,128)(2,1)}, bf16[2,8,4,32,128]{4,3,2,1,0:T(8,128)(2,1)}, bf16[8,4,64,128]{3,2,1,0:T(8,128)(2,1)}) custom-call(bf16[1,448]{1,0:T(2,128)(2,1)} %reshape.44.norm_gain, s32[1,64]{1,0:T(1,128)} %bitcast.13, s32[1,32]{1,0:T(1,128)} %bitcast.10, f32[256,128]{1,0:T(8,128)} %get-tuple-element.14.cosine, ...), custom_call_target="tpu_custom_call" | custom-call | tf_op jit(solution)/shard_map/intake/pallas_call | solution.py:410
  92.4 0.0 copy-done.2
  92.4 0.1 select_reduce_fusion.slot_of
  92.5 0.0 copy-start
  92.5 1.0 copy-done
  93.5 0.0 copy-start.1
  93.5 1.0 copy-done.1
  94.6 103.2 %attention.1 = bf16[2,512,448]{2,1,0:T(8,128)(2,1)} custom-call(s32[32]{0:T(128)S(1)} %select_reduce_fusion.slot_of, s32[32]{0:T(128)S(1)} %copy-done.2, bf16[2,32,32,128]{3,2,1,0:T(8,128)(2,1)S(1)} %bitcast.8, bf16[32,64,128]{2,1,0:T(8,128)(2,1)S(1)} %bitcast.9, bf16[256,3584]{1,0:T(8,128)(2,1)} %out_weight.1, bf16[4,2,128,448]{3,2,1,0:T(8,128)(2,1)} %get-tuple-element.10.rows), custom_call_target="tpu_custom_call" | custom-call | tf_op jit(solution)/shard_map/attention/pallas_call | solution.py:830
  197.8 2.2 %copy.14 = bf16[1024,448]{0,1:T(8,128)(2,1)} copy(bf16[1024,448]{1,0:T(8,128)(2,1)} %bitcast.12) | data formatting | bytes 1835008 | tf_op jit(solution)/shard_map/reshape | solution.py:905
  (1 shorter events, 0.0 us)
Async XLA Ops:
  5.7 86.7 %copy-start.2 = (s32[32]{0:T(128)S(1)}, s32[32]{0:T(128)}, u32[]{:S(2)}) copy-start(s32[32]{0:T(128)} %span_order.1) | copy-start | bytes 388
  92.5 1.0 copy-start
  93.5 1.0 copy-start.1

commit v8 on v7

--- a/solution.py
+++ b/solution.py
@@ -47,10 +47,10 @@
 
 
 def intake_kernel(
-    norm_gain, pos_row, order_row, cosine, sine,
+    gain, pos_row, order_row, cosine, sine,
     text, frame_features, projector, query_weight, key_weight, value_weight,
     rows_out, query_out, kv_out,
-    features, gain, pweight, outgoing, incoming, placed, rows, gains, normed, weight, kv_weight, query, kv,
+    features, turned_text, pweight, outgoing, incoming, placed, rows, gains, normed, weight, kv_weight, query, kv,
     tsem, psem, own_sem, kv_sem, fr_send, fr_recv, wsend, wrecv, csend, crecv,
     send, recv, gsend, grecv, osem, qsend, qrecv, ksend, krecv,
 ):
@@ -61,7 +61,7 @@
     sibling = c + 1 - 2 * core
     devices = N_CTX * N_TP
     me = c * N_TP + t
-    part = text.shape[-1]
+    part = text.shape[0]
     width = N_TP * part
     base = pair // 4 * 4
     z = pair % 4
@@ -78,7 +78,7 @@
     block = 4 * HS
     take_features = pltpu.make_async_copy(frame_features, features, tsem.at[0])
     take_features.start()
-    take_text = pltpu.make_async_copy(text, placed, tsem.at[1])
+    take_text = pltpu.make_async_copy(text, turned_text, tsem.at[1])
 
     def load(d):
         j = lax.rem(t + d, N_TP)
@@ -108,7 +108,6 @@
     lax.fori_loop(1, devices, greet, 0)
 
     f32 = jnp.float32
-    gain[...] = jnp.broadcast_to(norm_gain[...], gain.shape)
     spans = order_row.shape[1]
     tokens = pos_row.shape[1]
     entries = N_CTX * CAP
@@ -215,6 +214,13 @@
             for m in range(3, 12):
                 wmove(m).start()
 
+    take_text.wait()
+    for a in range(2):
+        for n in range(4):
+            block_cols = slice((4 * a + n) * HS, (4 * a + n + 1) * HS)
+            placed[a, n] = jnp.transpose(turned_text[:, block_cols].astype(f32)).astype(
+                jnp.bfloat16
+            )
     pltpu.make_async_copy(incoming, incoming, fr_recv).wait()
 
     def row_block(n, across):
@@ -240,7 +246,6 @@
     left = left.astype(jnp.bfloat16)
     right = right.astype(jnp.bfloat16)
     group = 2 * HS
-    take_text.wait()
     offset = lax.broadcasted_iota(jnp.int32, (group, 1), 0)
     offset = offset // HS * CH + offset % HS
     for n in range(4):
@@ -263,10 +268,6 @@
         else:
             row_block(n, 0).start()
 
-    for m in range(3, 12):
-        warrive(m)
-    for n in range(1, 4):
-        share(n).start()
     for one in kv_loads:
         one.wait()
 
@@ -281,6 +282,10 @@
     keep = pltpu.make_async_copy(rows.at[pl.ds(side, 4)], rows_out, osem)
     keep.start()
 
+    for m in range(3, 12):
+        warrive(m)
+    for n in range(1, 4):
+        share(n).start()
     inverse = lax.rsqrt(total / width + 1e-06)
     for j in range(N_TP):
         x = rows[j].reshape(group, part).astype(f32)
@@ -418,7 +423,7 @@
         out_specs=(vm, vm, vm),
         scratch_shapes=[
             pltpu.VMEM(frame_features.shape, bf16),
-            pltpu.VMEM((16, part), bf16),
+            pltpu.VMEM((part, tok_rows), bf16),
             pltpu.VMEM((N_TP, projector.shape[0], 4 * HS), bf16),
             pltpu.VMEM((N_TP, N_CTX, 2 * CAP, 2 * HS), bf16),
             pltpu.VMEM((devices, 2 * CAP, 2 * HS), bf16),
@@ -455,11 +460,11 @@
         ),
         name="intake",
     )(
-        norm_gain.reshape(1, part),
+        jnp.broadcast_to(norm_gain[None, :], (16, part)),
         frame_positions.reshape(1, -1),
         span_order.reshape(1, -1),
         *tables,
-        text_embed.reshape(2, 4, HS, part),
+        text_embed.T,
         frame_features,
         projector,
         query_weight,
@@ -469,9 +474,9 @@
 
 
 def attention_kernel(
-    slot_of, span_order, query, kv_own, out_weight, rows, out,
-    kv, q, summed, largest, limit, attended, heads, weight, product, result,
-    send, recv, pass_send, wsend, wrecv, csend, crecv, own_sem,
+    slot_of, span_order, query_in, kv_in, out_weight, rows_in, out,
+    query, kv_own, rows, kv, q, summed, largest, limit, attended, heads, weight, product, result,
+    isem, send, recv, pass_send, wsend, wrecv, csend, crecv, own_sem,
     hsend, hrecv, rsend, rrecv,
 ):
     f32 = jnp.float32
@@ -499,8 +504,15 @@
     def columns(of_half):
         return out_weight.at[:, pl.ds(pl.multiple_of(cols * (2 * of_half + core), HS), cols)]
 
+    take_kv, take_query, take_rows = (
+        pltpu.make_async_copy(src, dst, isem.at[n])
+        for n, (src, dst) in enumerate(((kv_in, kv_own), (query_in, query), (rows_in, rows)))
+    )
+    take_kv.start()
+    take_query.start()
     own_copy = pltpu.make_async_copy(columns(half), weight.at[core, t], own_sem)
     own_copy.start()
+    take_rows.start()
     barrier = pltpu.get_barrier_semaphore()
     signal(barrier, sibling, t)
     for e in (z_up, z_down, z_far, x_own):
@@ -522,38 +534,23 @@
 
                 else:
                     signal(barrier, 2 * origin + k, j)
+    take_kv.wait()
     for j in range(32):
         kv[pair, core, j * OFF : (j + 1) * OFF] = kv_own[slot_of[j]]
     pl.semaphore_wait(barrier, 9 + 32 - jnp.where(first, 1, 0))
-
-    def quarter(ref, n):
-        return ref.at[pl.ds(depth // 4 * n, depth // 4)]
 
     def wmove(m):
         own = weight.at[core, t]
         passed = weight.at[core, a_own]
         if m == 0:
             src, dst, ctx, tp = columns(1 - half), own, x_next, a_own
-        elif m < 7:
-            dst, tp = (
-                (own, t_up), (own, t_down), (quarter(own, z), t_far),
-                (passed, t_up), (passed, t_down), (quarter(passed, z), t_far),
-            )[m - 1]
-            src, ctx = dst, c
         else:
-            n = m - 7
-            dst = quarter(weight.at[core, (t_far, a_far)[n // 3]], z)
-            src, tp, ctx = dst, t, 2 * (z_up, z_down, z_far)[n % 3] + core
+            src = dst = own if m < 4 else passed
+            ctx, tp = c, (t_up, t_down, t_far)[(m - 1) % 3]
         return push(src, dst, wsend.at[m], wrecv.at[m], ctx, tp)
 
     def warrive(m):
-        if m < 7:
-            ref = weight.at[core, (a_own, t_down, t_up, t_far, a_down, a_up, a_far)[m]]
-            if m % 3 == 0 and m:
-                ref = quarter(ref, z)
-        else:
-            n = m - 7
-            ref = quarter(weight.at[core, (t_far, a_far)[n // 3]], (down, up, far)[n % 3])
+        ref = weight.at[core, (a_own, t_down, t_up, t_far, a_down, a_up, a_far)[m]]
         push(ref, ref, wsend.at[m], wrecv.at[m], sibling, t).wait_recv()
 
     def give(g):
@@ -580,8 +577,9 @@
     for index in range(3):
         transfer(*moves[index], index).start()
     own_copy.wait()
-    for m in (3, 1, 2):
+    for m in (1, 2, 3):
         wmove(m).start()
+    take_query.wait()
     for j in range(32):
         q[j * OFF : (j + 1) * OFF] = query[:, slot_of[j]].reshape(2 * HALF, HS)
 
@@ -672,14 +670,11 @@
             arrive(z_far, core)
             transfer(*moves[6], 6).start()
             share(z_far).start()
-            warrive(3)
-            for m in (7, 8, 9):
-                wmove(m).start()
 
         @pl.when(n == 4)
         def _():
             warrive(0)
-            for m in (6, 4, 5):
+            for m in (4, 5, 6):
                 wmove(m).start()
             give(a_own).start()
             arrive(x_up, core)
@@ -691,9 +686,6 @@
         def _():
             arrive(x_far, core)
             share(x_far).start()
-            warrive(6)
-            for m in (10, 11, 12):
-                wmove(m).start()
 
         arrive(e, 1 - core)
         update(e, False)
@@ -742,7 +734,7 @@
                     def _():
                         head_push(d, a, n).start()
 
-    for m in (1, 2, 4, 5, 7, 8, 9, 10, 11, 12):
+    for m in range(1, 7):
         warrive(m)
     for g in (t_up, t_down, t_far, a_up, a_down, a_far):
         give(g).start()
@@ -754,6 +746,8 @@
             for k in range(2):
                 ref = heads.at[g, :, pl.ds(OFF * n + HALF * k, HALF), :]
                 push(ref, ref, hsend.at[0, 0, 0], hrecv.at[g, n, k], sibling, t).wait_recv()
+
+    take_rows.wait()
 
     part = out.shape[-1]
     place = pl.ds(HS * y, HS)
@@ -796,7 +790,7 @@
         transfer(*moves[index], index).wait_send()
     for e in range(PAIRS):
         share(e).wait_send()
-    for m in range(13):
+    for m in range(7):
         wmove(m).wait_send()
     for g in range(N_TP):
         give(g).wait_send()
@@ -830,9 +824,12 @@
     return pl.pallas_call(
         attention_kernel,
         out_shape=jax.ShapeDtypeStruct((2, CH, part), bf16),
-        in_specs=[sm, sm, vm, vm, anywhere, vm],
+        in_specs=[sm, sm, anywhere, anywhere, anywhere, anywhere],
         out_specs=vm,
         scratch_shapes=[
+            pltpu.VMEM(query.shape, bf16),
+            pltpu.VMEM(kv.shape, bf16),
+            pltpu.VMEM(rows.shape, bf16),
             pltpu.VMEM((PAIRS, 2, keys, HS), bf16),
             pltpu.VMEM((keys, HS), bf16),
             pltpu.VMEM((keys, 2 * HS), jnp.float32),
@@ -843,11 +840,12 @@
             pltpu.VMEM((2, N_TP, depth, width // 4), bf16),
             pltpu.VMEM((2 * HS, width // 4), jnp.float32),
             pltpu.VMEM((4, 2, HS, part), bf16),
+            dma((3,)),
             dma((7,)),
             dma((PAIRS, 2)),
             dma((PAIRS,)),
-            dma((13,)),
-            dma((13,)),
+            dma((7,)),
+            dma((7,)),
             dma((N_TP,)),
             dma((N_TP,)),
             dma,
@@ -857,7 +855,7 @@
             dma((4,)),
         ],
         compiler_params=pltpu.CompilerParams(
-            collective_id=2, has_side_effects=True, vmem_limit_bytes=52 * 2**20
+            collective_id=2, has_side_effects=True, vmem_limit_bytes=60 * 2**20
         ),
         name="attention",
     )(slot_of, span_order, query, kv, out_weight, rows)
@@ -888,12 +886,11 @@
         spans[:, None] * CH + HS * (t % 4) + jnp.arange(HS, dtype=jnp.int32)[None, :]
     ).reshape(-1)
     half = HS // 2
-    freqs = 1000000.0 ** (-(jnp.arange(half, dtype=jnp.float32) * 2.0 / HS))
+    lane = jnp.arange(HS, dtype=jnp.int32)
+    freqs = 1000000.0 ** (-((lane % half).astype(jnp.float32) * 2.0 / HS))
     angles = positions.astype(jnp.float32)[:, None] * freqs[None, :]
-    cos = jnp.cos(angles)
-    sin = jnp.sin(angles)
-    cosine = jnp.concatenate([cos, cos], axis=1)
-    sine = jnp.concatenate([-sin, sin], axis=1)
+    cosine = jnp.cos(angles)
+    sine = jnp.where(lane[None, :] < half, -1.0, 1.0) * jnp.sin(angles)
     rows, query, kv = intake(
         text_embed, norm_gain, frame_features, frame_positions, span_order, (cosine, sine),
         projector, query_weight, key_weight, value_weight,

time: 200 us -> 195 us (0.975)
  the two profiles are of different devices: /device:TPU:22 before, /device:TPU:30 now
where the time goes in v8:
time: 195 us
  Pallas kernels  188 us (96%)
  local copies, waits for them, and re-layouts  3.5 us (2%)
  other arithmetic  3.34 us (2%)
    pallas_call x1, Pallas kernels, attention(): pl.pallas_call(attention_kernel, out_shape=jax.ShapeDtypeStruct((2, CH, p...  102 us
    pallas_call x1, Pallas kernels, intake(): pl.pallas_call(intake_kernel, out_shape=(jax.ShapeDtypeStruct((4, 2, HS,...  86.5 us

profile of v8, /device:TPU:30, one launch (start us, length us, event | category | flops | bytes accessed | tf_op | source)
XLA Modules:
  0.0 195.2 jit_solution(12426898652853911987)
XLA Ops:
  0.0 0.7 multiply_add_fusion
  0.7 0.1 convert_bitcast_fusion
  0.8 1.3 select_reduce_fusion.slot_of
  2.1 1.3 broadcast_in_dim.38.gain
  3.4 1.2 fusion
  4.6 86.5 %intake.1 = (bf16[4,2,128,448]{3,2,1,0:T(8,128)(2,1)}, bf16[2,8,4,32,128]{4,3,2,1,0:T(8,128)(2,1)}, bf16[8,4,64,128]{3,2,1,0:T(8,128)(2,1)}) custom-call(bf16[16,448]{1,0:T(8,128)(2,1)} %broadcast_in_dim.38.gain, s32[1,64]{1,0:T(1,128)} %bitcast.13, s32[1,32]{1,0:T(1,128)} %bitcast.12, f32[256,128]{1,0:T(8,128)} %get-tuple-element.12.cosine, ...), custom_call_target="tpu_custom_call" | custom-call | tf_op jit(solution)/shard_map/intake/pallas_call | solution.py:415
  91.1 101.9 %attention.1 = bf16[2,512,448]{2,1,0:T(8,128)(2,1)} custom-call(s32[32]{0:T(128)} %select_reduce_fusion.slot_of, s32[32]{0:T(128)} %span_order.1, bf16[2,32,32,128]{3,2,1,0:T(8,128)(2,1)} %bitcast.10, bf16[32,64,128]{2,1,0:T(8,128)(2,1)} %bitcast.11, bf16[256,3584]{1,0:T(8,128)(2,1)} %out_weight.1, bf16[4,2,128,448]{3,2,1,0:T(8,128)(2,1)} %get-tuple-element.10.rows_in), custom_call_target="tpu_custom_call" | custom-call | tf_op jit(solution)/shard_map/attention/pallas_call | solution.py:824
  193.0 2.2 %copy.12 = bf16[1024,448]{0,1:T(8,128)(2,1)} copy(bf16[1024,448]{1,0:T(8,128)(2,1)} %bitcast.8) | data formatting | bytes 1835008 | tf_op jit(solution)/shard_map/reshape | solution.py:902
  (1 shorter events, 0.0 us)

commit v9 on v8

--- a/solution.py
+++ b/solution.py
@@ -155,21 +155,29 @@
     def quarter(n):
         return pl.ds(depth // 4 * n, depth // 4)
 
+    def half_quarter(n, second):
+        return pl.ds(depth // 4 * n + depth // 8 * second, depth // 8)
+
+    z_next = (add4(z, 1), add4(z, 3))
+    y_others = (y_up, y_down, y_far)
+
     def wmove(m):
-        n = m - 3
-        shard = y if m < 3 else (y_up, y_down, y_far)[n // 3]
-        ref = weight.at[core, shard, quarter(z)]
         if m < 3:
-            ctx, tp = c, side + (y_up, y_down, y_far)[m]
+            ref, ctx, tp = weight.at[core, y, quarter(z)], c, side + y_others[m]
         else:
-            ctx, tp = 2 * (z_up, z_down, z_far)[n % 3] + core, t
+            n, up = (m - 3) % 6 // 2, (m - 3) % 2
+            cut = quarter(z) if m < 9 else half_quarter(z_next[1 - up], up)
+            ref, tp = weight.at[core, y_others[n], cut], t
+            ctx = 2 * (z_up, z_down)[up] + core
         return push(ref, ref, wsend.at[m], wrecv.at[m], ctx, tp)
 
     def warrive(m):
-        n = m - 3
-        shard = (y_down, y_up, y_far)[m] if m < 3 else (y_up, y_down, y_far)[n // 3]
-        origin = z if m < 3 else add4(z, (3, 1, 2)[n % 3])
-        ref = weight.at[core, shard, quarter(origin)]
+        if m < 3:
+            ref = weight.at[core, (y_down, y_up, y_far)[m], quarter(z)]
+        else:
+            n, up = (m - 3) % 6 // 2, (m - 3) % 2
+            cut = quarter(z_next[1 - up]) if m < 9 else half_quarter(add4(z, 2), up)
+            ref = weight.at[core, y_others[n], cut]
         push(ref, ref, wsend.at[m], wrecv.at[m], sibling, t).wait_recv()
 
     def share(n):
@@ -211,7 +219,7 @@
         if d == 4:
             for m in range(3):
                 warrive(m)
-            for m in range(3, 12):
+            for m in range(3, 9):
                 wmove(m).start()
 
     take_text.wait()
@@ -271,6 +279,10 @@
     for one in kv_loads:
         one.wait()
 
+    for m in range(3, 9):
+        warrive(m)
+    for m in range(9, 15):
+        wmove(m).start()
     total = jnp.zeros((group, 1), f32)
     for d in range(N_TP):
         j = lax.rem(t + d, N_TP)
@@ -282,7 +294,7 @@
     keep = pltpu.make_async_copy(rows.at[pl.ds(side, 4)], rows_out, osem)
     keep.start()
 
-    for m in range(3, 12):
+    for m in range(9, 15):
         warrive(m)
     for n in range(1, 4):
         share(n).start()
@@ -382,7 +394,7 @@
     pltpu.make_async_copy(
         incoming.at[pl.ds(0, devices - 1)], incoming.at[pl.ds(0, devices - 1)], fr_send
     ).wait()
-    for m in range(12):
+    for m in range(15):
         wmove(m).wait_send()
     for n in range(4):
         share(n).wait_send()
@@ -441,8 +453,8 @@
             dma((2,)),
             dma,
             dma,
-            dma((12,)),
-            dma((12,)),
+            dma((15,)),
+            dma((15,)),
             dma((4,)),
             dma((4,)),
             dma((4, 2)),
@@ -476,7 +488,7 @@
 def attention_kernel(
     slot_of, span_order, query_in, kv_in, out_weight, rows_in, out,
     query, kv_own, rows, kv, q, summed, largest, limit, attended, heads, weight, product, result,
-    isem, send, recv, pass_send, wsend, wrecv, csend, crecv, own_sem,
+    isem, send, recv, pass_send, half_send, half_recv, wsend, wrecv, csend, crecv, own_sem,
     hsend, hrecv, rsend, rrecv,
 ):
     f32 = jnp.float32
@@ -491,6 +503,7 @@
     z = pair % 4
     up, down, far = (add4(z, n) for n in (1, 3, 2))
     z_up, z_down, z_far = base + up, base + down, base + far
+    keys = kv.shape[2]
     x_own, x_up, x_down, x_far = other + z, other + up, other + down, other + far
     y = lax.rem(t, 4)
     side = t - y
@@ -571,9 +584,18 @@
 
     share(pair).start()
     moves = (
-        (pair, x_own), (pair, z_up), (pair, z_down), (pair, z_far),
-        (x_own, z_up), (x_own, z_down), (z_far, x_own),
-    )
+        (pair, x_own), (pair, z_up), (pair, z_down), (x_own, z_up), (x_own, z_down), (z_far, x_own),
+    )
+
+    def pass_half(n):
+        e, to = ((z_down, z_up), (z_up, z_down))[n]
+        block = kv.at[e, core, pl.ds(keys // 2 * n, keys // 2)]
+        return push(block, block, half_send.at[n], half_recv.at[n], 2 * to + core, t)
+
+    def arrive_half(n):
+        block = kv.at[z_far, core, pl.ds(keys // 2 * n, keys // 2)]
+        push(block, block, half_send.at[n], half_recv.at[n], sibling, t).wait_recv()
+
     for index in range(3):
         transfer(*moves[index], index).start()
     own_copy.wait()
@@ -643,9 +665,12 @@
     update(pair, True)
     arrive(x_own, core)
     share(x_own).start()
-    transfer(*moves[1], 1).wait_send()
-    transfer(*moves[2], 2).wait_send()
-    transfer(*moves[3], 3).start()
+    arrive(z_down, core)
+    pass_half(0).start()
+    share(z_down).start()
+    arrive(z_up, core)
+    pass_half(1).start()
+    share(z_up).start()
     wmove(0).start()
     give(t).start()
     order = (x_own, z_up, z_down, z_far, x_up, x_down, x_far)
@@ -657,18 +682,10 @@
 
         @pl.when(n == 1)
         def _():
-            arrive(z_up, core)
-            share(z_up).start()
-            arrive(z_down, core)
-            share(z_down).start()
-
-        @pl.when(n == 2)
-        def _():
-            transfer(*moves[3], 3).wait_send()
-            transfer(*moves[4], 4).start()
-            transfer(*moves[5], 5).start()
-            arrive(z_far, core)
-            transfer(*moves[6], 6).start()
+            arrive_half(0)
+            arrive_half(1)
+            for index in (5, 3, 4):
+                transfer(*moves[index], index).start()
             share(z_far).start()
 
         @pl.when(n == 4)
@@ -786,7 +803,9 @@
     for n in range(4):
         ref = out.at[:, pl.ds(HS * n, HS), :]
         push(ref, ref, rsend.at[0], rrecv.at[n], sibling, t).wait_recv()
-    for index in (0, 4, 5, 6):
+    for n in range(2):
+        pass_half(n).wait_send()
+    for index in range(6):
         transfer(*moves[index], index).wait_send()
     for e in range(PAIRS):
         share(e).wait_send()
@@ -841,9 +860,11 @@
             pltpu.VMEM((2 * HS, width // 4), jnp.float32),
             pltpu.VMEM((4, 2, HS, part), bf16),
             dma((3,)),
-            dma((7,)),
+            dma((6,)),
             dma((PAIRS, 2)),
             dma((PAIRS,)),
+            dma((2,)),
+            dma((2,)),
             dma((7,)),
             dma((7,)),
             dma((N_TP,)),

time: 195 us -> 189 us (0.969)
  the two profiles are of different devices: /device:TPU:30 before, /device:TPU:29 now
where the time goes in v9:
time: 189 us; the launch traced here: 188 us
  Pallas kernels  181 us (96%)
  local copies, waits for them, and re-layouts  3.5 us (2%)
  other arithmetic  3.34 us (2%)
    pallas_call x1, Pallas kernels, attention(): pl.pallas_call(attention_kernel, out_shape=jax.ShapeDtypeStruct((2, CH, p...  94.1 us
    pallas_call x1, Pallas kernels, intake(): pl.pallas_call(intake_kernel, out_shape=(jax.ShapeDtypeStruct((4, 2, HS,...  86.6 us

profile of v9, /device:TPU:29, one launch (start us, length us, event | category | flops | bytes accessed | tf_op | source)
XLA Modules:
  0.0 187.5 jit_solution(15221121180149977975)
XLA Ops:
  0.0 0.7 multiply_add_fusion
  0.7 0.1 convert_bitcast_fusion
  0.8 1.3 select_reduce_fusion.slot_of
  2.1 1.3 broadcast_in_dim.38.gain
  3.4 1.2 fusion
  4.6 86.6 %intake.1 = (bf16[4,2,128,448]{3,2,1,0:T(8,128)(2,1)}, bf16[2,8,4,32,128]{4,3,2,1,0:T(8,128)(2,1)}, bf16[8,4,64,128]{3,2,1,0:T(8,128)(2,1)}) custom-call(bf16[16,448]{1,0:T(8,128)(2,1)} %broadcast_in_dim.38.gain, s32[1,64]{1,0:T(1,128)} %bitcast.13, s32[1,32]{1,0:T(1,128)} %bitcast.12, f32[256,128]{1,0:T(8,128)} %get-tuple-element.12.cosine, ...), custom_call_target="tpu_custom_call" | custom-call | tf_op jit(solution)/shard_map/intake/pallas_call | solution.py:427
  91.2 94.1 %attention.1 = bf16[2,512,448]{2,1,0:T(8,128)(2,1)} custom-call(s32[32]{0:T(128)} %select_reduce_fusion.slot_of, s32[32]{0:T(128)} %span_order.1, bf16[2,32,32,128]{3,2,1,0:T(8,128)(2,1)} %bitcast.10, bf16[32,64,128]{2,1,0:T(8,128)(2,1)} %bitcast.11, bf16[256,3584]{1,0:T(8,128)(2,1)} %out_weight.1, bf16[4,2,128,448]{3,2,1,0:T(8,128)(2,1)} %get-tuple-element.10.rows_in), custom_call_target="tpu_custom_call" | custom-call | tf_op jit(solution)/shard_map/attention/pallas_call | solution.py:843
  185.3 2.2 %copy.12 = bf16[1024,448]{0,1:T(8,128)(2,1)} copy(bf16[1024,448]{1,0:T(8,128)(2,1)} %bitcast.8) | data formatting | bytes 1835008 | tf_op jit(solution)/shard_map/reshape | solution.py:923
  (1 shorter events, 0.0 us)

commit v10 on v9

--- a/solution.py
+++ b/solution.py
@@ -650,10 +650,10 @@
             new = jnp.dot(weights, beside, preferred_element_type=f32)
             summed[here] = new if first_set else summed[here] + new
 
-        s = scores(0)
+        s = scores(7)
         held = None
-        for i in range(8):
-            ahead = scores(i + 1) if i < 7 else None
+        for i in range(7, -1, -1):
+            ahead = scores(i - 1) if i else None
             weights = soft(i, s)
             if held is not None:
                 gather(*held)

time: 189 us -> 186 us (0.984)
  Pallas kernels: 181 us -> 178 us
    pallas_call x1, Pallas kernels: 94.1 us -> 90.9 us  [attention(): pl.pallas_call(attention_kernel, out_shape=jax.ShapeDtypeStruct((2, CH, p...]
where the time goes in v10:
time: 186 us; the launch traced here: 184 us
  Pallas kernels  178 us (96%)
  local copies, waits for them, and re-layouts  3.5 us (2%)
  other arithmetic  3.34 us (2%)
    pallas_call x1, Pallas kernels, attention(): pl.pallas_call(attention_kernel, out_shape=jax.ShapeDtypeStruct((2, CH, p...  90.9 us
    pallas_call x1, Pallas kernels, intake(): pl.pallas_call(intake_kernel, out_shape=(jax.ShapeDtypeStruct((4, 2, HS,...  86.6 us

profile of v10, /device:TPU:29, one launch (start us, length us, event | category | flops | bytes accessed | tf_op | source)
XLA Modules:
  0.0 184.4 jit_solution(11373547241803140880)
XLA Ops:
  0.0 0.7 multiply_add_fusion
  0.7 0.1 convert_bitcast_fusion
  0.8 1.3 select_reduce_fusion.slot_of
  2.1 1.3 broadcast_in_dim.38.gain
  3.4 1.2 fusion
  4.6 86.6 %intake.1 = (bf16[4,2,128,448]{3,2,1,0:T(8,128)(2,1)}, bf16[2,8,4,32,128]{4,3,2,1,0:T(8,128)(2,1)}, bf16[8,4,64,128]{3,2,1,0:T(8,128)(2,1)}) custom-call(bf16[16,448]{1,0:T(8,128)(2,1)} %broadcast_in_dim.38.gain, s32[1,64]{1,0:T(1,128)} %bitcast.13, s32[1,32]{1,0:T(1,128)} %bitcast.12, f32[256,128]{1,0:T(8,128)} %get-tuple-element.12.cosine, ...), custom_call_target="tpu_custom_call" | custom-call | tf_op jit(solution)/shard_map/intake/pallas_call | solution.py:427
  91.2 90.9 %attention.1 = bf16[2,512,448]{2,1,0:T(8,128)(2,1)} custom-call(s32[32]{0:T(128)} %select_reduce_fusion.slot_of, s32[32]{0:T(128)} %span_order.1, bf16[2,32,32,128]{3,2,1,0:T(8,128)(2,1)} %bitcast.10, bf16[32,64,128]{2,1,0:T(8,128)(2,1)} %bitcast.11, bf16[256,3584]{1,0:T(8,128)(2,1)} %out_weight.1, bf16[4,2,128,448]{3,2,1,0:T(8,128)(2,1)} %get-tuple-element.10.rows_in), custom_call_target="tpu_custom_call" | custom-call | tf_op jit(solution)/shard_map/attention/pallas_call | solution.py:843
  182.2 2.2 %copy.12 = bf16[1024,448]{0,1:T(8,128)(2,1)} copy(bf16[1024,448]{1,0:T(8,128)(2,1)} %bitcast.8) | data formatting | bytes 1835008 | tf_op jit(solution)/shard_map/reshape | solution.py:923
  (1 shorter events, 0.0 us)

commit v11 on v10

--- a/solution.py
+++ b/solution.py
@@ -690,14 +690,17 @@
 
         @pl.when(n == 4)
         def _():
+            arrive(x_up, core)
+            share(x_up).start()
+            arrive(x_down, core)
+            share(x_down).start()
+
+        @pl.when(n == 5)
+        def _():
             warrive(0)
             for m in (4, 5, 6):
                 wmove(m).start()
             give(a_own).start()
-            arrive(x_up, core)
-            share(x_up).start()
-            arrive(x_down, core)
-            share(x_down).start()
 
         @pl.when(n == 6)
         def _():

time: 186 us -> 197 us (1.059)
  Pallas kernels: 178 us -> 188 us
    pallas_call x1, Pallas kernels: 90.9 us -> 102 us  [attention(): pl.pallas_call(attention_kernel, out_shape=jax.ShapeDtypeStruct((2, CH, p...]
where the time goes in v11:
time: 197 us; the launch traced here: 195 us
  Pallas kernels  188 us (95%)
  local copies, waits for them, and re-layouts  3.5 us (2%)
  other arithmetic  3.34 us (2%)
    pallas_call x1, Pallas kernels, attention(): pl.pallas_call(attention_kernel, out_shape=jax.ShapeDtypeStruct((2, CH, p...  102 us
    pallas_call x1, Pallas kernels, intake(): pl.pallas_call(intake_kernel, out_shape=(jax.ShapeDtypeStruct((4, 2, HS,...  86.6 us

profile of v11, /device:TPU:29, one launch (start us, length us, event | category | flops | bytes accessed | tf_op | source)
XLA Modules:
  0.0 195.1 jit_solution(13116238496297349932)
XLA Ops:
  0.0 0.7 multiply_add_fusion
  0.7 0.1 convert_bitcast_fusion
  0.8 1.3 select_reduce_fusion.slot_of
  2.1 1.3 broadcast_in_dim.38.gain
  3.4 1.2 fusion
  4.6 86.6 %intake.1 = (bf16[4,2,128,448]{3,2,1,0:T(8,128)(2,1)}, bf16[2,8,4,32,128]{4,3,2,1,0:T(8,128)(2,1)}, bf16[8,4,64,128]{3,2,1,0:T(8,128)(2,1)}) custom-call(bf16[16,448]{1,0:T(8,128)(2,1)} %broadcast_in_dim.38.gain, s32[1,64]{1,0:T(1,128)} %bitcast.13, s32[1,32]{1,0:T(1,128)} %bitcast.12, f32[256,128]{1,0:T(8,128)} %get-tuple-element.12.cosine, ...), custom_call_target="tpu_custom_call" | custom-call | tf_op jit(solution)/shard_map/intake/pallas_call | solution.py:427
  91.2 101.6 %attention.1 = bf16[2,512,448]{2,1,0:T(8,128)(2,1)} custom-call(s32[32]{0:T(128)} %select_reduce_fusion.slot_of, s32[32]{0:T(128)} %span_order.1, bf16[2,32,32,128]{3,2,1,0:T(8,128)(2,1)} %bitcast.10, bf16[32,64,128]{2,1,0:T(8,128)(2,1)} %bitcast.11, bf16[256,3584]{1,0:T(8,128)(2,1)} %out_weight.1, bf16[4,2,128,448]{3,2,1,0:T(8,128)(2,1)} %get-tuple-element.10.rows_in), custom_call_target="tpu_custom_call" | custom-call | tf_op jit(solution)/shard_map/attention/pallas_call | solution.py:846
  192.9 2.2 %copy.12 = bf16[1024,448]{0,1:T(8,128)(2,1)} copy(bf16[1024,448]{1,0:T(8,128)(2,1)} %bitcast.8) | data formatting | bytes 1835008 | tf_op jit(solution)/shard_map/reshape | solution.py:926
  (1 shorter events, 0.0 us)
